TPU v7x, 256 devices: a whole 4x4x8 slice. The times are simulated.
256 devices in a mesh: dp: 8 (over y, x_hi), ctx: 32 (over z, x_lo, core).
Axes of the slice: x: 4 (x_hi: 2, x_lo: 2; x = x_hi * 2 + x_lo), y: 4, z: 8, core: 2. Of those that a mesh axis runs over, the one named last changes fastest.
Arguments:
- span_ids: int32 [8, 64], P('dp'), may hold values from 0 to 63, as said below
- q_nope: bfloat16 [8, 4096, 1024], P('dp', 'ctx'), may hold values from -4 to 4
- q_rope: bfloat16 [8, 4096, 512], P('dp', 'ctx'), may hold values from -4 to 4
- w_uk: bfloat16 [8, 128, 512], replicated, may hold values from -1 to 1
- latent: bfloat16 [8, 4096, 512], P('dp', 'ctx'), may hold values from -4 to 4
- rope_key: bfloat16 [8, 4096, 64], P('dp', 'ctx'), may hold values from -4 to 4
- w_uv: bfloat16 [8, 512, 128], replicated, may hold values from -0.25 to 0.25
- d_out: bfloat16 [8, 4096, 1024], P('dp', 'ctx'), may hold values from -6 to 6
- lse: float32 [8, 4096, 8], P('dp', 'ctx'), as said below
- saved_out: bfloat16 [8, 4096, 4096], P('dp', 'ctx'), may hold values from -4 to 4, as said below
Outputs:
- d_q_nope: bfloat16 [8, 4096, 1024], P('dp', 'ctx')
- d_q_rope: bfloat16 [8, 4096, 512], P('dp', 'ctx')
- d_latent: bfloat16 [8, 4096, 512], P('dp', 'ctx')
- d_rope_key: bfloat16 [8, 4096, 64], P('dp', 'ctx')
- d_w_uk: float32 [8, 128, 512], replicated
- d_w_uv: float32 [8, 512, 128], replicated
Inputs may be any that keep to these rules, and one draw needn't show every extreme that they name: `span_ids`: the stored spans 2 i and 2 i + 1 of a sequence are its spans c and 2 * 32 - 1 - c for some c; every span is stored once. `lse`: the log-sum-exp over allowed keys of the scores of the forward pass. `saved_out`: the forward pass's softmax-weighted sum of allowed latent rows.
All inputs are finite; a program needn't handle non-finite values.
Results may differ from a plain program's by a relative error of at most 0.025.
Values may be sent and summed in bfloat16 or wider, within the bound.
No kernel may reach another device: no remote copies, remote signals or barrier semaphores. Data moves between devices by JAX's collectives and lax.ppermute only.
A program may use at most 128 MiB of HBM per device.

v0:
```python
import functools
import itertools
import math

import jax
import jax.numpy as jnp
from jax import lax
from jax.experimental import pallas as pl
from jax.experimental.pallas import tpu as pltpu
from jax.sharding import PartitionSpec as P

F32 = jnp.float32
BF = jnp.bfloat16
LOG2E = math.log2(math.e)
VMEM = pl.BlockSpec(memory_space=pltpu.VMEM)
SMEM = pl.BlockSpec(memory_space=pltpu.SMEM)
ANY = pl.BlockSpec(memory_space=pl.ANY)


def vmem(mib):
    return pltpu.CompilerParams(vmem_limit_bytes=mib * 1024 * 1024)


def dot_nn(a, b):
    return lax.dot_general(a, b, (((1,), (0,)), ((), ())), preferred_element_type=F32)


def dot_nt(a, b):
    return lax.dot_general(a, b, (((1,), (1,)), ((), ())), preferred_element_type=F32)


def dot_tn(a, b):
    return lax.dot_general(a, b, (((0,), (0,)), ((), ())), preferred_element_type=F32)


def add(*terms):
    return sum(t.astype(F32) for t in terms).astype(BF)


def places(grid, dp, ctx):
    ny, nxh, nz, nxl, nc = grid
    return (
        dp // nxh,
        (dp % nxh) * nxl + (ctx // nc) % nxl,
        ctx // (nc * nxl),
        ctx % nc,
    )


def own_kernel(grid, dp_ref, ctx_ref, qn, qr, do_ref, sv_ref, lse_ref, lat, rope, wv_ref, key, pack, *dwv):
    ny, nxh, nz, nxl, nc = grid
    y, x, z, core = places(grid, dp_ref[0], ctx_ref[0])
    nx = nxh * nxl
    rows = do_ref.shape[0]
    heads, dc, hd = wv_ref.shape
    dr = rope.shape[0]
    group = hd // nx
    key[:, :dc] = lat[...]
    key[:, dc:] = (
        jnp.concatenate([rope[...].astype(F32), jnp.zeros((128 - dr, rows), F32)], axis=0)
        .T.astype(BF)
    )
    per_core = heads // nc
    per_y = per_core // ny
    lane = lax.broadcasted_iota(jnp.int32, (rows, 128), 1)
    part = lane % (2 * heads)
    lse = lse_ref[...] * LOG2E
    gap = jnp.zeros_like(lse)
    rest = jnp.zeros((128 - 6 * heads, rows), F32)
    acc = jnp.concatenate([lse, gap, lse, gap, lse, gap, rest], axis=0).T
    for i, j, k in itertools.product(range(nc), range(ny), range(per_y)):
        h = (core + i) % nc * per_core + (y + j) % ny * per_y + k
        do = do_ref[:, pl.ds(pl.multiple_of(h * hd, hd), hd)]
        sv = sv_ref[:, pl.ds(pl.multiple_of(h * dc, dc), dc)]
        g = dot_nt(do, wv_ref[h]).astype(BF)
        delta = jnp.sum(g.astype(F32) * sv.astype(F32), axis=1, keepdims=True)
        acc = jnp.where(part == heads + h, delta, acc)
        dv = dot_tn(sv, do).astype(BF)
        for n in range(nx):
            at = pl.multiple_of((n - x + nx) % nx * group, group)
            for m in range(dc // hd):
                dwv[i][j * per_y + k, pl.ds(at, group), m * hd : (m + 1) * hd] = dv[
                    m * hd + n * group : m * hd + (n + 1) * group
                ]
    high = acc.astype(BF)
    rest = acc - high.astype(F32)
    mid = rest.astype(BF)
    low = (rest - mid.astype(F32)).astype(BF)
    wn, wr, wd = qn.shape[1], qr.shape[1], do_ref.shape[1]
    pack[:, :wn] = qn[...]
    pack[:, wn : wn + wr] = qr[...]
    pack[:, wn + wr : wn + wr + wd] = do_ref[...]
    pack[:, wn + wr + wd :] = jnp.where(
        lane < 2 * heads, high, jnp.where(lane < 4 * heads, mid, low)
    )


def own_call(grid, dp, ctx, qn, qr, do, sv, lse, lat, rope, wv):
    rows = do.shape[0]
    heads, dc, hd = wv.shape
    nc = grid[4]
    return pl.pallas_call(
        functools.partial(own_kernel, grid),
        in_specs=[SMEM, SMEM] + [VMEM] * 8,
        out_specs=(VMEM,) * (2 + nc),
        out_shape=(
            jax.ShapeDtypeStruct((rows, dc + 128), BF),
            jax.ShapeDtypeStruct((rows, qn.shape[1] + qr.shape[1] + do.shape[1] + 128), BF),
        )
        + (jax.ShapeDtypeStruct((heads // nc, hd, dc), BF),) * nc,
        compiler_params=vmem(60),
        cost_estimate=pl.CostEstimate(flops=4 * 10**9, bytes_accessed=4 * 10**6, transcendentals=0),
        name="own_rows",
    )(dp, ctx, qn, qr, do, sv, lse, lat, rope, wv)


def attn_kernel(grid, offsets, na, heads, spans, scaling, *refs):
    ny, nxh, nz, nxl, nc = grid
    nx = nxh * nxl
    nb = len(offsets)
    ids, dp_ref, ctx_ref = refs[:3]
    packs = refs[3 : 3 + na]
    keys = refs[3 + na : 3 + na + nb]
    wk, wv = refs[3 + na + nb : 5 + na + nb]
    out = refs[5 + na + nb :]
    far, dk, (keep, send), weights = out[:2], out[2 : nb + 1], out[nb + 1 : nb + 3], out[nb + 3 : nb + 3 + nc]
    PK, KC, Q, G, LB, DB, K, KP, DL, DQ, DO, WA, sems = out[nb + 3 + nc :]
    y, x, z, core = places(grid, dp_ref[0], ctx_ref[0])
    xl = x % nxl

    hd, dc = wk.shape[1], wk.shape[2]
    width = K.shape[2]
    tokens = KC.shape[1]
    wn = heads * hd
    wr = DO.shape[2] - wn
    dr = wr // heads
    ch = tokens // 2
    nkb = K.shape[0] // 2
    rows = heads * ch
    per = nb // nkb
    kw = per * ch

    copies = [pltpu.make_async_copy(packs[a], PK.at[a], sems.at[a]) for a in range(na)]
    copies += [pltpu.make_async_copy(keys[b], KC.at[b], sems.at[na + b]) for b in range(nb)]
    for c in copies:
        c.start()

    def first_of(z_, xl_, c_):
        return ids[0, 2 * ((z_ * nxl + xl_) * nc + c_)]

    qc = [
        first_of(z, xl, core),
        first_of(z, nxl - 1 - xl, core),
        first_of(z, xl, nc - 1 - core),
        first_of(z, nxl - 1 - xl, nc - 1 - core),
    ][:na]
    kc = [first_of((z + o + nz) % nz, xl, core) for o in offsets]

    def low_span(c):
        return jnp.minimum(c, spans - 1 - c)

    klow = [low_span(c) for c in kc]
    slots = [sum(jnp.where(other < mine, 1, 0) for other in klow) for mine in klow]

    def pick(values, a):
        out = values[0]
        for i in range(1, len(values)):
            out = jnp.where(a == i, values[i], out)
        return out

    DL[...] = jnp.zeros_like(DL)
    WA[...] = jnp.zeros_like(WA)

    for c in copies[:na]:
        c.wait()

    def prepare(a, _):
        first = 2 * pick(qc, a) < spans
        stats = PK[a, :, wn + wr + heads * hd :].astype(F32)
        stats = stats[:, : 2 * heads] + stats[:, 2 * heads : 4 * heads] + stats[:, 4 * heads : 6 * heads]
        flipped = jnp.concatenate([stats[ch:], stats[:ch]], axis=0)
        stats = jnp.where(first, stats, flipped)
        for h in range(heads):
            ql = dot_nn(PK[a, :, h * hd : (h + 1) * hd], wk[h]).astype(BF)
            gl = dot_nt(PK[a, :, wn + wr + h * hd : wn + wr + (h + 1) * hd], wv[h]).astype(BF)
            qrot = PK[a, :, wn + h * dr : wn + (h + 1) * dr]
            to = slice(h * ch, (h + 1) * ch)
            for half in range(2):
                mine = slice(half * ch, (half + 1) * ch)
                other = slice((1 - half) * ch, (2 - half) * ch)
                Q[a, half, to, :dc] = jnp.where(first, ql[mine], ql[other])
                Q[a, half, to, dc : dc + dr] = jnp.where(first, qrot[mine], qrot[other])
                Q[a, half, to, dc + dr :] = jnp.zeros((ch, width - dc - dr), BF)
                G[a, half, to, :] = jnp.where(first, gl[mine], gl[other])
                LB[a, half, to, :] = jnp.broadcast_to(stats[mine, h : h + 1], (ch, 128))
                DB[a, half, to, :] = jnp.broadcast_to(
                    stats[mine, heads + h : heads + h + 1], (ch, 128)
                )
        return 0

    lax.fori_loop(0, na, prepare, 0)

    for c in copies[na:]:
        c.wait()
    lane = lax.broadcasted_iota(jnp.int32, (8, kw), 1)
    kps = [jnp.zeros((8, kw), jnp.int32) for _ in range(2 * nkb)]
    key_at = []
    for b in range(nb):
        blk = slots[b] // per
        pos = pl.multiple_of((slots[b] % per) * ch, ch)
        first = 2 * kc[b] < spans
        low_at = pl.multiple_of(jnp.where(first, 0, ch), ch)
        high_at = pl.multiple_of(jnp.where(first, ch, 0), ch)
        key_at.append((blk, pos, low_at, high_at))
        K[blk, pl.ds(pos, ch), :] = KC[b, pl.ds(low_at, ch), :]
        K[nkb + blk, pl.ds(pos, ch), :] = KC[b, pl.ds(high_at, ch), :]
        inside = jnp.logical_and(lane >= pos, lane < pos + ch)
        for i in range(nkb):
            here = jnp.logical_and(inside, blk == i)
            kps[i] = jnp.where(here, klow[b] * ch + (lane - pos), kps[i])
            kps[nkb + i] = jnp.where(here, (spans - 1 - klow[b]) * ch + (lane - pos), kps[nkb + i])
    for i in range(2 * nkb):
        KP[i] = kps[i]

    sub = min(rows, 512)
    wide = kw // 128
    qtok = lax.broadcasted_iota(jnp.int32, (sub, kw), 0) % ch

    def unit(a, half, kb, span, fresh):
        kpos = KP[kb][0:1, :]
        dss, pbs = [], []
        for r in range(rows // sub):
            rr = slice(r * sub, (r + 1) * sub)
            s = dot_nt(Q[a, half, rr, :], K[kb])
            dp = dot_nt(G[a, half, rr, :], K[kb, :, :dc])
            lb = jnp.concatenate([LB[a, half, rr, :]] * wide, axis=1)
            db = jnp.concatenate([DB[a, half, rr, :]] * wide, axis=1)
            p = jnp.exp2(s * (scaling * LOG2E) - lb)
            p = jnp.where(kpos <= span * ch + qtok, p, 0.0)
            ds = (p * ((dp - db) * scaling)).astype(BF)
            DQ[half, rr, :] = jnp.where(fresh, 0.0, DQ[half, rr, :]) + dot_nn(ds, K[kb])
            dss.append(ds)
            pbs.append(p.astype(BF))
        ds = jnp.concatenate(dss, axis=0)
        pb = jnp.concatenate(pbs, axis=0)
        DL[kb, :, :dc] += dot_tn(pb, G[a, half]) + dot_tn(ds, Q[a, half, :, :dc])
        DL[kb, :, dc:] += dot_tn(ds, Q[a, half, :, dc:])

    def query_set(a, _):
        c = pick(qc, a)
        lo = low_span(c)
        hi = spans - 1 - lo
        below = sum(jnp.where(k <= lo, 1, 0) for k in klow)
        above = sum(jnp.where(k >= lo, 1, 0) for k in klow)

        @pl.when(below == 0)
        def _():
            DQ[0] = jnp.zeros_like(DQ[0])


        def step(u, _):
            blk = u // 3
            kind = u % 3
            half = jnp.where(kind == 1, 0, 1)
            kb = jnp.where(kind == 2, nkb + blk, blk)
            need = jnp.where(
                kind == 1, below > per * blk, jnp.where(kind == 2, nb - above < per * (blk + 1), True)
            )

            @pl.when(need)
            def _():
                unit(a, half, kb, jnp.where(kind == 1, lo, hi), u < 2)

            return 0

        lax.fori_loop(0, 3 * nkb, step, 0)

        first = 2 * c < spans
        for h in range(heads):
            to = slice(h * ch, (h + 1) * ch)
            d0 = DQ[0, to, dc : dc + dr]
            d1 = DQ[1, to, dc : dc + dr]
            d = jnp.concatenate([jnp.where(first, d0, d1), jnp.where(first, d1, d0)], axis=0)
            DO[a, :, wn + h * dr : wn + (h + 1) * dr] = d.astype(BF)
            d0 = DQ[0, to, :dc]
            d1 = DQ[1, to, :dc]
            d = jnp.concatenate([jnp.where(first, d0, d1), jnp.where(first, d1, d0)], axis=0)
            d = d.astype(BF)
            DO[a, :, h * hd : (h + 1) * hd] = dot_nt(d, wk[h]).astype(BF)
            WA[h] += dot_tn(PK[a, :, h * hd : (h + 1) * hd], d)
        return 0

    lax.fori_loop(0, na, query_set, 0)

    keep[...] = DO[: na // 2]
    send[...] = DO[na // 2 :]
    for b in range(nb):
        blk, pos, low_at, high_at = key_at[b]
        KC[b, pl.ds(low_at, ch), :] = DL[blk, pl.ds(pos, ch), :].astype(BF)
        KC[b, pl.ds(high_at, ch), :] = DL[nkb + blk, pl.ds(pos, ch), :].astype(BF)
        if b < nb - 1:
            dk[b][...] = KC[b]
        else:
            far[0][...] = KC[b, :ch]
            far[1][...] = KC[b, ch:]
    group = hd // nx
    per_core = heads // nc
    per_y = per_core // ny
    for i, j, k in itertools.product(range(nc), range(ny), range(per_y)):
        h = (core + i) % nc * per_core + (y + j) % ny * per_y + k
        for n in range(nx):
            at = pl.multiple_of((n - x + nx) % nx * group, group)
            weights[i][j * per_y + k, pl.ds(at, group), :] = WA[
                h, n * group : (n + 1) * group, :
            ].astype(BF)


def attn_call(grid, offsets, ids, dp, ctx, packs, keys, wk, wv, wr, scaling):
    na, nb = len(packs), len(keys)
    heads, hd, dc = wk.shape
    tokens, width = keys[0].shape
    ch = tokens // 2
    per = min(4, nb)
    nkb = nb // per
    rows = heads * ch
    nc = grid[4]
    out = heads * hd + wr
    return pl.pallas_call(
        functools.partial(attn_kernel, grid, offsets, na, heads, ids.shape[1], scaling),
        in_specs=[SMEM] * 3 + [ANY] * (na + nb) + [VMEM] * 2,
        out_shape=(
            (jax.ShapeDtypeStruct((ch, width), BF),) * 2
            + (jax.ShapeDtypeStruct((tokens, width), BF),) * (nb - 1)
            + (jax.ShapeDtypeStruct((na // 2, tokens, out), BF),) * 2
            + (jax.ShapeDtypeStruct((heads // nc, hd, dc), BF),) * nc
        ),
        out_specs=(VMEM,) * (nb + 3 + nc),
        scratch_shapes=[
            pltpu.VMEM((na,) + packs[0].shape, BF),
            pltpu.VMEM((nb, tokens, width), BF),
            pltpu.VMEM((na, 2, rows, width), BF),
            pltpu.VMEM((na, 2, rows, dc), BF),
            pltpu.VMEM((na, 2, rows, 128), F32),
            pltpu.VMEM((na, 2, rows, 128), F32),
            pltpu.VMEM((2 * nkb, per * ch, width), BF),
            pltpu.VMEM((2 * nkb, 8, per * ch), jnp.int32),
            pltpu.VMEM((2 * nkb, per * ch, width), F32),
            pltpu.VMEM((2, rows, width), F32),
            pltpu.VMEM((na, tokens, out), BF),
            pltpu.VMEM((heads, hd, dc), F32),
            pltpu.SemaphoreType.DMA((na + nb,)),
        ],
        compiler_params=vmem(44),
        cost_estimate=pl.CostEstimate(
            flops=3 * 10**10, bytes_accessed=10**7, transcendentals=10**7
        ),
        name="attn_grads",
    )(ids, dp, ctx, *packs, *keys, wk, wv)


def final_kernel(grid, heads, scale, dp_ref, ctx_ref, key_ref, plus, minus, q_ref, back_ref, *refs):
    ny, nxh, nz, nxl, nc = grid
    nx = nxh * nxl
    pieces, (dqn, dqr, dlat, drope, dwk, dwv) = refs[:-6], refs[-6:]
    dr = drope.shape[0]
    lat = dlat.shape[1]
    if plus.shape[0] == key_ref.shape[0]:
        got = plus[...].astype(F32) + minus[...].astype(F32)
    else:
        got = jnp.concatenate([plus[...].astype(F32), minus[...].astype(F32)], axis=0)
    key = key_ref[...].astype(F32) + got
    dlat[...] = key[:, :lat].astype(BF)
    drope[...] = key[:, lat:].T[:dr].astype(BF)
    q = add(q_ref[0], back_ref[...])
    dqn[...] = q[:, : dqn.shape[1]]
    dqr[...] = q[:, dqn.shape[1] :]
    y, x, z, core = places(grid, dp_ref[0], ctx_ref[0])
    hd = dwk.shape[1]
    dc = dwk.shape[2]
    per_core = heads // nc
    per_y = per_core // ny
    group = hd // nx
    for i, j, n, k in itertools.product(range(nc), range(ny), range(nx), range(per_y)):
        ref = pieces[i * ny + j]
        h = (core + i) % nc * per_core + (y - j + ny) % ny * per_y + k
        at = pl.multiple_of((x - n + nx) % nx * group, group)
        r = (n * 2 * per_y + k) * group
        dwk[h, pl.ds(at, group), :] = ref[r : r + group, :].astype(F32) * scale
        r += per_y * group
        for m in range(dc // hd):
            dwv[h, pl.ds(m * hd + at, group), :] = (
                ref[r : r + group, m * hd : (m + 1) * hd].astype(F32) * scale
            )


def final_call(grid, heads, hd, dr, scale, dp, ctx, key, plus, minus, q, back, pieces):
    tokens = key.shape[0]
    dc = pieces[0].shape[1]
    return pl.pallas_call(
        functools.partial(final_kernel, grid, heads, scale),
        in_specs=[SMEM, SMEM] + [VMEM] * (5 + len(pieces)),
        out_specs=(VMEM,) * 6,
        out_shape=(
            jax.ShapeDtypeStruct((tokens, heads * hd), BF),
            jax.ShapeDtypeStruct((tokens, heads * dr), BF),
            jax.ShapeDtypeStruct((tokens, dc), BF),
            jax.ShapeDtypeStruct((dr, tokens), BF),
            jax.ShapeDtypeStruct((heads, hd, dc), F32),
            jax.ShapeDtypeStruct((heads, dc, hd), F32),
        ),
        compiler_params=vmem(16),
        name="outputs",
    )(dp, ctx, key, plus, minus, q, back, *pieces)


def make_local(grid):
    ny, nxh, nz, nxl, nc = grid
    nx = nxh * nxl

    def all_perm(x, fn):
        pairs = []
        for y, xh, z, xl, c in itertools.product(*map(range, grid)):
            y2, xh2, z2, xl2, c2 = fn(y, xh, z, xl, c)
            src = (((y * nxh + xh) * nz + z) * nxl + xl) * nc + c
            dst = (((y2 * nxh + xh2) * nz + z2) * nxl + xl2) * nc + c2
            pairs.append((src, dst))
        return lax.ppermute(x, ("dp", "ctx"), pairs)

    def z_send(x, s):
        return all_perm(x, lambda y, xh, z, xl, c: (y, xh, (z + s) % nz, xl, c))

    def z_flip(x, bit):
        return all_perm(x, lambda y, xh, z, xl, c: (y, xh, z ^ bit, xl, c))

    def xl_swap(x):
        return all_perm(x, lambda y, xh, z, xl, c: (y, xh, z, nxl - 1 - xl, c))

    def c_swap(x):
        return all_perm(x, lambda y, xh, z, xl, c: (y, xh, z, xl, nc - 1 - c))

    def y_send(x, s):
        return all_perm(x, lambda y, xh, z, xl, c: ((y + s) % ny, xh, z, xl, c))

    def x_send(x, s):
        def fn(y, xh, z, xl, c):
            x2 = (xh * nxl + xl + s) % nx
            return y, x2 // nxl, z, x2 % nxl, c

        return all_perm(x, fn)

    def by_x(x, hd):
        x = x.reshape(ny, x.shape[0] // ny, nx, hd // nx, x.shape[2])
        return x.transpose(0, 2, 1, 3, 4).reshape(ny, nx, -1, x.shape[4])

    def local(span_ids, q_nope, q_rope, w_uk, latent, rope_key, w_uv, d_out, lse, saved_out):
        dp = lax.axis_index("dp").astype(jnp.int32).reshape(1)
        ctx = lax.axis_index("ctx").astype(jnp.int32).reshape(1)
        heads, hd, dc = w_uk.shape
        dr = rope_key.shape[2]
        tokens = q_nope.shape[1]
        ch = tokens // 2
        seq_rows = tokens * nz * nxl * nc
        scaling = (hd + dr) ** (-0.5)
        grad_scale = (ny * nxh * seq_rows) ** (-0.5)

        key, pack, *dwv = own_call(
            grid,
            dp,
            ctx,
            q_nope[0],
            q_rope[0],
            d_out[0],
            saved_out[0],
            lse[0].T,
            latent[0],
            rope_key[0].T,
            w_uv,
        )

        half = nz // 2
        back, ahead = {0: key}, {0: key}
        for s in range(1, half):
            back[s] = z_send(back[s - 1], 1)
            ahead[s] = z_send(ahead[s - 1], -1)
            back[s], ahead[s] = lax.optimization_barrier((back[s], ahead[s]))
        far = jnp.concatenate(
            [z_send(back[half - 1][:ch], 1), z_send(ahead[half - 1][ch:], -1)], axis=0
        )
        offsets = [0]
        keys = [key]
        for s in range(1, half):
            offsets += [s, -s]
            keys += [ahead[s], back[s]]
        offsets.append(half)
        keys.append(far)

        pack_x = xl_swap(pack)
        pack_c = c_swap(pack)
        pack_x, _ = lax.optimization_barrier((pack_x, back[half - 1]))
        packs = [pack, pack_x, pack_c, c_swap(pack_x)]

        dwv, dwv_send = dwv
        dwv_got = c_swap(dwv_send)
        res = attn_call(
            grid, offsets, span_ids, dp, ctx, packs, keys, w_uk, w_uv, heads * dr, scaling
        )
        nb = len(offsets)
        far_up, far_down = res[:2]
        parts = dict(zip(offsets[:-1], res[2 : nb + 1]))
        dq, dq_send, dwk, dwk_send = res[nb + 1 :]

        t = jnp.concatenate(
            [by_x(add(dwk, c_swap(dwk_send)), hd), by_x(add(dwv, dwv_got), hd)], axis=2
        )
        t = add(t[0], *[y_send(t[s], s) for s in range(1, ny)])
        t = add(t[0], *[x_send(t[s], s) for s in range(1, nx)])
        bit = 1
        while bit < nz:
            t = add(t, z_flip(t, bit))
            bit *= 2
        t = jnp.concatenate([t] + [x_send(t, s) for s in range(1, nx)], axis=0)
        pieces = [t] + [y_send(t, s) for s in range(1, ny)]
        pieces += [c_swap(p) for p in pieces]

        plus, minus = z_send(far_up, 1), z_send(far_down, -1)
        for o in range(half - 1, 0, -1):
            if o == half - 1:
                up = jnp.concatenate([add(parts[o][:ch], plus), parts[o][ch:]], axis=0)
                down = jnp.concatenate([parts[-o][:ch], add(parts[-o][ch:], minus)], axis=0)
            else:
                up, down = add(parts[o], plus), add(parts[-o], minus)
            up, down = lax.optimization_barrier((up, down))
            plus, minus = z_send(up, 1), z_send(down, -1)

        q = add(dq, c_swap(dq_send))
        back = xl_swap(q[1])

        d_q_nope, d_q_rope, d_latent, d_rope_key, d_w_uk, d_w_uv = final_call(
            grid, heads, hd, dr, grad_scale, dp, ctx, parts[0], plus, minus, q, back, pieces
        )
        return (d_q_nope[None], d_q_rope[None], d_latent[None], d_rope_key.T[None], d_w_uk, d_w_uv)

    return local


def solution(mesh):
    dp, ctx = mesh.shape["dp"], mesh.shape["ctx"]
    grid = (dp // 2, 2, ctx // 4, 2, 2)
    rows = P("dp", "ctx", None)
    in_specs = (P("dp", None), rows, rows, P(), rows, rows, P(), rows, rows, rows)
    out_specs = (rows, rows, rows, rows, P(), P())
    return jax.shard_map(
        make_local(grid), mesh=mesh, in_specs=in_specs, out_specs=out_specs, check_vma=False
    )
```

profile of v0, /device:TPU:1, one launch (start us, length us, event | category | flops | bytes accessed | tf_op | source)
XLA Modules:
  0.0 152.3 jit_solution(5348193351476057012)
XLA Ops:
  0.7 4.0 %own_rows.1 = (bf16[128,640]{1,0:T(8,128)(2,1)}, bf16[128,2688]{1,0:T(8,128)(2,1)}, bf16[4,128,512]{2,1,0:T(8,128)(2,1)}, bf16[4,128,512]{2,1,0:T(8,128)(2,1)}) custom-call(s32[1]{0:T(128)} %bitcast.dp_ref.refs_1_, s32[1]{0:T(128)} %bitcast.1.ctx_ref.refs_2_, bf16[128,1024]{1,0:T(8,128)(2,1)} %bitcast.50, bf16[128,512]{1,0:T(8,128)(2,1)} %bitcast.53, ...), custom_call_target="tpu_custom_call" | custom-call | flops 4000000000 | bytes 4000000 | tf_op jit(solution)/shard_map/own_rows/pallas_call | solution.py:102
  4.7 2.0 %collective-permute-start = (bf16[128,2688]{1,0:T(8,128)(2,1)}, bf16[128,2688]{1,0:T(8,128)(2,1)S(1)}, u32[]{:S(2)}, u32[]{:S(2)}) collective-permute-start(bf16[128,2688]{1,0:T(8,128)(2,1)} %get-tuple-element.42.refs_3_), channel_id=1, source_target_pairs={{0,2},{1,3},{2,0},{3,1},{4,6},{5,7},{6,4},{7,5},{8,10},{9,11},{10,... | collective-permute-start | bytes 2064392 | tf_op jit(solution)/shard_map/ppermute | solution.py:427
  6.7 5.6 %collective-permute-start.2 = (bf16[128,640]{1,0:T(8,128)(2,1)}, bf16[128,640]{1,0:T(8,128)(2,1)S(1)}, u32[]{:S(2)}, u32[]{:S(2)}) collective-permute-start(bf16[128,640]{1,0:T(8,128)(2,1)} %get-tuple-element.43.refs_7_), channel_id=1, source_target_pairs={{0,28},{1,29},{2,30},{3,31},{4,0},{5,1},{6,2},{7,3},{8,4},{9,5},{1... | collective-permute-start | bytes 491528 | tf_op jit(solution)/shard_map/ppermute | solution.py:427
  12.3 2.9 %collective-permute-done.2.refs_8_ = bf16[128,640]{1,0:T(8,128)(2,1)S(1)} collective-permute-done((bf16[128,640]{1,0:T(8,128)(2,1)}, bf16[128,640]{1,0:T(8,128)(2,1)S(1)}, u32[]{:S(2)}, u32[]{:S(2)}) %collective-permute-start.2) | collective-permute-done | bytes 163872 | tf_op jit(solution)/shard_map/ppermute | solution.py:427
  15.2 2.7 %collective-permute-done.1.refs_9_ = bf16[128,640]{1,0:T(8,128)(2,1)S(1)} collective-permute-done((bf16[128,640]{1,0:T(8,128)(2,1)}, bf16[128,640]{1,0:T(8,128)(2,1)S(1)}, u32[]{:S(2)}, u32[]{:S(2)}) %collective-permute-start.1) | collective-permute-done | bytes 163872 | tf_op jit(solution)/shard_map/ppermute | solution.py:427
  17.9 2.7 %collective-permute-start.4 = (bf16[128,640]{1,0:T(8,128)(2,1)S(1)}, bf16[128,640]{1,0:T(8,128)(2,1)S(1)}, u32[]{:S(2)}, u32[]{:S(2)}) collective-permute-start(bf16[128,640]{1,0:T(8,128)(2,1)S(1)} %collective-permute-done.2.refs_8_), channel_id=1, source_target_pairs={{0,28},{1,29},{2,30},{3,31},{4,0},{5,1},{6,2},{7,3},{8,4},{9,5},{1... | collective-permute-start | bytes 491528 | tf_op jit(solution)/shard_map/ppermute | solution.py:427
  20.6 2.7 %collective-permute-done.3.refs_11_ = bf16[128,640]{1,0:T(8,128)(2,1)S(1)} collective-permute-done((bf16[128,640]{1,0:T(8,128)(2,1)S(1)}, bf16[128,640]{1,0:T(8,128)(2,1)S(1)}, u32[]{:S(2)}, u32[]{:S(2)}) %collective-permute-start.3) | collective-permute-done | bytes 163872 | tf_op jit(solution)/shard_map/ppermute | solution.py:427
  23.3 2.7 %collective-permute-start.6 = (bf16[128,640]{1,0:T(8,128)(2,1)S(1)}, bf16[128,640]{1,0:T(8,128)(2,1)S(1)}, u32[]{:S(2)}, u32[]{:S(2)}) collective-permute-start(bf16[128,640]{1,0:T(8,128)(2,1)S(1)} %collective-permute-done.4.refs_10_), channel_id=1, source_target_pairs={{0,28},{1,29},{2,30},{3,31},{4,0},{5,1},{6,2},{7,3},{8,4},{9,5},{1... | collective-permute-start | bytes 491528 | tf_op jit(solution)/shard_map/ppermute | solution.py:427
  26.0 4.2 %collective-permute-start.7 = (bf16[128,2688]{1,0:T(8,128)(2,1)}, bf16[128,2688]{1,0:T(8,128)(2,1)S(1)}, u32[]{:S(2)}, u32[]{:S(2)}) collective-permute-start(bf16[128,2688]{1,0:T(8,128)(2,1)} %get-tuple-element.42.refs_3_), channel_id=1, source_target_pairs={{0,1},{1,0},{2,3},{3,2},{4,5},{5,4},{6,7},{7,6},{8,9},{9,8},{10,11... | collective-permute-start | bytes 2064392 | tf_op jit(solution)/shard_map/ppermute | solution.py:427
  30.1 3.3 %collective-permute-start.8 = (bf16[128,2688]{1,0:T(8,128)(2,1)S(1)}, bf16[128,2688]{1,0:T(8,128)(2,1)S(1)}, u32[]{:S(2)}, u32[]{:S(2)}) collective-permute-start(bf16[128,2688]{1,0:T(8,128)(2,1)S(1)} %collective-permute-done.refs_4_), channel_id=1, source_target_pairs={{0,1},{1,0},{2,3},{3,2},{4,5},{5,4},{6,7},{7,6},{8,9},{9,8},{10,11... | collective-permute-start | bytes 2064392 | tf_op jit(solution)/shard_map/ppermute | solution.py:427
  33.5 3.0 %collective-permute-start.10 = (bf16[64,640]{1,0:T(8,128)(2,1)S(1)}, bf16[64,640]{1,0:T(8,128)(2,1)S(1)}, u32[]{:S(2)}, u32[]{:S(2)}) collective-permute-start(bf16[64,640]{1,0:T(8,128)(2,1)S(1)} %slice.46), channel_id=1, source_target_pairs={{0,28},{1,29},{2,30},{3,31},{4,0},{5,1},{6,2},{7,3},{8,4},{9,5},{1... | collective-permute-start | bytes 245768 | tf_op jit(solution)/shard_map/ppermute | solution.py:427
  36.8 2.4 %collective-permute-done.9 = bf16[64,640]{1,0:T(8,128)(2,1)S(1)} collective-permute-done((bf16[64,640]{1,0:T(8,128)(2,1)S(1)}, bf16[64,640]{1,0:T(8,128)(2,1)S(1)}, u32[]{:S(2)}, u32[]{:S(2)}) %collective-permute-start.9) | collective-permute-done | bytes 81952 | tf_op jit(solution)/shard_map/ppermute | solution.py:427
  39.4 1.1 copy-done.2
  40.5 0.9 copy-done.3
  41.4 34.2 %attn_grads.1 = (bf16[64,640]{1,0:T(8,128)(2,1)S(1)}, bf16[64,640]{1,0:T(8,128)(2,1)S(1)}, bf16[128,640]{1,0:T(8,128)(2,1)S(1)}, bf16[128,640]{1,0:T(8,128)(2,1)...) custom-call(s32[1,64]{1,0:T(1,128)S(1)} %copy-done.4, ...), custom_call_target="tpu_custom_call" | custom-call | flops 30000001024 | bytes 10000000 | tf_op jit(solution)/shard_map/attn_grads/pallas_call | solution.py:328
  75.6 0.7 collective-permute-start.21
  76.7 2.7 %collective-permute-start.12 = (bf16[64,640]{1,0:T(8,128)(2,1)S(1)}, bf16[64,640]{1,0:T(8,128)(2,1)S(1)}, u32[]{:S(2)}, u32[]{:S(2)}) collective-permute-start(bf16[64,640]{1,0:T(8,128)(2,1)S(1)} %get-tuple-element.57), channel_id=1, source_target_pairs={{0,28},{1,29},{2,30},{3,31},{4,0},{5,1},{6,2},{7,3},{8,4},{9,5},{1... | collective-permute-start | bytes 245768 | tf_op jit(solution)/shard_map/ppermute | solution.py:427
  79.4 0.4 collective-permute-start.19
  79.8 2.0 %collective-permute-done.11 = bf16[64,640]{1,0:T(8,128)(2,1)S(1)} collective-permute-done((bf16[64,640]{1,0:T(8,128)(2,1)S(1)}, bf16[64,640]{1,0:T(8,128)(2,1)S(1)}, u32[]{:S(2)}, u32[]{:S(2)}) %collective-permute-start.11) | collective-permute-done | bytes 81952 | tf_op jit(solution)/shard_map/ppermute | solution.py:427
  82.1 1.3 collective-permute-start.23
  83.3 2.7 %collective-permute-start.25 = (bf16[4,64,512]{2,1,0:T(8,128)(2,1)S(1)}, bf16[4,64,512]{2,1,0:T(8,128)(2,1)S(1)}, u32[]{:S(2)}, u32[]{:S(2)}) collective-permute-start(bf16[4,64,512]{2,1,0:T(8,128)(2,1)S(1)} %get-tuple-element.79), channel_id=1, source_target_pairs={{0,192},{1,193},{2,194},{3,195},{4,196},{5,197},{6,198},{7,199},{8... | collective-permute-start | bytes 786440 | tf_op jit(solution)/shard_map/ppermute | solution.py:427
  86.1 1.1 collective-permute-start.24
  87.3 4.7 %collective-permute-done.23 = bf16[4,64,512]{2,1,0:T(8,128)(2,1)S(1)} collective-permute-done((bf16[4,64,512]{2,1,0:T(8,128)(2,1)S(1)}, bf16[4,64,512]{2,1,0:T(8,128)(2,1)S(1)}, u32[]{:S(2)}, u32[]{:S(2)}) %collective-permute-start.23) | collective-permute-done | bytes 262176 | tf_op jit(solution)/shard_map/ppermute | solution.py:427
  92.0 1.1 collective-permute-start.14
  93.1 5.4 %collective-permute-done.24 = bf16[4,64,512]{2,1,0:T(8,128)(2,1)S(1)} collective-permute-done((bf16[4,64,512]{2,1,0:T(8,128)(2,1)S(1)}, bf16[4,64,512]{2,1,0:T(8,128)(2,1)S(1)}, u32[]{:S(2)}, u32[]{:S(2)}) %collective-permute-start.24) | collective-permute-done | bytes 262176 | tf_op jit(solution)/shard_map/ppermute | solution.py:427
  98.7 2.7 %collective-permute-start.28 = (bf16[64,512]{1,0:T(8,128)(2,1)S(1)}, bf16[64,512]{1,0:T(8,128)(2,1)S(1)}, u32[]{:S(2)}, u32[]{:S(2)}) collective-permute-start(bf16[64,512]{1,0:T(8,128)(2,1)S(1)} %get-tuple-element.82), channel_id=1, source_target_pairs={{0,34},{1,35},{2,0},{3,1},{4,38},{5,39},{6,4},{7,5},{8,42},{9,43},... | collective-permute-start | bytes 196616 | tf_op jit(solution)/shard_map/ppermute | solution.py:427
  101.5 1.6 %collective-permute-done.26 = bf16[64,512]{1,0:T(8,128)(2,1)S(1)} collective-permute-done((bf16[64,512]{1,0:T(8,128)(2,1)S(1)}, bf16[64,512]{1,0:T(8,128)(2,1)S(1)}, u32[]{:S(2)}, u32[]{:S(2)}) %collective-permute-start.26) | collective-permute-done | bytes 65568 | tf_op jit(solution)/shard_map/ppermute | solution.py:427
  103.3 2.7 %collective-permute-done.27 = bf16[64,512]{1,0:T(8,128)(2,1)S(1)} collective-permute-done((bf16[64,512]{1,0:T(8,128)(2,1)S(1)}, bf16[64,512]{1,0:T(8,128)(2,1)S(1)}, u32[]{:S(2)}, u32[]{:S(2)}) %collective-permute-start.27) | collective-permute-done | bytes 65568 | tf_op jit(solution)/shard_map/ppermute | solution.py:427
  106.2 1.5 collective-permute-start.15
  107.7 1.2 collective-permute-start.16
  109.4 2.3 %collective-permute-done.15 = bf16[128,640]{1,0:T(8,128)(2,1)S(1)} collective-permute-done((bf16[128,640]{1,0:T(8,128)(2,1)S(1)}, bf16[128,640]{1,0:T(8,128)(2,1)S(1)}, u32[]{:S(2)}, u32[]{:S(2)}) %collective-permute-start.15) | collective-permute-done | bytes 163872 | tf_op jit(solution)/shard_map/ppermute | solution.py:427
  111.7 2.4 %collective-permute-done.30 = bf16[64,512]{1,0:T(8,128)(2,1)S(1)} collective-permute-done((bf16[64,512]{1,0:T(8,128)(2,1)S(1)}, bf16[64,512]{1,0:T(8,128)(2,1)S(1)}, u32[]{:S(2)}, u32[]{:S(2)}) %collective-permute-start.30) | collective-permute-done | bytes 65568 | tf_op jit(solution)/shard_map/ppermute | solution.py:427
  114.1 2.4 %collective-permute-start.31 = (bf16[64,512]{1,0:T(8,128)(2,1)S(1)}, bf16[64,512]{1,0:T(8,128)(2,1)S(1)}, u32[]{:S(2)}, u32[]{:S(2)}) collective-permute-start(bf16[64,512]{1,0:T(8,128)(2,1)S(1)} %add_convert_fusion.10), channel_id=1, source_target_pairs={{0,16},{1,17},{2,18},{3,19},{4,20},{5,21},{6,22},{7,23},{8,24},{9,... | collective-permute-start | bytes 196616 | tf_op jit(solution)/shard_map/ppermute | solution.py:427
  116.7 2.7 %collective-permute-start.18 = (bf16[128,640]{1,0:T(8,128)(2,1)S(1)}, bf16[128,640]{1,0:T(8,128)(2,1)S(1)}, u32[]{:S(2)}, u32[]{:S(2)}) collective-permute-start(bf16[128,640]{1,0:T(8,128)(2,1)S(1)} %add_convert_fusion.3), channel_id=1, source_target_pairs={{0,28},{1,29},{2,30},{3,31},{4,0},{5,1},{6,2},{7,3},{8,4},{9,5},{1... | collective-permute-start | bytes 491528 | tf_op jit(solution)/shard_map/ppermute | solution.py:427
  119.4 2.8 %collective-permute-done.31 = bf16[64,512]{1,0:T(8,128)(2,1)S(1)} collective-permute-done((bf16[64,512]{1,0:T(8,128)(2,1)S(1)}, bf16[64,512]{1,0:T(8,128)(2,1)S(1)}, u32[]{:S(2)}, u32[]{:S(2)}) %collective-permute-start.31) | collective-permute-done | bytes 65568 | tf_op jit(solution)/shard_map/ppermute | solution.py:427
  122.4 0.6 collective-permute-start.33
  123.0 0.8 collective-permute-start.32
  124.0 1.4 collective-permute-done.34
  125.4 1.9 %collective-permute-done.33 = bf16[64,512]{1,0:T(8,128)(2,1)S(1)} collective-permute-done((bf16[64,512]{1,0:T(8,128)(2,1)S(1)}, bf16[64,512]{1,0:T(8,128)(2,1)S(1)}, u32[]{:S(2)}, u32[]{:S(2)}) %collective-permute-start.33) | collective-permute-done | bytes 65568 | tf_op jit(solution)/shard_map/ppermute | solution.py:427
  127.3 0.8 collective-permute-done.32
  128.1 1.9 %collective-permute-start.37 = (bf16[256,512]{1,0:T(8,128)(2,1)S(1)}, bf16[256,512]{1,0:T(8,128)(2,1)S(1)}, u32[]{:S(2)}, u32[]{:S(2)}) collective-permute-start(bf16[256,512]{1,0:T(8,128)(2,1)S(1)} %pad_maximum_fusion.1.refs_0_), channel_id=1, source_target_pairs={{0,192},{1,193},{2,194},{3,195},{4,196},{5,197},{6,198},{7,199},{8... | collective-permute-start | bytes 786440 | tf_op jit(solution)/shard_map/ppermute | solution.py:427
  130.0 0.7 collective-permute-start.36
  131.0 10.5 %collective-permute-start.38 = (bf16[256,512]{1,0:T(8,128)(2,1)S(1)}, bf16[256,512]{1,0:T(8,128)(2,1)S(1)}, u32[]{:S(2)}, u32[]{:S(2)}) collective-permute-start(bf16[256,512]{1,0:T(8,128)(2,1)S(1)} %pad_maximum_fusion.1.refs_0_), channel_id=1, source_target_pairs={{0,1},{1,0},{2,3},{3,2},{4,5},{5,4},{6,7},{7,6},{8,9},{9,8},{10,11... | collective-permute-start | bytes 786440 | tf_op jit(solution)/shard_map/ppermute | solution.py:427
  141.5 2.4 %collective-permute-start.41 = (bf16[256,512]{1,0:T(8,128)(2,1)S(1)}, bf16[256,512]{1,0:T(8,128)(2,1)S(1)}, u32[]{:S(2)}, u32[]{:S(2)}) collective-permute-start(bf16[256,512]{1,0:T(8,128)(2,1)S(1)} %collective-permute-done.37.refs_3_), channel_id=1, source_target_pairs={{0,1},{1,0},{2,3},{3,2},{4,5},{5,4},{6,7},{7,6},{8,9},{9,8},{10,11... | collective-permute-start | bytes 786440 | tf_op jit(solution)/shard_map/ppermute | solution.py:427
  143.9 1.9 %collective-permute-start.40 = (bf16[256,512]{1,0:T(8,128)(2,1)S(1)}, bf16[256,512]{1,0:T(8,128)(2,1)S(1)}, u32[]{:S(2)}, u32[]{:S(2)}) collective-permute-start(bf16[256,512]{1,0:T(8,128)(2,1)S(1)} %collective-permute-done.36.refs_2_), channel_id=1, source_target_pairs={{0,1},{1,0},{2,3},{3,2},{4,5},{5,4},{6,7},{7,6},{8,9},{9,8},{10,11... | collective-permute-start | bytes 786440 | tf_op jit(solution)/shard_map/ppermute | solution.py:427
  145.8 2.7 %collective-permute-start.39 = (bf16[256,512]{1,0:T(8,128)(2,1)S(1)}, bf16[256,512]{1,0:T(8,128)(2,1)S(1)}, u32[]{:S(2)}, u32[]{:S(2)}) collective-permute-start(bf16[256,512]{1,0:T(8,128)(2,1)S(1)} %collective-permute-done.35.refs_1_), channel_id=1, source_target_pairs={{0,1},{1,0},{2,3},{3,2},{4,5},{5,4},{6,7},{7,6},{8,9},{9,8},{10,11... | collective-permute-start | bytes 786440 | tf_op jit(solution)/shard_map/ppermute | solution.py:427
  148.5 1.1 collective-permute-done.39.refs_5_
  149.7 2.6 %outputs.1 = (bf16[128,1024]{1,0:T(8,128)(2,1)}, bf16[128,512]{1,0:T(8,128)(2,1)}, bf16[128,512]{1,0:T(8,128)(2,1)}, bf16[64,128]{1,0:T(8,128)(2,1)}, f32[8,128,512]{2,1,0:T(8,128)}, /*index=5*/f32[8,512,128]{2,1,0:T(8,128)}) custom-call(s32[1]{0:T(128)} %bitcast.dp_ref.refs_1_, s32[1]{0:T(128)} %bitcast.1.ctx_ref.refs_2_, ...), custom_call_target="tpu_custom_call" | custom-call | tf_op jit(solution)/shard_map/outputs/pallas_call | solution.py:399
  (76 shorter events, 3.2 us)
Async XLA Ops:
  0.6 38.7 %copy-start = (bf16[8,512,128]{2,1,0:T(8,128)(2,1)S(1)}, bf16[8,512,128]{2,1,0:T(8,128)(2,1)}, u32[]{:S(2)}) copy-start(bf16[8,512,128]{2,1,0:T(8,128)(2,1)} %refs_16_.1) | copy-start | bytes 3145732
  0.7 38.7 %copy-start.1 = (bf16[8,128,512]{2,1,0:T(8,128)(2,1)S(1)}, bf16[8,128,512]{2,1,0:T(8,128)(2,1)}, u32[]{:S(2)}) copy-start(bf16[8,128,512]{2,1,0:T(8,128)(2,1)} %refs_15_.1) | copy-start | bytes 3145732
  0.7 38.7 %copy-start.4 = (s32[1,64]{1,0:T(1,128)S(1)}, s32[1,64]{1,0:T(1,128)}, u32[]{:S(2)}) copy-start(s32[1,64]{1,0:T(1,128)} %refs_0_.1) | copy-start | bytes 772
  4.7 25.4 %collective-permute-start = (bf16[128,2688]{1,0:T(8,128)(2,1)}, bf16[128,2688]{1,0:T(8,128)(2,1)S(1)}, u32[]{:S(2)}, u32[]{:S(2)}) collective-permute-start(bf16[128,2688]{1,0:T(8,128)(2,1)} %get-tuple-element.42.refs_3_), channel_id=1, source_target_pairs={{0,2},{1,3},{2,0},{3,1},{4,6},{5,7},{6,4},{7,5},{8,10},{9,11},{10,... | collective-permute-start | bytes 2064392 | tf_op jit(solution)/shard_map/ppermute | solution.py:427
  6.7 8.4 %collective-permute-start.2 = (bf16[128,640]{1,0:T(8,128)(2,1)}, bf16[128,640]{1,0:T(8,128)(2,1)S(1)}, u32[]{:S(2)}, u32[]{:S(2)}) collective-permute-start(bf16[128,640]{1,0:T(8,128)(2,1)} %get-tuple-element.43.refs_7_), channel_id=1, source_target_pairs={{0,28},{1,29},{2,30},{3,31},{4,0},{5,1},{6,2},{7,3},{8,4},{9,5},{1... | collective-permute-start | bytes 491528 | tf_op jit(solution)/shard_map/ppermute | solution.py:427
  12.3 5.6 %collective-permute-start.1 = (bf16[128,640]{1,0:T(8,128)(2,1)}, bf16[128,640]{1,0:T(8,128)(2,1)S(1)}, u32[]{:S(2)}, u32[]{:S(2)}) collective-permute-start(bf16[128,640]{1,0:T(8,128)(2,1)} %get-tuple-element.43.refs_7_), channel_id=1, source_target_pairs={{0,4},{1,5},{2,6},{3,7},{4,8},{5,9},{6,10},{7,11},{8,12},{9,13},{1... | collective-permute-start | bytes 491528 | tf_op jit(solution)/shard_map/ppermute | solution.py:427
  17.9 5.4 %collective-permute-start.3 = (bf16[128,640]{1,0:T(8,128)(2,1)S(1)}, bf16[128,640]{1,0:T(8,128)(2,1)S(1)}, u32[]{:S(2)}, u32[]{:S(2)}) collective-permute-start(bf16[128,640]{1,0:T(8,128)(2,1)S(1)} %collective-permute-done.1.refs_9_), channel_id=1, source_target_pairs={{0,4},{1,5},{2,6},{3,7},{4,8},{5,9},{6,10},{7,11},{8,12},{9,13},{1... | collective-permute-start | bytes 491528 | tf_op jit(solution)/shard_map/ppermute | solution.py:427
  17.9 5.4 %collective-permute-start.4 = (bf16[128,640]{1,0:T(8,128)(2,1)S(1)}, bf16[128,640]{1,0:T(8,128)(2,1)S(1)}, u32[]{:S(2)}, u32[]{:S(2)}) collective-permute-start(bf16[128,640]{1,0:T(8,128)(2,1)S(1)} %collective-permute-done.2.refs_8_), channel_id=1, source_target_pairs={{0,28},{1,29},{2,30},{3,31},{4,0},{5,1},{6,2},{7,3},{8,4},{9,5},{1... | collective-permute-start | bytes 491528 | tf_op jit(solution)/shard_map/ppermute | solution.py:427
  23.3 6.8 %collective-permute-start.5 = (bf16[128,640]{1,0:T(8,128)(2,1)S(1)}, bf16[128,640]{1,0:T(8,128)(2,1)S(1)}, u32[]{:S(2)}, u32[]{:S(2)}) collective-permute-start(bf16[128,640]{1,0:T(8,128)(2,1)S(1)} %collective-permute-done.3.refs_11_), channel_id=1, source_target_pairs={{0,4},{1,5},{2,6},{3,7},{4,8},{5,9},{6,10},{7,11},{8,12},{9,13},{1... | collective-permute-start | bytes 491528 | tf_op jit(solution)/shard_map/ppermute | solution.py:427
  23.3 6.8 %collective-permute-start.6 = (bf16[128,640]{1,0:T(8,128)(2,1)S(1)}, bf16[128,640]{1,0:T(8,128)(2,1)S(1)}, u32[]{:S(2)}, u32[]{:S(2)}) collective-permute-start(bf16[128,640]{1,0:T(8,128)(2,1)S(1)} %collective-permute-done.4.refs_10_), channel_id=1, source_target_pairs={{0,28},{1,29},{2,30},{3,31},{4,0},{5,1},{6,2},{7,3},{8,4},{9,5},{1... | collective-permute-start | bytes 491528 | tf_op jit(solution)/shard_map/ppermute | solution.py:427
  26.0 13.3 %collective-permute-start.7 = (bf16[128,2688]{1,0:T(8,128)(2,1)}, bf16[128,2688]{1,0:T(8,128)(2,1)S(1)}, u32[]{:S(2)}, u32[]{:S(2)}) collective-permute-start(bf16[128,2688]{1,0:T(8,128)(2,1)} %get-tuple-element.42.refs_3_), channel_id=1, source_target_pairs={{0,1},{1,0},{2,3},{3,2},{4,5},{5,4},{6,7},{7,6},{8,9},{9,8},{10,11... | collective-permute-start | bytes 2064392 | tf_op jit(solution)/shard_map/ppermute | solution.py:427
  30.1 9.2 %collective-permute-start.8 = (bf16[128,2688]{1,0:T(8,128)(2,1)S(1)}, bf16[128,2688]{1,0:T(8,128)(2,1)S(1)}, u32[]{:S(2)}, u32[]{:S(2)}) collective-permute-start(bf16[128,2688]{1,0:T(8,128)(2,1)S(1)} %collective-permute-done.refs_4_), channel_id=1, source_target_pairs={{0,1},{1,0},{2,3},{3,2},{4,5},{5,4},{6,7},{7,6},{8,9},{9,8},{10,11... | collective-permute-start | bytes 2064392 | tf_op jit(solution)/shard_map/ppermute | solution.py:427
  33.4 5.8 %collective-permute-start.9 = (bf16[64,640]{1,0:T(8,128)(2,1)S(1)}, bf16[64,640]{1,0:T(8,128)(2,1)S(1)}, u32[]{:S(2)}, u32[]{:S(2)}) collective-permute-start(bf16[64,640]{1,0:T(8,128)(2,1)S(1)} %slice.45), channel_id=1, source_target_pairs={{0,4},{1,5},{2,6},{3,7},{4,8},{5,9},{6,10},{7,11},{8,12},{9,13},{1... | collective-permute-start | bytes 245768 | tf_op jit(solution)/shard_map/ppermute | solution.py:427
  33.5 5.7 %collective-permute-start.10 = (bf16[64,640]{1,0:T(8,128)(2,1)S(1)}, bf16[64,640]{1,0:T(8,128)(2,1)S(1)}, u32[]{:S(2)}, u32[]{:S(2)}) collective-permute-start(bf16[64,640]{1,0:T(8,128)(2,1)S(1)} %slice.46), channel_id=1, source_target_pairs={{0,28},{1,29},{2,30},{3,31},{4,0},{5,1},{6,2},{7,3},{8,4},{9,5},{1... | collective-permute-start | bytes 245768 | tf_op jit(solution)/shard_map/ppermute | solution.py:427
  36.6 39.9 %collective-permute-start.22 = (bf16[4,128,512]{2,1,0:T(8,128)(2,1)}, bf16[4,128,512]{2,1,0:T(8,128)(2,1)S(1)}, u32[]{:S(2)}, u32[]{:S(2)}) collective-permute-start(bf16[4,128,512]{2,1,0:T(8,128)(2,1)} %get-tuple-element.71), channel_id=1, source_target_pairs={{0,1},{1,0},{2,3},{3,2},{4,5},{5,4},{6,7},{7,6},{8,9},{9,8},{10,11... | collective-permute-start | bytes 1572872 | tf_op jit(solution)/shard_map/ppermute | solution.py:427
  39.4 1.1 copy-start.2
  40.5 0.9 copy-start.3
  41.4 35.1 %copy-start.5 = (bf16[4,128,512]{2,1,0:T(8,128)(2,1)S(1)}, bf16[4,128,512]{2,1,0:T(8,128)(2,1)}, u32[]{:S(2)}) copy-start(bf16[4,128,512]{2,1,0:T(8,128)(2,1)} %get-tuple-element.70) | copy-start | bytes 1572868
  75.6 6.3 %collective-permute-start.21 = (bf16[4,128,512]{2,1,0:T(8,128)(2,1)S(1)}, bf16[4,128,512]{2,1,0:T(8,128)(2,1)S(1)}, u32[]{:S(2)}, u32[]{:S(2)}) collective-permute-start(bf16[4,128,512]{2,1,0:T(8,128)(2,1)S(1)} %get-tuple-element.69), channel_id=1, source_target_pairs={{0,1},{1,0},{2,3},{3,2},{4,5},{5,4},{6,7},{7,6},{8,9},{9,8},{10,11... | collective-permute-start | bytes 1572872 | tf_op jit(solution)/shard_map/ppermute | solution.py:427
  76.2 5.6 %collective-permute-start.11 = (bf16[64,640]{1,0:T(8,128)(2,1)S(1)}, bf16[64,640]{1,0:T(8,128)(2,1)S(1)}, u32[]{:S(2)}, u32[]{:S(2)}) collective-permute-start(bf16[64,640]{1,0:T(8,128)(2,1)S(1)} %get-tuple-element.55), channel_id=1, source_target_pairs={{0,4},{1,5},{2,6},{3,7},{4,8},{5,9},{6,10},{7,11},{8,12},{9,13},{1... | collective-permute-start | bytes 245768 | tf_op jit(solution)/shard_map/ppermute | solution.py:427
  76.7 10.5 %collective-permute-start.12 = (bf16[64,640]{1,0:T(8,128)(2,1)S(1)}, bf16[64,640]{1,0:T(8,128)(2,1)S(1)}, u32[]{:S(2)}, u32[]{:S(2)}) collective-permute-start(bf16[64,640]{1,0:T(8,128)(2,1)S(1)} %get-tuple-element.57), channel_id=1, source_target_pairs={{0,28},{1,29},{2,30},{3,31},{4,0},{5,1},{6,2},{7,3},{8,4},{9,5},{1... | collective-permute-start | bytes 245768 | tf_op jit(solution)/shard_map/ppermute | solution.py:427
  79.4 43.6 %collective-permute-start.19 = (bf16[2,128,1536]{2,1,0:T(8,128)(2,1)S(1)}, bf16[2,128,1536]{2,1,0:T(8,128)(2,1)S(1)}, u32[]{:S(2)}, u32[]{:S(2)}) collective-permute-start(bf16[2,128,1536]{2,1,0:T(8,128)(2,1)S(1)} %get-tuple-element.67), channel_id=1, source_target_pairs={{0,1},{1,0},{2,3},{3,2},{4,5},{5,4},{6,7},{7,6},{8,9},{9,8},{10,11... | collective-permute-start | bytes 2359304 | tf_op jit(solution)/shard_map/ppermute | solution.py:427
  82.1 9.9 %collective-permute-start.23 = (bf16[4,64,512]{2,1,0:T(8,128)(2,1)S(1)}, bf16[4,64,512]{2,1,0:T(8,128)(2,1)S(1)}, u32[]{:S(2)}, u32[]{:S(2)}) collective-permute-start(bf16[4,64,512]{2,1,0:T(8,128)(2,1)S(1)} %get-tuple-element.78), channel_id=1, source_target_pairs={{0,64},{1,65},{2,66},{3,67},{4,68},{5,69},{6,70},{7,71},{8,72},{9,... | collective-permute-start | bytes 786440 | tf_op jit(solution)/shard_map/ppermute | solution.py:427
  83.3 9.7 %collective-permute-start.25 = (bf16[4,64,512]{2,1,0:T(8,128)(2,1)S(1)}, bf16[4,64,512]{2,1,0:T(8,128)(2,1)S(1)}, u32[]{:S(2)}, u32[]{:S(2)}) collective-permute-start(bf16[4,64,512]{2,1,0:T(8,128)(2,1)S(1)} %get-tuple-element.79), channel_id=1, source_target_pairs={{0,192},{1,193},{2,194},{3,195},{4,196},{5,197},{6,198},{7,199},{8... | collective-permute-start | bytes 786440 | tf_op jit(solution)/shard_map/ppermute | solution.py:427
  86.1 12.4 %collective-permute-start.24 = (bf16[4,64,512]{2,1,0:T(8,128)(2,1)S(1)}, bf16[4,64,512]{2,1,0:T(8,128)(2,1)S(1)}, u32[]{:S(2)}, u32[]{:S(2)}) collective-permute-start(bf16[4,64,512]{2,1,0:T(8,128)(2,1)S(1)} %get-tuple-element.80), channel_id=1, source_target_pairs={{0,128},{1,129},{2,130},{3,131},{4,132},{5,133},{6,134},{7,135},{8... | collective-permute-start | bytes 786440 | tf_op jit(solution)/shard_map/ppermute | solution.py:427
  87.2 14.2 %collective-permute-start.13 = (bf16[128,640]{1,0:T(8,128)(2,1)S(1)}, bf16[128,640]{1,0:T(8,128)(2,1)S(1)}, u32[]{:S(2)}, u32[]{:S(2)}) collective-permute-start(bf16[128,640]{1,0:T(8,128)(2,1)S(1)} %pad_maximum_fusion.3), channel_id=1, source_target_pairs={{0,4},{1,5},{2,6},{3,7},{4,8},{5,9},{6,10},{7,11},{8,12},{9,13},{1... | collective-permute-start | bytes 491528 | tf_op jit(solution)/shard_map/ppermute | solution.py:427
  92.0 14.2 %collective-permute-start.14 = (bf16[128,640]{1,0:T(8,128)(2,1)S(1)}, bf16[128,640]{1,0:T(8,128)(2,1)S(1)}, u32[]{:S(2)}, u32[]{:S(2)}) collective-permute-start(bf16[128,640]{1,0:T(8,128)(2,1)S(1)} %pad_maximum_fusion.4), channel_id=1, source_target_pairs={{0,28},{1,29},{2,30},{3,31},{4,0},{5,1},{6,2},{7,3},{8,4},{9,5},{1... | collective-permute-start | bytes 491528 | tf_op jit(solution)/shard_map/ppermute | solution.py:427
  98.6 4.4 %collective-permute-start.26 = (bf16[64,512]{1,0:T(8,128)(2,1)S(1)}, bf16[64,512]{1,0:T(8,128)(2,1)S(1)}, u32[]{:S(2)}, u32[]{:S(2)}) collective-permute-start(bf16[64,512]{1,0:T(8,128)(2,1)S(1)} %get-tuple-element.81), channel_id=1, source_target_pairs={{0,2},{1,3},{2,32},{3,33},{4,6},{5,7},{6,36},{7,37},{8,10},{9,11},... | collective-permute-start | bytes 196616 | tf_op jit(solution)/shard_map/ppermute | solution.py:427
  98.7 4.6 %collective-permute-start.28 = (bf16[64,512]{1,0:T(8,128)(2,1)S(1)}, bf16[64,512]{1,0:T(8,128)(2,1)S(1)}, u32[]{:S(2)}, u32[]{:S(2)}) collective-permute-start(bf16[64,512]{1,0:T(8,128)(2,1)S(1)} %get-tuple-element.82), channel_id=1, source_target_pairs={{0,34},{1,35},{2,0},{3,1},{4,38},{5,39},{6,4},{7,5},{8,42},{9,43},... | collective-permute-start | bytes 196616 | tf_op jit(solution)/shard_map/ppermute | solution.py:427
  101.4 4.6 %collective-permute-start.27 = (bf16[64,512]{1,0:T(8,128)(2,1)S(1)}, bf16[64,512]{1,0:T(8,128)(2,1)S(1)}, u32[]{:S(2)}, u32[]{:S(2)}) collective-permute-start(bf16[64,512]{1,0:T(8,128)(2,1)S(1)} %get-tuple-element.83), channel_id=1, source_target_pairs={{0,32},{1,33},{2,34},{3,35},{4,36},{5,37},{6,38},{7,39},{8,40},{9,... | collective-permute-start | bytes 196616 | tf_op jit(solution)/shard_map/ppermute | solution.py:427
  106.1 3.2 %collective-permute-start.29 = (bf16[64,512]{1,0:T(8,128)(2,1)S(1)}, bf16[64,512]{1,0:T(8,128)(2,1)S(1)}, u32[]{:S(2)}, u32[]{:S(2)}) collective-permute-start(bf16[64,512]{1,0:T(8,128)(2,1)S(1)} %fusion.12), channel_id=1, source_target_pairs={{0,4},{1,5},{2,6},{3,7},{4,0},{5,1},{6,2},{7,3},{8,12},{9,13},{10,... | collective-permute-start | bytes 196616 | tf_op jit(solution)/shard_map/ppermute | solution.py:427
  106.2 5.5 %collective-permute-start.15 = (bf16[128,640]{1,0:T(8,128)(2,1)S(1)}, bf16[128,640]{1,0:T(8,128)(2,1)S(1)}, u32[]{:S(2)}, u32[]{:S(2)}) collective-permute-start(bf16[128,640]{1,0:T(8,128)(2,1)S(1)} %add_convert_fusion.6), channel_id=1, source_target_pairs={{0,4},{1,5},{2,6},{3,7},{4,8},{5,9},{6,10},{7,11},{8,12},{9,13},{1... | collective-permute-start | bytes 491528 | tf_op jit(solution)/shard_map/ppermute | solution.py:427
  107.7 8.8 %collective-permute-start.16 = (bf16[128,640]{1,0:T(8,128)(2,1)S(1)}, bf16[128,640]{1,0:T(8,128)(2,1)S(1)}, u32[]{:S(2)}, u32[]{:S(2)}) collective-permute-start(bf16[128,640]{1,0:T(8,128)(2,1)S(1)} %add_convert_fusion.5), channel_id=1, source_target_pairs={{0,28},{1,29},{2,30},{3,31},{4,0},{5,1},{6,2},{7,3},{8,4},{9,5},{1... | collective-permute-start | bytes 491528 | tf_op jit(solution)/shard_map/ppermute | solution.py:427
  109.3 4.8 %collective-permute-start.30 = (bf16[64,512]{1,0:T(8,128)(2,1)S(1)}, bf16[64,512]{1,0:T(8,128)(2,1)S(1)}, u32[]{:S(2)}, u32[]{:S(2)}) collective-permute-start(bf16[64,512]{1,0:T(8,128)(2,1)S(1)} %add_convert_fusion.11), channel_id=1, source_target_pairs={{0,8},{1,9},{2,10},{3,11},{4,12},{5,13},{6,14},{7,15},{8,0},{9,1},... | collective-permute-start | bytes 196616 | tf_op jit(solution)/shard_map/ppermute | solution.py:427
  114.1 8.1 %collective-permute-start.31 = (bf16[64,512]{1,0:T(8,128)(2,1)S(1)}, bf16[64,512]{1,0:T(8,128)(2,1)S(1)}, u32[]{:S(2)}, u32[]{:S(2)}) collective-permute-start(bf16[64,512]{1,0:T(8,128)(2,1)S(1)} %add_convert_fusion.10), channel_id=1, source_target_pairs={{0,16},{1,17},{2,18},{3,19},{4,20},{5,21},{6,22},{7,23},{8,24},{9,... | collective-permute-start | bytes 196616 | tf_op jit(solution)/shard_map/ppermute | solution.py:427
  116.6 14.2 %collective-permute-start.17 = (bf16[128,640]{1,0:T(8,128)(2,1)S(1)}, bf16[128,640]{1,0:T(8,128)(2,1)S(1)}, u32[]{:S(2)}, u32[]{:S(2)}) collective-permute-start(bf16[128,640]{1,0:T(8,128)(2,1)S(1)} %add_convert_fusion.4), channel_id=1, source_target_pairs={{0,4},{1,5},{2,6},{3,7},{4,8},{5,9},{6,10},{7,11},{8,12},{9,13},{1... | collective-permute-start | bytes 491528 | tf_op jit(solution)/shard_map/ppermute | solution.py:427
  116.7 14.3 %collective-permute-start.18 = (bf16[128,640]{1,0:T(8,128)(2,1)S(1)}, bf16[128,640]{1,0:T(8,128)(2,1)S(1)}, u32[]{:S(2)}, u32[]{:S(2)}) collective-permute-start(bf16[128,640]{1,0:T(8,128)(2,1)S(1)} %add_convert_fusion.3), channel_id=1, source_target_pairs={{0,28},{1,29},{2,30},{3,31},{4,0},{5,1},{6,2},{7,3},{8,4},{9,5},{1... | collective-permute-start | bytes 491528 | tf_op jit(solution)/shard_map/ppermute | solution.py:427
  122.2 3.2 %collective-permute-start.34 = (bf16[64,512]{1,0:T(8,128)(2,1)S(1)}, bf16[64,512]{1,0:T(8,128)(2,1)S(1)}, u32[]{:S(2)}, u32[]{:S(2)}) collective-permute-start(bf16[64,512]{1,0:T(8,128)(2,1)S(1)} %add_convert_fusion.9), channel_id=1, source_target_pairs={{0,34},{1,35},{2,0},{3,1},{4,38},{5,39},{6,4},{7,5},{8,42},{9,43},... | collective-permute-start | bytes 196616 | tf_op jit(solution)/shard_map/ppermute | solution.py:427
  122.4 4.9 %collective-permute-start.33 = (bf16[64,512]{1,0:T(8,128)(2,1)S(1)}, bf16[64,512]{1,0:T(8,128)(2,1)S(1)}, u32[]{:S(2)}, u32[]{:S(2)}) collective-permute-start(bf16[64,512]{1,0:T(8,128)(2,1)S(1)} %add_convert_fusion.9), channel_id=1, source_target_pairs={{0,32},{1,33},{2,34},{3,35},{4,36},{5,37},{6,38},{7,39},{8,40},{9,... | collective-permute-start | bytes 196616 | tf_op jit(solution)/shard_map/ppermute | solution.py:427
  123.0 5.1 %collective-permute-start.32 = (bf16[64,512]{1,0:T(8,128)(2,1)S(1)}, bf16[64,512]{1,0:T(8,128)(2,1)S(1)}, u32[]{:S(2)}, u32[]{:S(2)}) collective-permute-start(bf16[64,512]{1,0:T(8,128)(2,1)S(1)} %add_convert_fusion.9), channel_id=1, source_target_pairs={{0,2},{1,3},{2,32},{3,33},{4,6},{5,7},{6,36},{7,37},{8,10},{9,11},... | collective-permute-start | bytes 196616 | tf_op jit(solution)/shard_map/ppermute | solution.py:427
  128.1 13.4 %collective-permute-start.37 = (bf16[256,512]{1,0:T(8,128)(2,1)S(1)}, bf16[256,512]{1,0:T(8,128)(2,1)S(1)}, u32[]{:S(2)}, u32[]{:S(2)}) collective-permute-start(bf16[256,512]{1,0:T(8,128)(2,1)S(1)} %pad_maximum_fusion.1.refs_0_), channel_id=1, source_target_pairs={{0,192},{1,193},{2,194},{3,195},{4,196},{5,197},{6,198},{7,199},{8... | collective-permute-start | bytes 786440 | tf_op jit(solution)/shard_map/ppermute | solution.py:427
  130.0 13.9 %collective-permute-start.36 = (bf16[256,512]{1,0:T(8,128)(2,1)S(1)}, bf16[256,512]{1,0:T(8,128)(2,1)S(1)}, u32[]{:S(2)}, u32[]{:S(2)}) collective-permute-start(bf16[256,512]{1,0:T(8,128)(2,1)S(1)} %pad_maximum_fusion.1.refs_0_), channel_id=1, source_target_pairs={{0,128},{1,129},{2,130},{3,131},{4,132},{5,133},{6,134},{7,135},{8... | collective-permute-start | bytes 786440 | tf_op jit(solution)/shard_map/ppermute | solution.py:427
  130.7 15.0 %collective-permute-start.35 = (bf16[256,512]{1,0:T(8,128)(2,1)S(1)}, bf16[256,512]{1,0:T(8,128)(2,1)S(1)}, u32[]{:S(2)}, u32[]{:S(2)}) collective-permute-start(bf16[256,512]{1,0:T(8,128)(2,1)S(1)} %pad_maximum_fusion.1.refs_0_), channel_id=1, source_target_pairs={{0,64},{1,65},{2,66},{3,67},{4,68},{5,69},{6,70},{7,71},{8,72},{9,... | collective-permute-start | bytes 786440 | tf_op jit(solution)/shard_map/ppermute | solution.py:427
  130.8 17.7 %collective-permute-start.20 = (bf16[128,1536]{1,0:T(8,128)(2,1)S(1)}, bf16[128,1536]{1,0:T(8,128)(2,1)S(1)}, u32[]{:S(2)}, u32[]{:S(2)}) collective-permute-start(bf16[128,1536]{1,0:T(8,128)(2,1)S(1)} %slice_bitcast_fusion), channel_id=1, source_target_pairs={{0,2},{1,3},{2,0},{3,1},{4,6},{5,7},{6,4},{7,5},{8,10},{9,11},{10,... | collective-permute-start | bytes 1179656 | tf_op jit(solution)/shard_map/ppermute | solution.py:427
  131.0 17.5 %collective-permute-start.38 = (bf16[256,512]{1,0:T(8,128)(2,1)S(1)}, bf16[256,512]{1,0:T(8,128)(2,1)S(1)}, u32[]{:S(2)}, u32[]{:S(2)}) collective-permute-start(bf16[256,512]{1,0:T(8,128)(2,1)S(1)} %pad_maximum_fusion.1.refs_0_), channel_id=1, source_target_pairs={{0,1},{1,0},{2,3},{3,2},{4,5},{5,4},{6,7},{7,6},{8,9},{9,8},{10,11... | collective-permute-start | bytes 786440 | tf_op jit(solution)/shard_map/ppermute | solution.py:427
  141.5 7.0 %collective-permute-start.41 = (bf16[256,512]{1,0:T(8,128)(2,1)S(1)}, bf16[256,512]{1,0:T(8,128)(2,1)S(1)}, u32[]{:S(2)}, u32[]{:S(2)}) collective-permute-start(bf16[256,512]{1,0:T(8,128)(2,1)S(1)} %collective-permute-done.37.refs_3_), channel_id=1, source_target_pairs={{0,1},{1,0},{2,3},{3,2},{4,5},{5,4},{6,7},{7,6},{8,9},{9,8},{10,11... | collective-permute-start | bytes 786440 | tf_op jit(solution)/shard_map/ppermute | solution.py:427
  143.9 4.6 %collective-permute-start.40 = (bf16[256,512]{1,0:T(8,128)(2,1)S(1)}, bf16[256,512]{1,0:T(8,128)(2,1)S(1)}, u32[]{:S(2)}, u32[]{:S(2)}) collective-permute-start(bf16[256,512]{1,0:T(8,128)(2,1)S(1)} %collective-permute-done.36.refs_2_), channel_id=1, source_target_pairs={{0,1},{1,0},{2,3},{3,2},{4,5},{5,4},{6,7},{7,6},{8,9},{9,8},{10,11... | collective-permute-start | bytes 786440 | tf_op jit(solution)/shard_map/ppermute | solution.py:427
  145.8 3.9 %collective-permute-start.39 = (bf16[256,512]{1,0:T(8,128)(2,1)S(1)}, bf16[256,512]{1,0:T(8,128)(2,1)S(1)}, u32[]{:S(2)}, u32[]{:S(2)}) collective-permute-start(bf16[256,512]{1,0:T(8,128)(2,1)S(1)} %collective-permute-done.35.refs_1_), channel_id=1, source_target_pairs={{0,1},{1,0},{2,3},{3,2},{4,5},{5,4},{6,7},{7,6},{8,9},{9,8},{10,11... | collective-permute-start | bytes 786440 | tf_op jit(solution)/shard_map/ppermute | solution.py:427
where the time goes:
time: 152 us
  starting transfers between devices  66.8 us (44%)
  Pallas kernels  40.8 us (27%)
  waiting for transfers between devices  40.5 us (27%)
  local copies, waits for them, and re-layouts  2.1 us (1%)
    ppermute x42, starting transfers between devices, all_perm(): return lax.ppermute(x, ('dp', 'ctx'), pairs)  66.8 us
    ppermute x42, waiting for transfers between devices, all_perm(): return lax.ppermute(x, ('dp', 'ctx'), pairs)  40.5 us
    pallas_call x1, Pallas kernels, attn_call(): pl.pallas_call(functools.partial(attn_kernel, grid, offsets, na, heads, i...  34.2 us
    pallas_call x1, Pallas kernels, own_call(): pl.pallas_call(functools.partial(own_kernel, grid), in_specs=[SMEM, SMEM]...  4.01 us
  transfers between devices with their start and end apart: 42, of which 18 were waited for; matrix products, arithmetic and copies ran while one was open for 1% of the time, Pallas kernels for 22%

commit v1 on v0

--- a/solution.py
+++ b/solution.py
@@ -47,19 +47,13 @@
     )
 
 
-def own_kernel(grid, dp_ref, ctx_ref, qn, qr, do_ref, sv_ref, lse_ref, lat, rope, wv_ref, key, pack, *dwv):
+def own_kernel(grid, dp_ref, ctx_ref, qn, qr, do_ref, sv_ref, lse_ref, wv_ref, pack, *dwv):
     ny, nxh, nz, nxl, nc = grid
     y, x, z, core = places(grid, dp_ref[0], ctx_ref[0])
     nx = nxh * nxl
     rows = do_ref.shape[0]
     heads, dc, hd = wv_ref.shape
-    dr = rope.shape[0]
     group = hd // nx
-    key[:, :dc] = lat[...]
-    key[:, dc:] = (
-        jnp.concatenate([rope[...].astype(F32), jnp.zeros((128 - dr, rows), F32)], axis=0)
-        .T.astype(BF)
-    )
     per_core = heads // nc
     per_y = per_core // ny
     lane = lax.broadcasted_iota(jnp.int32, (rows, 128), 1)
@@ -95,37 +89,57 @@
     )
 
 
-def own_call(grid, dp, ctx, qn, qr, do, sv, lse, lat, rope, wv):
+def own_call(grid, dp, ctx, qn, qr, do, sv, lse, wv):
     rows = do.shape[0]
     heads, dc, hd = wv.shape
     nc = grid[4]
     return pl.pallas_call(
         functools.partial(own_kernel, grid),
-        in_specs=[SMEM, SMEM] + [VMEM] * 8,
-        out_specs=(VMEM,) * (2 + nc),
+        in_specs=[SMEM, SMEM] + [VMEM] * 6,
+        out_specs=(VMEM,) * (1 + nc),
         out_shape=(
-            jax.ShapeDtypeStruct((rows, dc + 128), BF),
             jax.ShapeDtypeStruct((rows, qn.shape[1] + qr.shape[1] + do.shape[1] + 128), BF),
         )
         + (jax.ShapeDtypeStruct((heads // nc, hd, dc), BF),) * nc,
         compiler_params=vmem(60),
         cost_estimate=pl.CostEstimate(flops=4 * 10**9, bytes_accessed=4 * 10**6, transcendentals=0),
         name="own_rows",
-    )(dp, ctx, qn, qr, do, sv, lse, lat, rope, wv)
-
-
-def attn_kernel(grid, offsets, na, heads, spans, scaling, *refs):
+    )(dp, ctx, qn, qr, do, sv, lse, wv)
+
+
+def key_kernel(lat, rope, key):
+    dc = lat.shape[1]
+    pad = jnp.zeros((key.shape[1] - dc - rope.shape[0], rope.shape[1]), F32)
+    key[:, :dc] = lat[...]
+    key[:, dc:] = jnp.concatenate([rope[...].astype(F32), pad], axis=0).T.astype(BF)
+
+
+def key_call(lat, rope):
+    return pl.pallas_call(
+        key_kernel,
+        in_specs=[VMEM] * 2,
+        out_specs=VMEM,
+        out_shape=jax.ShapeDtypeStruct((lat.shape[0], lat.shape[1] + 128), BF),
+        compiler_params=vmem(60),
+        name="key_rows",
+    )(lat, rope)
+
+
+def attn_kernel(grid, na, heads, spans, scaling, *refs):
     ny, nxh, nz, nxl, nc = grid
     nx = nxh * nxl
-    nb = len(offsets)
+    nb = nz
     ids, dp_ref, ctx_ref = refs[:3]
     packs = refs[3 : 3 + na]
-    keys = refs[3 + na : 3 + na + nb]
-    wk, wv = refs[3 + na + nb : 5 + na + nb]
-    out = refs[5 + na + nb :]
-    far, dk, (keep, send), weights = out[:2], out[2 : nb + 1], out[nb + 1 : nb + 3], out[nb + 3 : nb + 3 + nc]
-    PK, KC, Q, G, LB, DB, K, KP, DL, DQ, DO, WA, sems = out[nb + 3 + nc :]
+    keys = refs[3 + na : 4 + na + nb]
+    wk, wv = refs[4 + na + nb : 6 + na + nb]
+    out = refs[6 + na + nb :]
+    n = 2 + nb // 2
+    dk_own, dk_far, dk, dk_send = out[0], out[1], out[2 : n - 1], out[n - 1]
+    (keep, send), weights = out[n : n + 2], out[n + 2 : n + 2 + nc]
+    PK, KC, Q, G, LB, DB, K, KP, DL, DQ, DO, WA, sems = out[n + 2 + nc :]
     y, x, z, core = places(grid, dp_ref[0], ctx_ref[0])
+    offsets = [0] + [o for s in range(1, nb // 2) for o in (-s, s)] + [nb // 2]
     xl = x % nxl
 
     hd, dc = wk.shape[1], wk.shape[2]
@@ -140,8 +154,21 @@
     per = nb // nkb
     kw = per * ch
 
-    copies = [pltpu.make_async_copy(packs[a], PK.at[a], sems.at[a]) for a in range(na)]
-    copies += [pltpu.make_async_copy(keys[b], KC.at[b], sems.at[na + b]) for b in range(nb)]
+    copies = [pltpu.make_async_copy(
+            packs[a], PK.at[pl.ds(a * tokens, tokens)], sems.at[a]
+        ) for a in range(na)]
+    copies += [
+        pltpu.make_async_copy(keys[b].at[pl.ds(0, tokens)], KC.at[b], sems.at[na + b])
+        for b in range(nb - 1)
+    ]
+    own_half = pl.ds(pl.multiple_of(core * ch, ch), ch)
+    other_half = pl.ds(pl.multiple_of((1 - core) * ch, ch), ch)
+    for b, rows_at in ((nb - 1, pl.ds(0, ch)), (nb, pl.ds(ch, ch))):
+        copies.append(
+            pltpu.make_async_copy(
+                keys[b].at[pl.ds(0, ch)], KC.at[nb - 1, rows_at], sems.at[na + b]
+            )
+        )
     for c in copies:
         c.start()
 
@@ -169,36 +196,29 @@
         return out
 
     DL[...] = jnp.zeros_like(DL)
-    WA[...] = jnp.zeros_like(WA)
 
     for c in copies[:na]:
         c.wait()
 
-    def prepare(a, _):
-        first = 2 * pick(qc, a) < spans
-        stats = PK[a, :, wn + wr + heads * hd :].astype(F32)
-        stats = stats[:, : 2 * heads] + stats[:, 2 * heads : 4 * heads] + stats[:, 4 * heads : 6 * heads]
-        flipped = jnp.concatenate([stats[ch:], stats[:ch]], axis=0)
-        stats = jnp.where(first, stats, flipped)
-        for h in range(heads):
-            ql = dot_nn(PK[a, :, h * hd : (h + 1) * hd], wk[h]).astype(BF)
-            gl = dot_nt(PK[a, :, wn + wr + h * hd : wn + wr + (h + 1) * hd], wv[h]).astype(BF)
-            qrot = PK[a, :, wn + h * dr : wn + (h + 1) * dr]
-            to = slice(h * ch, (h + 1) * ch)
-            for half in range(2):
-                mine = slice(half * ch, (half + 1) * ch)
-                other = slice((1 - half) * ch, (2 - half) * ch)
-                Q[a, half, to, :dc] = jnp.where(first, ql[mine], ql[other])
-                Q[a, half, to, dc : dc + dr] = jnp.where(first, qrot[mine], qrot[other])
-                Q[a, half, to, dc + dr :] = jnp.zeros((ch, width - dc - dr), BF)
-                G[a, half, to, :] = jnp.where(first, gl[mine], gl[other])
-                LB[a, half, to, :] = jnp.broadcast_to(stats[mine, h : h + 1], (ch, 128))
-                DB[a, half, to, :] = jnp.broadcast_to(
-                    stats[mine, heads + h : heads + h + 1], (ch, 128)
-                )
-        return 0
-
-    lax.fori_loop(0, na, prepare, 0)
+    lows = [jnp.where(2 * c < spans, 0, 1) for c in qc]
+    stats = PK[:, wn + wr + wn :].astype(F32)
+    stats = stats[:, : 2 * heads] + stats[:, 2 * heads : 4 * heads] + stats[:, 4 * heads : 6 * heads]
+    for h in range(heads):
+        ql = dot_nn(PK[:, h * hd : (h + 1) * hd], wk[h]).astype(BF)
+        gl = dot_nt(PK[:, wn + wr + h * hd : wn + wr + (h + 1) * hd], wv[h]).astype(BF)
+        qrot = PK[:, wn + h * dr : wn + (h + 1) * dr]
+        to = slice(h * ch, (h + 1) * ch)
+        for a, slot in itertools.product(range(na), range(2)):
+            mine = slice((2 * a + slot) * ch, (2 * a + slot + 1) * ch)
+            half = lows[a] if slot == 0 else 1 - lows[a]
+            Q[a, half, to, :dc] = ql[mine]
+            Q[a, half, to, dc : dc + dr] = qrot[mine]
+            Q[a, half, to, dc + dr :] = jnp.zeros((ch, width - dc - dr), BF)
+            G[a, half, to, :] = gl[mine]
+            LB[a, half, to, :] = jnp.broadcast_to(stats[mine, h : h + 1], (ch, 128))
+            DB[a, half, to, :] = jnp.broadcast_to(
+                stats[mine, heads + h : heads + h + 1], (ch, 128)
+            )
 
     for c in copies[na:]:
         c.wait()
@@ -222,27 +242,33 @@
     for i in range(2 * nkb):
         KP[i] = kps[i]
 
-    sub = min(rows, 512)
+    sub = min(rows, 256)
     wide = kw // 128
     qtok = lax.broadcasted_iota(jnp.int32, (sub, kw), 0) % ch
 
     def unit(a, half, kb, span, fresh):
         kpos = KP[kb][0:1, :]
+
+        def scores(r):
+            rr = slice(r * sub, (r + 1) * sub)
+            return dot_nt(Q[a, half, rr, :], K[kb]), dot_nt(G[a, half, rr, :], K[kb, :, :dc])
+
         dss, pbs = [], []
+        ready = scores(0)
         for r in range(rows // sub):
             rr = slice(r * sub, (r + 1) * sub)
-            s = dot_nt(Q[a, half, rr, :], K[kb])
-            dp = dot_nt(G[a, half, rr, :], K[kb, :, :dc])
+            s, dp = ready
+            if r + 1 < rows // sub:
+                ready = scores(r + 1)
             lb = jnp.concatenate([LB[a, half, rr, :]] * wide, axis=1)
             db = jnp.concatenate([DB[a, half, rr, :]] * wide, axis=1)
             p = jnp.exp2(s * (scaling * LOG2E) - lb)
             p = jnp.where(kpos <= span * ch + qtok, p, 0.0)
-            ds = (p * ((dp - db) * scaling)).astype(BF)
-            DQ[half, rr, :] = jnp.where(fresh, 0.0, DQ[half, rr, :]) + dot_nn(ds, K[kb])
-            dss.append(ds)
+            dss.append((p * ((dp - db) * scaling)).astype(BF))
             pbs.append(p.astype(BF))
         ds = jnp.concatenate(dss, axis=0)
         pb = jnp.concatenate(pbs, axis=0)
+        DQ[half] = jnp.where(fresh, 0.0, DQ[half]) + dot_nn(ds, K[kb])
         DL[kb, :, :dc] += dot_tn(pb, G[a, half]) + dot_tn(ds, Q[a, half, :, :dc])
         DL[kb, :, dc:] += dot_tn(ds, Q[a, half, :, dc:])
 
@@ -275,48 +301,51 @@
 
         lax.fori_loop(0, 3 * nkb, step, 0)
 
-        first = 2 * c < spans
+        low = jnp.where(2 * c < spans, 0, 1)
         for h in range(heads):
             to = slice(h * ch, (h + 1) * ch)
-            d0 = DQ[0, to, dc : dc + dr]
-            d1 = DQ[1, to, dc : dc + dr]
-            d = jnp.concatenate([jnp.where(first, d0, d1), jnp.where(first, d1, d0)], axis=0)
-            DO[a, :, wn + h * dr : wn + (h + 1) * dr] = d.astype(BF)
-            d0 = DQ[0, to, :dc]
-            d1 = DQ[1, to, :dc]
-            d = jnp.concatenate([jnp.where(first, d0, d1), jnp.where(first, d1, d0)], axis=0)
-            d = d.astype(BF)
-            DO[a, :, h * hd : (h + 1) * hd] = dot_nt(d, wk[h]).astype(BF)
-            WA[h] += dot_tn(PK[a, :, h * hd : (h + 1) * hd], d)
+            d = jnp.concatenate([DQ[low, to, :], DQ[1 - low, to, :]], axis=0).astype(BF)
+            DO[a, :, wn + h * dr : wn + (h + 1) * dr] = d[:, dc : dc + dr]
+            WA[h, pl.ds(pl.multiple_of(a * tokens, tokens), tokens), :] = d[:, :dc]
         return 0
 
     lax.fori_loop(0, na, query_set, 0)
 
+    for h in range(heads):
+        d = dot_nt(WA[h], wk[h]).astype(BF)
+        for a in range(na):
+            DO[a, :, h * hd : (h + 1) * hd] = d[a * tokens : (a + 1) * tokens]
     keep[...] = DO[: na // 2]
     send[...] = DO[na // 2 :]
     for b in range(nb):
         blk, pos, low_at, high_at = key_at[b]
         KC[b, pl.ds(low_at, ch), :] = DL[blk, pl.ds(pos, ch), :].astype(BF)
         KC[b, pl.ds(high_at, ch), :] = DL[nkb + blk, pl.ds(pos, ch), :].astype(BF)
-        if b < nb - 1:
-            dk[b][...] = KC[b]
-        else:
-            far[0][...] = KC[b, :ch]
-            far[1][...] = KC[b, ch:]
+    dk_own[...] = KC[0]
+    dk_far[...] = KC[nb - 1, own_half, :]
+    dk_send[:ch] = KC[nb - 1, other_half, :]
+    at = ch
+    for i, o in enumerate(range(nb // 2 - 1, 0, -1)):
+        mine, other = 2 * o - core, 2 * o - 1 + core
+        dk[i][:ch] = KC[mine, own_half, :]
+        dk[i][ch:] = KC[mine, other_half, :]
+        dk_send[at : at + ch] = KC[other, other_half, :]
+        dk_send[at + ch : at + tokens] = KC[other, own_half, :]
+        at += tokens
     group = hd // nx
     per_core = heads // nc
     per_y = per_core // ny
     for i, j, k in itertools.product(range(nc), range(ny), range(per_y)):
         h = (core + i) % nc * per_core + (y + j) % ny * per_y + k
+        cols = pl.ds(pl.multiple_of(h * hd, hd), hd)
+        w = dot_tn(PK[:, cols], WA[h]).astype(BF)
         for n in range(nx):
             at = pl.multiple_of((n - x + nx) % nx * group, group)
-            weights[i][j * per_y + k, pl.ds(at, group), :] = WA[
-                h, n * group : (n + 1) * group, :
-            ].astype(BF)
-
-
-def attn_call(grid, offsets, ids, dp, ctx, packs, keys, wk, wv, wr, scaling):
-    na, nb = len(packs), len(keys)
+            weights[i][j * per_y + k, pl.ds(at, group), :] = w[n * group : (n + 1) * group]
+
+
+def attn_call(grid, ids, dp, ctx, packs, keys, wk, wv, wr, scaling):
+    na, nb = len(packs), grid[2]
     heads, hd, dc = wk.shape
     tokens, width = keys[0].shape
     ch = tokens // 2
@@ -326,17 +355,21 @@
     nc = grid[4]
     out = heads * hd + wr
     return pl.pallas_call(
-        functools.partial(attn_kernel, grid, offsets, na, heads, ids.shape[1], scaling),
-        in_specs=[SMEM] * 3 + [ANY] * (na + nb) + [VMEM] * 2,
+        functools.partial(attn_kernel, grid, na, heads, ids.shape[1], scaling),
+        in_specs=[SMEM] * 3 + [ANY] * (na + nb + 1) + [VMEM] * 2,
         out_shape=(
-            (jax.ShapeDtypeStruct((ch, width), BF),) * 2
-            + (jax.ShapeDtypeStruct((tokens, width), BF),) * (nb - 1)
+            (
+                jax.ShapeDtypeStruct((tokens, width), BF),
+                jax.ShapeDtypeStruct((ch, width), BF),
+            )
+            + (jax.ShapeDtypeStruct((tokens, width), BF),) * (nb // 2 - 1)
+            + (jax.ShapeDtypeStruct((ch + (nb // 2 - 1) * tokens, width), BF),)
             + (jax.ShapeDtypeStruct((na // 2, tokens, out), BF),) * 2
             + (jax.ShapeDtypeStruct((heads // nc, hd, dc), BF),) * nc
         ),
-        out_specs=(VMEM,) * (nb + 3 + nc),
+        out_specs=(VMEM,) * (nb // 2 + 4 + nc),
         scratch_shapes=[
-            pltpu.VMEM((na,) + packs[0].shape, BF),
+            pltpu.VMEM((na * tokens, packs[0].shape[1]), BF),
             pltpu.VMEM((nb, tokens, width), BF),
             pltpu.VMEM((na, 2, rows, width), BF),
             pltpu.VMEM((na, 2, rows, dc), BF),
@@ -347,8 +380,8 @@
             pltpu.VMEM((2 * nkb, per * ch, width), F32),
             pltpu.VMEM((2, rows, width), F32),
             pltpu.VMEM((na, tokens, out), BF),
-            pltpu.VMEM((heads, hd, dc), F32),
-            pltpu.SemaphoreType.DMA((na + nb,)),
+            pltpu.VMEM((heads, na * tokens, dc), BF),
+            pltpu.SemaphoreType.DMA((na + nb + 1,)),
         ],
         compiler_params=vmem(44),
         cost_estimate=pl.CostEstimate(
@@ -358,17 +391,23 @@
     )(ids, dp, ctx, *packs, *keys, wk, wv)
 
 
-def final_kernel(grid, heads, scale, dp_ref, ctx_ref, key_ref, plus, minus, q_ref, back_ref, *refs):
+def final_kernel(grid, heads, scale, dp_ref, ctx_ref, key_ref, mine, other, q_ref, back_ref, *refs):
     ny, nxh, nz, nxl, nc = grid
     nx = nxh * nxl
-    pieces, (dqn, dqr, dlat, drope, dwk, dwv) = refs[:-6], refs[-6:]
+    pieces, (dqn, dqr, dlat, drope, dwk, dwv, total) = refs[:-7], refs[-7:]
+    y, x, z, core = places(grid, dp_ref[0], ctx_ref[0])
     dr = drope.shape[0]
     lat = dlat.shape[1]
-    if plus.shape[0] == key_ref.shape[0]:
-        got = plus[...].astype(F32) + minus[...].astype(F32)
-    else:
-        got = jnp.concatenate([plus[...].astype(F32), minus[...].astype(F32)], axis=0)
-    key = key_ref[...].astype(F32) + got
+    ch = key_ref.shape[0] // 2
+    own_half = pl.ds(pl.multiple_of(core * ch, ch), ch)
+    other_half = pl.ds(pl.multiple_of((1 - core) * ch, ch), ch)
+    total[...] = key_ref[...].astype(F32)
+    total[own_half, :] += mine[:ch].astype(F32)
+    total[other_half, :] += other[:ch].astype(F32)
+    if other.shape[0] > ch:
+        total[other_half, :] += mine[ch : 2 * ch].astype(F32)
+        total[own_half, :] += other[ch:].astype(F32)
+    key = total[...]
     dlat[...] = key[:, :lat].astype(BF)
     drope[...] = key[:, lat:].T[:dr].astype(BF)
     q = add(q_ref[0], back_ref[...])
@@ -393,7 +432,7 @@
             )
 
 
-def final_call(grid, heads, hd, dr, scale, dp, ctx, key, plus, minus, q, back, pieces):
+def final_call(grid, heads, hd, dr, scale, dp, ctx, key, mine, other, q, back, pieces):
     tokens = key.shape[0]
     dc = pieces[0].shape[1]
     return pl.pallas_call(
@@ -408,9 +447,10 @@
             jax.ShapeDtypeStruct((heads, hd, dc), F32),
             jax.ShapeDtypeStruct((heads, dc, hd), F32),
         ),
+        scratch_shapes=[pltpu.VMEM(key.shape, F32)],
         compiler_params=vmem(16),
         name="outputs",
-    )(dp, ctx, key, plus, minus, q, back, *pieces)
+    )(dp, ctx, key, mine, other, q, back, *pieces)
 
 
 def make_local(grid):
@@ -428,6 +468,9 @@
 
     def z_send(x, s):
         return all_perm(x, lambda y, xh, z, xl, c: (y, xh, (z + s) % nz, xl, c))
+
+    def z_relay(x):
+        return all_perm(x, lambda y, xh, z, xl, c: (y, xh, (z + 1 - 2 * c) % nz, xl, c))
 
     def z_flip(x, bit):
         return all_perm(x, lambda y, xh, z, xl, c: (y, xh, z ^ bit, xl, c))
@@ -463,51 +506,33 @@
         scaling = (hd + dr) ** (-0.5)
         grad_scale = (ny * nxh * seq_rows) ** (-0.5)
 
-        key, pack, *dwv = own_call(
-            grid,
-            dp,
-            ctx,
-            q_nope[0],
-            q_rope[0],
-            d_out[0],
-            saved_out[0],
-            lse[0].T,
-            latent[0],
-            rope_key[0].T,
-            w_uv,
+        key = key_call(latent[0], rope_key[0].T)
+        pack, *dwv = own_call(
+            grid, dp, ctx, q_nope[0], q_rope[0], d_out[0], saved_out[0], lse[0].T, w_uv
         )
 
         half = nz // 2
-        back, ahead = {0: key}, {0: key}
-        for s in range(1, half):
-            back[s] = z_send(back[s - 1], 1)
-            ahead[s] = z_send(ahead[s - 1], -1)
-            back[s], ahead[s] = lax.optimization_barrier((back[s], ahead[s]))
-        far = jnp.concatenate(
-            [z_send(back[half - 1][:ch], 1), z_send(ahead[half - 1][ch:], -1)], axis=0
-        )
-        offsets = [0]
+        back, ahead = key, key
         keys = [key]
         for s in range(1, half):
-            offsets += [s, -s]
-            keys += [ahead[s], back[s]]
-        offsets.append(half)
-        keys.append(far)
+            back, ahead = z_send(back, 1), z_send(ahead, -1)
+            if s == 1:
+                back, ahead, pack = lax.optimization_barrier((back, ahead, pack))
+            else:
+                back, ahead = lax.optimization_barrier((back, ahead))
+            keys += [back, ahead]
+        middle = back
+        keys += [z_send(back[:ch], 1), z_send(ahead[ch:], -1)]
 
         pack_x = xl_swap(pack)
         pack_c = c_swap(pack)
-        pack_x, _ = lax.optimization_barrier((pack_x, back[half - 1]))
+        pack_x, _ = lax.optimization_barrier((pack_x, middle))
         packs = [pack, pack_x, pack_c, c_swap(pack_x)]
 
         dwv, dwv_send = dwv
         dwv_got = c_swap(dwv_send)
-        res = attn_call(
-            grid, offsets, span_ids, dp, ctx, packs, keys, w_uk, w_uv, heads * dr, scaling
-        )
-        nb = len(offsets)
-        far_up, far_down = res[:2]
-        parts = dict(zip(offsets[:-1], res[2 : nb + 1]))
-        dq, dq_send, dwk, dwk_send = res[nb + 1 :]
+        res = attn_call(grid, span_ids, dp, ctx, packs, keys, w_uk, w_uv, heads * dr, scaling)
+        dk_own, dk_far, *dk, dk_send, dq, dq_send, dwk, dwk_send = res
 
         t = jnp.concatenate(
             [by_x(add(dwk, c_swap(dwk_send)), hd), by_x(add(dwv, dwv_got), hd)], axis=2
@@ -522,21 +547,24 @@
         pieces = [t] + [y_send(t, s) for s in range(1, ny)]
         pieces += [c_swap(p) for p in pieces]
 
-        plus, minus = z_send(far_up, 1), z_send(far_down, -1)
-        for o in range(half - 1, 0, -1):
-            if o == half - 1:
-                up = jnp.concatenate([add(parts[o][:ch], plus), parts[o][ch:]], axis=0)
-                down = jnp.concatenate([parts[-o][:ch], add(parts[-o][ch:], minus)], axis=0)
+        dk_got = c_swap(dk_send)
+        relay = z_relay(jnp.concatenate([dk_far, dk_got[:ch]], axis=0))
+        at = ch
+        for i, mine in enumerate(dk):
+            other = dk_got[at : at + tokens]
+            if i == 0:
+                parts = [add(mine[:ch], relay[:ch]), mine[ch:], add(other[:ch], relay[ch:]), other[ch:]]
             else:
-                up, down = add(parts[o], plus), add(parts[-o], minus)
-            up, down = lax.optimization_barrier((up, down))
-            plus, minus = z_send(up, 1), z_send(down, -1)
+                parts = [add(mine, relay[:tokens]), add(other, relay[tokens:])]
+            relay = z_relay(jnp.concatenate(parts, axis=0))
+            at += tokens
+        dk_other = c_swap(relay[relay.shape[0] // 2 :])
 
         q = add(dq, c_swap(dq_send))
         back = xl_swap(q[1])
 
         d_q_nope, d_q_rope, d_latent, d_rope_key, d_w_uk, d_w_uv = final_call(
-            grid, heads, hd, dr, grad_scale, dp, ctx, parts[0], plus, minus, q, back, pieces
+            grid, heads, hd, dr, grad_scale, dp, ctx, dk_own, relay, dk_other, q, back, pieces
         )
         return (d_q_nope[None], d_q_rope[None], d_latent[None], d_rope_key.T[None], d_w_uk, d_w_uv)
 

time: 152 us -> 145 us (0.954)
  starting transfers between devices: 66.8 us -> 60.4 us
    ppermute x42 -> x40, starting transfers between devices: 66.8 us -> 60.4 us  [all_perm(): return lax.ppermute(x, ('dp', 'ctx'), pairs)]
    pallas_call x1 -> x2, Pallas kernels: 34.2 us -> 34.1 us  [the longest x1 32.4 us: attn_call(): pl.pallas_call(functools.partial(attn_kernel, grid, na, heads, ids.shape[...]
    ppermute x42 -> x40, waiting for transfers between devices: 40.5 us -> 40.6 us  [all_perm(): return lax.ppermute(x, ('dp', 'ctx'), pairs)]
  transfers between devices with their start and end apart: 42 -> 40, of which waited for: 18 -> 19; matrix products, arithmetic and copies ran while one was open for 1% -> 1% of each run, Pallas kernels for 22% -> 25%
where the time goes in v1:
time: 145 us
  starting transfers between devices  60.4 us (42%)
  waiting for transfers between devices  40.6 us (28%)
  Pallas kernels  40.5 us (28%)
    ppermute x40, starting transfers between devices, all_perm(): return lax.ppermute(x, ('dp', 'ctx'), pairs)  60.4 us
    ppermute x40, waiting for transfers between devices, all_perm(): return lax.ppermute(x, ('dp', 'ctx'), pairs)  40.6 us
    pallas_call x1, Pallas kernels, attn_call(): pl.pallas_call(functools.partial(attn_kernel, grid, na, heads, ids.shape[...  32.4 us
    pallas_call x1, Pallas kernels, own_call(): pl.pallas_call(functools.partial(own_kernel, grid), in_specs=[SMEM, SMEM]...  3.8 us
  transfers between devices with their start and end apart: 40, of which 19 were waited for; matrix products, arithmetic and copies ran while one was open for 1% of the time, Pallas kernels for 25%

profile of v1, /device:TPU:1, one launch (start us, length us, event | category | flops | bytes accessed | tf_op | source)
XLA Modules:
  0.0 144.7 jit_solution(9559621183195277178)
XLA Ops:
  0.6 1.7 %key_rows.1.refs_7_ = bf16[128,640]{1,0:T(8,128)(2,1)} custom-call(bf16[128,512]{1,0:T(8,128)(2,1)} %bitcast.49, bf16[64,128]{1,0:T(8,128)(2,1)} %bitcast.50), custom_call_target="tpu_custom_call" | custom-call | tf_op jit(solution)/shard_map/key_rows/pallas_call | solution.py:118
  2.3 6.4 %collective-permute-start.1 = (bf16[128,640]{1,0:T(8,128)(2,1)}, bf16[128,640]{1,0:T(8,128)(2,1)S(1)}, u32[]{:S(2)}, u32[]{:S(2)}) collective-permute-start(bf16[128,640]{1,0:T(8,128)(2,1)} %key_rows.1.refs_7_), channel_id=1, source_target_pairs={{0,28},{1,29},{2,30},{3,31},{4,0},{5,1},{6,2},{7,3},{8,4},{9,5},{1... | collective-permute-start | bytes 491528 | tf_op jit(solution)/shard_map/ppermute | solution.py:467
  8.7 3.8 %own_rows.1 = (bf16[128,2688]{1,0:T(8,128)(2,1)}, bf16[4,128,512]{2,1,0:T(8,128)(2,1)}, bf16[4,128,512]{2,1,0:T(8,128)(2,1)}) custom-call(s32[1]{0:T(128)} %bitcast.dp_ref.refs_1_, s32[1]{0:T(128)} %bitcast.1.ctx_ref.refs_2_, bf16[128,1024]{1,0:T(8,128)(2,1)} %bitcast.52, bf16[128,512]{1,0:T(8,128)(2,1)} %bitcast.55, bf16[128,1024]{1,0:T(8,128)(2,1)} %bitcast.53, ...), custom_call_target="tpu_custom_call" | custom-call | flops 4000000000 | bytes 4000000 | tf_op jit(solution)/shard_map/own_rows/pallas_call | solution.py:96
  12.5 2.3 %collective-permute-done.refs_8_ = bf16[128,640]{1,0:T(8,128)(2,1)S(1)} collective-permute-done((bf16[128,640]{1,0:T(8,128)(2,1)}, bf16[128,640]{1,0:T(8,128)(2,1)S(1)}, u32[]{:S(2)}, u32[]{:S(2)}) %collective-permute-start) | collective-permute-done | bytes 163872 | tf_op jit(solution)/shard_map/ppermute | solution.py:467
  14.9 1.2 collective-permute-start.2
  16.1 2.7 %collective-permute-start.4 = (bf16[128,640]{1,0:T(8,128)(2,1)S(1)}, bf16[128,640]{1,0:T(8,128)(2,1)S(1)}, u32[]{:S(2)}, u32[]{:S(2)}) collective-permute-start(bf16[128,640]{1,0:T(8,128)(2,1)S(1)} %collective-permute-done.1.refs_9_), channel_id=1, source_target_pairs={{0,28},{1,29},{2,30},{3,31},{4,0},{5,1},{6,2},{7,3},{8,4},{9,5},{1... | collective-permute-start | bytes 491528 | tf_op jit(solution)/shard_map/ppermute | solution.py:467
  18.8 2.7 %collective-permute-done.3.refs_10_ = bf16[128,640]{1,0:T(8,128)(2,1)S(1)} collective-permute-done((bf16[128,640]{1,0:T(8,128)(2,1)S(1)}, bf16[128,640]{1,0:T(8,128)(2,1)S(1)}, u32[]{:S(2)}, u32[]{:S(2)}) %collective-permute-start.3) | collective-permute-done | bytes 163872 | tf_op jit(solution)/shard_map/ppermute | solution.py:467
  21.5 2.7 %collective-permute-start.6 = (bf16[128,640]{1,0:T(8,128)(2,1)S(1)}, bf16[128,640]{1,0:T(8,128)(2,1)S(1)}, u32[]{:S(2)}, u32[]{:S(2)}) collective-permute-start(bf16[128,640]{1,0:T(8,128)(2,1)S(1)} %collective-permute-done.4.refs_11_), channel_id=1, source_target_pairs={{0,28},{1,29},{2,30},{3,31},{4,0},{5,1},{6,2},{7,3},{8,4},{9,5},{1... | collective-permute-start | bytes 491528 | tf_op jit(solution)/shard_map/ppermute | solution.py:467
  24.2 3.9 %collective-permute-start.7 = (bf16[128,2688]{1,0:T(8,128)(2,1)}, bf16[128,2688]{1,0:T(8,128)(2,1)S(1)}, u32[]{:S(2)}, u32[]{:S(2)}) collective-permute-start(bf16[128,2688]{1,0:T(8,128)(2,1)} %get-tuple-element.34.refs_3_), channel_id=1, source_target_pairs={{0,1},{1,0},{2,3},{3,2},{4,5},{5,4},{6,7},{7,6},{8,9},{9,8},{10,11... | collective-permute-start | bytes 2064392 | tf_op jit(solution)/shard_map/ppermute | solution.py:467
  28.0 2.1 %collective-permute-done.2.refs_4_ = bf16[128,2688]{1,0:T(8,128)(2,1)S(1)} collective-permute-done((bf16[128,2688]{1,0:T(8,128)(2,1)}, bf16[128,2688]{1,0:T(8,128)(2,1)S(1)}, u32[]{:S(2)}, u32[]{:S(2)}) %collective-permute-start.2) | collective-permute-done | bytes 688160 | tf_op jit(solution)/shard_map/ppermute | solution.py:467
  30.2 2.8 %collective-permute-start.8 = (bf16[128,2688]{1,0:T(8,128)(2,1)S(1)}, bf16[128,2688]{1,0:T(8,128)(2,1)S(1)}, u32[]{:S(2)}, u32[]{:S(2)}) collective-permute-start(bf16[128,2688]{1,0:T(8,128)(2,1)S(1)} %collective-permute-done.2.refs_4_), channel_id=1, source_target_pairs={{0,1},{1,0},{2,3},{3,2},{4,5},{5,4},{6,7},{7,6},{8,9},{9,8},{10,11... | collective-permute-start | bytes 2064392 | tf_op jit(solution)/shard_map/ppermute | solution.py:467
  33.1 2.7 %collective-permute-start.10 = (bf16[64,640]{1,0:T(8,128)(2,1)S(1)}, bf16[64,640]{1,0:T(8,128)(2,1)S(1)}, u32[]{:S(2)}, u32[]{:S(2)}) collective-permute-start(bf16[64,640]{1,0:T(8,128)(2,1)S(1)} %slice.79), channel_id=1, source_target_pairs={{0,28},{1,29},{2,30},{3,31},{4,0},{5,1},{6,2},{7,3},{8,4},{9,5},{1... | collective-permute-start | bytes 245768 | tf_op jit(solution)/shard_map/ppermute | solution.py:467
  35.7 0.6 collective-permute-start.20
  36.3 2.0 %collective-permute-done.9.refs_14_ = bf16[64,640]{1,0:T(8,128)(2,1)S(1)} collective-permute-done((bf16[64,640]{1,0:T(8,128)(2,1)S(1)}, bf16[64,640]{1,0:T(8,128)(2,1)S(1)}, u32[]{:S(2)}, u32[]{:S(2)}) %collective-permute-start.9) | collective-permute-done | bytes 81952 | tf_op jit(solution)/shard_map/ppermute | solution.py:467
  38.4 1.1 copy-done.3
  39.5 32.4 %attn_grads.1 = (bf16[128,640]{1,0:T(8,128)(2,1)S(1)}, bf16[64,640]{1,0:T(8,128)(2,1)S(1)}, bf16[128,640]{1,0:T(8,128)(2,1)S(1)}, bf16[128,640]{1,0:T(8,128)(2,1...) custom-call(s32[1,64]{1,0:T(1,128)S(1)} %copy-done.4, ...), custom_call_target="tpu_custom_call" | custom-call | flops 30000001024 | bytes 10000000 | tf_op jit(solution)/shard_map/attn_grads/pallas_call | solution.py:357
  72.0 0.5 collective-permute-start.11
  72.8 1.0 collective-permute-done.19
  74.1 1.8 %collective-permute-start.21 = (bf16[4,64,512]{2,1,0:T(8,128)(2,1)S(1)}, bf16[4,64,512]{2,1,0:T(8,128)(2,1)S(1)}, u32[]{:S(2)}, u32[]{:S(2)}) collective-permute-start(bf16[4,64,512]{2,1,0:T(8,128)(2,1)S(1)} %get-tuple-element.60), channel_id=1, source_target_pairs={{0,64},{1,65},{2,66},{3,67},{4,68},{5,69},{6,70},{7,71},{8,72},{9,... | collective-permute-start | bytes 786440 | tf_op jit(solution)/shard_map/ppermute | solution.py:467
  75.9 1.5 %collective-permute-start.23 = (bf16[4,64,512]{2,1,0:T(8,128)(2,1)S(1)}, bf16[4,64,512]{2,1,0:T(8,128)(2,1)S(1)}, u32[]{:S(2)}, u32[]{:S(2)}) collective-permute-start(bf16[4,64,512]{2,1,0:T(8,128)(2,1)S(1)} %get-tuple-element.61), channel_id=1, source_target_pairs={{0,192},{1,193},{2,194},{3,195},{4,196},{5,197},{6,198},{7,199},{8... | collective-permute-start | bytes 786440 | tf_op jit(solution)/shard_map/ppermute | solution.py:467
  77.4 1.1 collective-permute-start.22
  78.6 2.8 %collective-permute-start.12 = (bf16[128,640]{1,0:T(8,128)(2,1)S(1)}, bf16[128,640]{1,0:T(8,128)(2,1)S(1)}, u32[]{:S(2)}, u32[]{:S(2)}) collective-permute-start(bf16[128,640]{1,0:T(8,128)(2,1)S(1)} %pad_maximum_fusion.5), channel_id=1, source_target_pairs={{0,4},{1,29},{2,6},{3,31},{4,8},{5,1},{6,10},{7,3},{8,12},{9,5},{1... | collective-permute-start | bytes 491528 | tf_op jit(solution)/shard_map/ppermute | solution.py:467
  81.3 2.4 %collective-permute-done.21 = bf16[4,64,512]{2,1,0:T(8,128)(2,1)S(1)} collective-permute-done((bf16[4,64,512]{2,1,0:T(8,128)(2,1)S(1)}, bf16[4,64,512]{2,1,0:T(8,128)(2,1)S(1)}, u32[]{:S(2)}, u32[]{:S(2)}) %collective-permute-start.21) | collective-permute-done | bytes 262176 | tf_op jit(solution)/shard_map/ppermute | solution.py:467
  83.7 6.5 %collective-permute-done.22 = bf16[4,64,512]{2,1,0:T(8,128)(2,1)S(1)} collective-permute-done((bf16[4,64,512]{2,1,0:T(8,128)(2,1)S(1)}, bf16[4,64,512]{2,1,0:T(8,128)(2,1)S(1)}, u32[]{:S(2)}, u32[]{:S(2)}) %collective-permute-start.22) | collective-permute-done | bytes 262176 | tf_op jit(solution)/shard_map/ppermute | solution.py:467
  90.5 2.8 %collective-permute-start.26 = (bf16[64,512]{1,0:T(8,128)(2,1)S(1)}, bf16[64,512]{1,0:T(8,128)(2,1)S(1)}, u32[]{:S(2)}, u32[]{:S(2)}) collective-permute-start(bf16[64,512]{1,0:T(8,128)(2,1)S(1)} %get-tuple-element.70), channel_id=1, source_target_pairs={{0,34},{1,35},{2,0},{3,1},{4,38},{5,39},{6,4},{7,5},{8,42},{9,43},... | collective-permute-start | bytes 196616 | tf_op jit(solution)/shard_map/ppermute | solution.py:467
  93.2 0.9 collective-permute-start.25
  94.1 0.6 collective-permute-done.24
  94.8 3.3 %collective-permute-done.25 = bf16[64,512]{1,0:T(8,128)(2,1)S(1)} collective-permute-done((bf16[64,512]{1,0:T(8,128)(2,1)S(1)}, bf16[64,512]{1,0:T(8,128)(2,1)S(1)}, u32[]{:S(2)}, u32[]{:S(2)}) %collective-permute-start.25) | collective-permute-done | bytes 65568 | tf_op jit(solution)/shard_map/ppermute | solution.py:467
  98.3 2.4 %collective-permute-start.13 = (bf16[256,640]{1,0:T(8,128)(2,1)S(1)}, bf16[256,640]{1,0:T(8,128)(2,1)S(1)}, u32[]{:S(2)}, u32[]{:S(2)}) collective-permute-start(bf16[256,640]{1,0:T(8,128)(2,1)S(1)} %pad_maximum_fusion), channel_id=1, source_target_pairs={{0,4},{1,29},{2,6},{3,31},{4,8},{5,1},{6,10},{7,3},{8,12},{9,5},{1... | collective-permute-start | bytes 983048 | tf_op jit(solution)/shard_map/ppermute | solution.py:467
  100.7 0.7 collective-permute-done.27
  101.7 5.5 %collective-permute-done.28 = bf16[64,512]{1,0:T(8,128)(2,1)S(1)} collective-permute-done((bf16[64,512]{1,0:T(8,128)(2,1)S(1)}, bf16[64,512]{1,0:T(8,128)(2,1)S(1)}, u32[]{:S(2)}, u32[]{:S(2)}) %collective-permute-start.28) | collective-permute-done | bytes 65568 | tf_op jit(solution)/shard_map/ppermute | solution.py:467
  107.2 2.3 %collective-permute-start.29 = (bf16[64,512]{1,0:T(8,128)(2,1)S(1)}, bf16[64,512]{1,0:T(8,128)(2,1)S(1)}, u32[]{:S(2)}, u32[]{:S(2)}) collective-permute-start(bf16[64,512]{1,0:T(8,128)(2,1)S(1)} %add_convert_fusion.10), channel_id=1, source_target_pairs={{0,16},{1,17},{2,18},{3,19},{4,20},{5,21},{6,22},{7,23},{8,24},{9,... | collective-permute-start | bytes 196616 | tf_op jit(solution)/shard_map/ppermute | solution.py:467
  110.2 4.1 %collective-permute-done.29 = bf16[64,512]{1,0:T(8,128)(2,1)S(1)} collective-permute-done((bf16[64,512]{1,0:T(8,128)(2,1)S(1)}, bf16[64,512]{1,0:T(8,128)(2,1)S(1)}, u32[]{:S(2)}, u32[]{:S(2)}) %collective-permute-start.29) | collective-permute-done | bytes 65568 | tf_op jit(solution)/shard_map/ppermute | solution.py:467
  114.6 1.0 collective-permute-start.31
  115.9 2.4 %collective-permute-done.14 = bf16[256,640]{1,0:T(8,128)(2,1)S(1)} collective-permute-done((bf16[256,640]{1,0:T(8,128)(2,1)S(1)}, bf16[256,640]{1,0:T(8,128)(2,1)S(1)}, u32[]{:S(2)}, u32[]{:S(2)}) %collective-permute-start.14) | collective-permute-done | bytes 327712 | tf_op jit(solution)/shard_map/ppermute | solution.py:467
  118.4 0.7 collective-permute-start.15
  119.1 0.9 collective-permute-done.31
  119.9 0.6 collective-permute-done.30
  120.6 1.5 %collective-permute-start.35 = (bf16[256,512]{1,0:T(8,128)(2,1)S(1)}, bf16[256,512]{1,0:T(8,128)(2,1)S(1)}, u32[]{:S(2)}, u32[]{:S(2)}) collective-permute-start(bf16[256,512]{1,0:T(8,128)(2,1)S(1)} %pad_maximum_fusion.4.refs_0_), channel_id=1, source_target_pairs={{0,192},{1,193},{2,194},{3,195},{4,196},{5,197},{6,198},{7,199},{8... | collective-permute-start | bytes 786440 | tf_op jit(solution)/shard_map/ppermute | solution.py:467
  122.1 1.9 %collective-permute-start.34 = (bf16[256,512]{1,0:T(8,128)(2,1)S(1)}, bf16[256,512]{1,0:T(8,128)(2,1)S(1)}, u32[]{:S(2)}, u32[]{:S(2)}) collective-permute-start(bf16[256,512]{1,0:T(8,128)(2,1)S(1)} %pad_maximum_fusion.4.refs_0_), channel_id=1, source_target_pairs={{0,128},{1,129},{2,130},{3,131},{4,132},{5,133},{6,134},{7,135},{8... | collective-permute-start | bytes 786440 | tf_op jit(solution)/shard_map/ppermute | solution.py:467
  124.0 2.3 %collective-permute-done.35.refs_3_ = bf16[256,512]{1,0:T(8,128)(2,1)S(1)} collective-permute-done((bf16[256,512]{1,0:T(8,128)(2,1)S(1)}, bf16[256,512]{1,0:T(8,128)(2,1)S(1)}, u32[]{:S(2)}, u32[]{:S(2)}) %collective-permute-start.35) | collective-permute-done | bytes 262176 | tf_op jit(solution)/shard_map/ppermute | solution.py:467
  126.2 10.1 %collective-permute-start.36 = (bf16[256,512]{1,0:T(8,128)(2,1)S(1)}, bf16[256,512]{1,0:T(8,128)(2,1)S(1)}, u32[]{:S(2)}, u32[]{:S(2)}) collective-permute-start(bf16[256,512]{1,0:T(8,128)(2,1)S(1)} %pad_maximum_fusion.4.refs_0_), channel_id=1, source_target_pairs={{0,1},{1,0},{2,3},{3,2},{4,5},{5,4},{6,7},{7,6},{8,9},{9,8},{10,11... | collective-permute-start | bytes 786440 | tf_op jit(solution)/shard_map/ppermute | solution.py:467
  136.4 1.2 collective-permute-start.39
  137.6 2.7 %collective-permute-start.38 = (bf16[256,512]{1,0:T(8,128)(2,1)S(1)}, bf16[256,512]{1,0:T(8,128)(2,1)S(1)}, u32[]{:S(2)}, u32[]{:S(2)}) collective-permute-start(bf16[256,512]{1,0:T(8,128)(2,1)S(1)} %collective-permute-done.34.refs_2_), channel_id=1, source_target_pairs={{0,1},{1,0},{2,3},{3,2},{4,5},{5,4},{6,7},{7,6},{8,9},{9,8},{10,11... | collective-permute-start | bytes 786440 | tf_op jit(solution)/shard_map/ppermute | solution.py:467
  140.3 0.6 collective-permute-start.16
  140.9 0.5 collective-permute-done.38.refs_6_
  141.5 0.4 collective-permute-done.37.refs_5_
  142.1 2.6 %outputs.1 = (bf16[128,1024]{1,0:T(8,128)(2,1)}, bf16[128,512]{1,0:T(8,128)(2,1)}, bf16[128,512]{1,0:T(8,128)(2,1)}, bf16[64,128]{1,0:T(8,128)(2,1)}, f32[8,128,512]{2,1,0:T(8,128)}, /*index=5*/f32[8,512,128]{2,1,0:T(8,128)}) custom-call(s32[1]{0:T(128)} %bitcast.dp_ref.refs_1_, s32[1]{0:T(128)} %bitcast.1.ctx_ref.refs_2_, ...), custom_call_target="tpu_custom_call" | custom-call | tf_op jit(solution)/shard_map/outputs/pallas_call | solution.py:438
  (72 shorter events, 3.3 us)
Async XLA Ops:
  2.3 10.2 %collective-permute-start.1 = (bf16[128,640]{1,0:T(8,128)(2,1)}, bf16[128,640]{1,0:T(8,128)(2,1)S(1)}, u32[]{:S(2)}, u32[]{:S(2)}) collective-permute-start(bf16[128,640]{1,0:T(8,128)(2,1)} %key_rows.1.refs_7_), channel_id=1, source_target_pairs={{0,28},{1,29},{2,30},{3,31},{4,0},{5,1},{6,2},{7,3},{8,4},{9,5},{1... | collective-permute-start | bytes 491528 | tf_op jit(solution)/shard_map/ppermute | solution.py:467
  8.7 6.2 %collective-permute-start = (bf16[128,640]{1,0:T(8,128)(2,1)}, bf16[128,640]{1,0:T(8,128)(2,1)S(1)}, u32[]{:S(2)}, u32[]{:S(2)}) collective-permute-start(bf16[128,640]{1,0:T(8,128)(2,1)} %key_rows.1.refs_7_), channel_id=1, source_target_pairs={{0,4},{1,5},{2,6},{3,7},{4,8},{5,9},{6,10},{7,11},{8,12},{9,13},{1... | collective-permute-start | bytes 491528 | tf_op jit(solution)/shard_map/ppermute | solution.py:467
  8.7 29.6 %copy-start = (bf16[128,640]{1,0:T(8,128)(2,1)S(1)}, bf16[128,640]{1,0:T(8,128)(2,1)}, u32[]{:S(2)}) copy-start(bf16[128,640]{1,0:T(8,128)(2,1)} %key_rows.1.refs_7_) | copy-start | bytes 491524
  8.7 29.6 %copy-start.1 = (bf16[8,512,128]{2,1,0:T(8,128)(2,1)S(1)}, bf16[8,512,128]{2,1,0:T(8,128)(2,1)}, u32[]{:S(2)}) copy-start(bf16[8,512,128]{2,1,0:T(8,128)(2,1)} %refs_17_.1) | copy-start | bytes 3145732
  8.7 29.7 %copy-start.2 = (bf16[8,128,512]{2,1,0:T(8,128)(2,1)S(1)}, bf16[8,128,512]{2,1,0:T(8,128)(2,1)}, u32[]{:S(2)}) copy-start(bf16[8,128,512]{2,1,0:T(8,128)(2,1)} %refs_16_.1) | copy-start | bytes 3145732
  8.7 29.7 %copy-start.4 = (s32[1,64]{1,0:T(1,128)S(1)}, s32[1,64]{1,0:T(1,128)}, u32[]{:S(2)}) copy-start(s32[1,64]{1,0:T(1,128)} %refs_0_.1) | copy-start | bytes 772
  14.9 15.3 %collective-permute-start.2 = (bf16[128,2688]{1,0:T(8,128)(2,1)}, bf16[128,2688]{1,0:T(8,128)(2,1)S(1)}, u32[]{:S(2)}, u32[]{:S(2)}) collective-permute-start(bf16[128,2688]{1,0:T(8,128)(2,1)} %get-tuple-element.34.refs_3_), channel_id=1, source_target_pairs={{0,2},{1,3},{2,0},{3,1},{4,6},{5,7},{6,4},{7,5},{8,10},{9,11},{10,... | collective-permute-start | bytes 2064392 | tf_op jit(solution)/shard_map/ppermute | solution.py:467
  16.1 5.4 %collective-permute-start.3 = (bf16[128,640]{1,0:T(8,128)(2,1)S(1)}, bf16[128,640]{1,0:T(8,128)(2,1)S(1)}, u32[]{:S(2)}, u32[]{:S(2)}) collective-permute-start(bf16[128,640]{1,0:T(8,128)(2,1)S(1)} %collective-permute-done.refs_8_), channel_id=1, source_target_pairs={{0,4},{1,5},{2,6},{3,7},{4,8},{5,9},{6,10},{7,11},{8,12},{9,13},{1... | collective-permute-start | bytes 491528 | tf_op jit(solution)/shard_map/ppermute | solution.py:467
  16.1 5.4 %collective-permute-start.4 = (bf16[128,640]{1,0:T(8,128)(2,1)S(1)}, bf16[128,640]{1,0:T(8,128)(2,1)S(1)}, u32[]{:S(2)}, u32[]{:S(2)}) collective-permute-start(bf16[128,640]{1,0:T(8,128)(2,1)S(1)} %collective-permute-done.1.refs_9_), channel_id=1, source_target_pairs={{0,28},{1,29},{2,30},{3,31},{4,0},{5,1},{6,2},{7,3},{8,4},{9,5},{1... | collective-permute-start | bytes 491528 | tf_op jit(solution)/shard_map/ppermute | solution.py:467
  21.5 6.5 %collective-permute-start.5 = (bf16[128,640]{1,0:T(8,128)(2,1)S(1)}, bf16[128,640]{1,0:T(8,128)(2,1)S(1)}, u32[]{:S(2)}, u32[]{:S(2)}) collective-permute-start(bf16[128,640]{1,0:T(8,128)(2,1)S(1)} %collective-permute-done.3.refs_10_), channel_id=1, source_target_pairs={{0,4},{1,5},{2,6},{3,7},{4,8},{5,9},{6,10},{7,11},{8,12},{9,13},{1... | collective-permute-start | bytes 491528 | tf_op jit(solution)/shard_map/ppermute | solution.py:467
  21.5 6.5 %collective-permute-start.6 = (bf16[128,640]{1,0:T(8,128)(2,1)S(1)}, bf16[128,640]{1,0:T(8,128)(2,1)S(1)}, u32[]{:S(2)}, u32[]{:S(2)}) collective-permute-start(bf16[128,640]{1,0:T(8,128)(2,1)S(1)} %collective-permute-done.4.refs_11_), channel_id=1, source_target_pairs={{0,28},{1,29},{2,30},{3,31},{4,0},{5,1},{6,2},{7,3},{8,4},{9,5},{1... | collective-permute-start | bytes 491528 | tf_op jit(solution)/shard_map/ppermute | solution.py:467
  24.2 14.2 %collective-permute-start.7 = (bf16[128,2688]{1,0:T(8,128)(2,1)}, bf16[128,2688]{1,0:T(8,128)(2,1)S(1)}, u32[]{:S(2)}, u32[]{:S(2)}) collective-permute-start(bf16[128,2688]{1,0:T(8,128)(2,1)} %get-tuple-element.34.refs_3_), channel_id=1, source_target_pairs={{0,1},{1,0},{2,3},{3,2},{4,5},{5,4},{6,7},{7,6},{8,9},{9,8},{10,11... | collective-permute-start | bytes 2064392 | tf_op jit(solution)/shard_map/ppermute | solution.py:467
  30.2 8.2 %collective-permute-start.8 = (bf16[128,2688]{1,0:T(8,128)(2,1)S(1)}, bf16[128,2688]{1,0:T(8,128)(2,1)S(1)}, u32[]{:S(2)}, u32[]{:S(2)}) collective-permute-start(bf16[128,2688]{1,0:T(8,128)(2,1)S(1)} %collective-permute-done.2.refs_4_), channel_id=1, source_target_pairs={{0,1},{1,0},{2,3},{3,2},{4,5},{5,4},{6,7},{7,6},{8,9},{9,8},{10,11... | collective-permute-start | bytes 2064392 | tf_op jit(solution)/shard_map/ppermute | solution.py:467
  33.0 5.4 %collective-permute-start.9 = (bf16[64,640]{1,0:T(8,128)(2,1)S(1)}, bf16[64,640]{1,0:T(8,128)(2,1)S(1)}, u32[]{:S(2)}, u32[]{:S(2)}) collective-permute-start(bf16[64,640]{1,0:T(8,128)(2,1)S(1)} %slice.78), channel_id=1, source_target_pairs={{0,4},{1,5},{2,6},{3,7},{4,8},{5,9},{6,10},{7,11},{8,12},{9,13},{1... | collective-permute-start | bytes 245768 | tf_op jit(solution)/shard_map/ppermute | solution.py:467
  33.1 5.3 %collective-permute-start.10 = (bf16[64,640]{1,0:T(8,128)(2,1)S(1)}, bf16[64,640]{1,0:T(8,128)(2,1)S(1)}, u32[]{:S(2)}, u32[]{:S(2)}) collective-permute-start(bf16[64,640]{1,0:T(8,128)(2,1)S(1)} %slice.79), channel_id=1, source_target_pairs={{0,28},{1,29},{2,30},{3,31},{4,0},{5,1},{6,2},{7,3},{8,4},{9,5},{1... | collective-permute-start | bytes 245768 | tf_op jit(solution)/shard_map/ppermute | solution.py:467
  35.7 36.8 %collective-permute-start.20 = (bf16[4,128,512]{2,1,0:T(8,128)(2,1)}, bf16[4,128,512]{2,1,0:T(8,128)(2,1)S(1)}, u32[]{:S(2)}, u32[]{:S(2)}) collective-permute-start(bf16[4,128,512]{2,1,0:T(8,128)(2,1)} %get-tuple-element.53), channel_id=1, source_target_pairs={{0,1},{1,0},{2,3},{3,2},{4,5},{5,4},{6,7},{7,6},{8,9},{9,8},{10,11... | collective-permute-start | bytes 1572872 | tf_op jit(solution)/shard_map/ppermute | solution.py:467
  38.4 1.1 copy-start.3
  39.5 33.0 %copy-start.5 = (bf16[4,128,512]{2,1,0:T(8,128)(2,1)S(1)}, bf16[4,128,512]{2,1,0:T(8,128)(2,1)}, u32[]{:S(2)}) copy-start(bf16[4,128,512]{2,1,0:T(8,128)(2,1)} %get-tuple-element.52) | copy-start | bytes 1572868
  71.9 2.0 %collective-permute-start.19 = (bf16[4,128,512]{2,1,0:T(8,128)(2,1)S(1)}, bf16[4,128,512]{2,1,0:T(8,128)(2,1)S(1)}, u32[]{:S(2)}, u32[]{:S(2)}) collective-permute-start(bf16[4,128,512]{2,1,0:T(8,128)(2,1)S(1)} %get-tuple-element.51), channel_id=1, source_target_pairs={{0,1},{1,0},{2,3},{3,2},{4,5},{5,4},{6,7},{7,6},{8,9},{9,8},{10,11... | collective-permute-start | bytes 1572872 | tf_op jit(solution)/shard_map/ppermute | solution.py:467
  72.0 6.5 %collective-permute-start.11 = (bf16[448,640]{1,0:T(8,128)(2,1)S(1)}, bf16[448,640]{1,0:T(8,128)(2,1)S(1)}, u32[]{:S(2)}, u32[]{:S(2)}) collective-permute-start(bf16[448,640]{1,0:T(8,128)(2,1)S(1)} %get-tuple-element.47), channel_id=1, source_target_pairs={{0,1},{1,0},{2,3},{3,2},{4,5},{5,4},{6,7},{7,6},{8,9},{9,8},{10,11... | collective-permute-start | bytes 1720328 | tf_op jit(solution)/shard_map/ppermute | solution.py:467
  72.7 28.8 %collective-permute-start.17 = (bf16[2,128,1536]{2,1,0:T(8,128)(2,1)S(1)}, bf16[2,128,1536]{2,1,0:T(8,128)(2,1)S(1)}, u32[]{:S(2)}, u32[]{:S(2)}) collective-permute-start(bf16[2,128,1536]{2,1,0:T(8,128)(2,1)S(1)} %get-tuple-element.49), channel_id=1, source_target_pairs={{0,1},{1,0},{2,3},{3,2},{4,5},{5,4},{6,7},{7,6},{8,9},{9,8},{10,11... | collective-permute-start | bytes 2359304 | tf_op jit(solution)/shard_map/ppermute | solution.py:467
  74.1 9.6 %collective-permute-start.21 = (bf16[4,64,512]{2,1,0:T(8,128)(2,1)S(1)}, bf16[4,64,512]{2,1,0:T(8,128)(2,1)S(1)}, u32[]{:S(2)}, u32[]{:S(2)}) collective-permute-start(bf16[4,64,512]{2,1,0:T(8,128)(2,1)S(1)} %get-tuple-element.60), channel_id=1, source_target_pairs={{0,64},{1,65},{2,66},{3,67},{4,68},{5,69},{6,70},{7,71},{8,72},{9,... | collective-permute-start | bytes 786440 | tf_op jit(solution)/shard_map/ppermute | solution.py:467
  75.9 7.8 %collective-permute-start.23 = (bf16[4,64,512]{2,1,0:T(8,128)(2,1)S(1)}, bf16[4,64,512]{2,1,0:T(8,128)(2,1)S(1)}, u32[]{:S(2)}, u32[]{:S(2)}) collective-permute-start(bf16[4,64,512]{2,1,0:T(8,128)(2,1)S(1)} %get-tuple-element.61), channel_id=1, source_target_pairs={{0,192},{1,193},{2,194},{3,195},{4,196},{5,197},{6,198},{7,199},{8... | collective-permute-start | bytes 786440 | tf_op jit(solution)/shard_map/ppermute | solution.py:467
  77.4 12.8 %collective-permute-start.22 = (bf16[4,64,512]{2,1,0:T(8,128)(2,1)S(1)}, bf16[4,64,512]{2,1,0:T(8,128)(2,1)S(1)}, u32[]{:S(2)}, u32[]{:S(2)}) collective-permute-start(bf16[4,64,512]{2,1,0:T(8,128)(2,1)S(1)} %get-tuple-element.62), channel_id=1, source_target_pairs={{0,128},{1,129},{2,130},{3,131},{4,132},{5,133},{6,134},{7,135},{8... | collective-permute-start | bytes 786440 | tf_op jit(solution)/shard_map/ppermute | solution.py:467
  78.6 15.5 %collective-permute-start.12 = (bf16[128,640]{1,0:T(8,128)(2,1)S(1)}, bf16[128,640]{1,0:T(8,128)(2,1)S(1)}, u32[]{:S(2)}, u32[]{:S(2)}) collective-permute-start(bf16[128,640]{1,0:T(8,128)(2,1)S(1)} %pad_maximum_fusion.5), channel_id=1, source_target_pairs={{0,4},{1,29},{2,6},{3,31},{4,8},{5,1},{6,10},{7,3},{8,12},{9,5},{1... | collective-permute-start | bytes 491528 | tf_op jit(solution)/shard_map/ppermute | solution.py:467
  90.4 4.4 %collective-permute-start.24 = (bf16[64,512]{1,0:T(8,128)(2,1)S(1)}, bf16[64,512]{1,0:T(8,128)(2,1)S(1)}, u32[]{:S(2)}, u32[]{:S(2)}) collective-permute-start(bf16[64,512]{1,0:T(8,128)(2,1)S(1)} %get-tuple-element.69), channel_id=1, source_target_pairs={{0,2},{1,3},{2,32},{3,33},{4,6},{5,7},{6,36},{7,37},{8,10},{9,11},... | collective-permute-start | bytes 196616 | tf_op jit(solution)/shard_map/ppermute | solution.py:467
  90.5 4.3 %collective-permute-start.26 = (bf16[64,512]{1,0:T(8,128)(2,1)S(1)}, bf16[64,512]{1,0:T(8,128)(2,1)S(1)}, u32[]{:S(2)}, u32[]{:S(2)}) collective-permute-start(bf16[64,512]{1,0:T(8,128)(2,1)S(1)} %get-tuple-element.70), channel_id=1, source_target_pairs={{0,34},{1,35},{2,0},{3,1},{4,38},{5,39},{6,4},{7,5},{8,42},{9,43},... | collective-permute-start | bytes 196616 | tf_op jit(solution)/shard_map/ppermute | solution.py:467
  93.2 4.9 %collective-permute-start.25 = (bf16[64,512]{1,0:T(8,128)(2,1)S(1)}, bf16[64,512]{1,0:T(8,128)(2,1)S(1)}, u32[]{:S(2)}, u32[]{:S(2)}) collective-permute-start(bf16[64,512]{1,0:T(8,128)(2,1)S(1)} %get-tuple-element.71), channel_id=1, source_target_pairs={{0,32},{1,33},{2,34},{3,35},{4,36},{5,37},{6,38},{7,39},{8,40},{9,... | collective-permute-start | bytes 196616 | tf_op jit(solution)/shard_map/ppermute | solution.py:467
  98.1 3.2 %collective-permute-start.27 = (bf16[64,512]{1,0:T(8,128)(2,1)S(1)}, bf16[64,512]{1,0:T(8,128)(2,1)S(1)}, u32[]{:S(2)}, u32[]{:S(2)}) collective-permute-start(bf16[64,512]{1,0:T(8,128)(2,1)S(1)} %fusion.12), channel_id=1, source_target_pairs={{0,4},{1,5},{2,6},{3,7},{4,0},{5,1},{6,2},{7,3},{8,12},{9,13},{10,... | collective-permute-start | bytes 196616 | tf_op jit(solution)/shard_map/ppermute | solution.py:467
  98.3 11.2 %collective-permute-start.13 = (bf16[256,640]{1,0:T(8,128)(2,1)S(1)}, bf16[256,640]{1,0:T(8,128)(2,1)S(1)}, u32[]{:S(2)}, u32[]{:S(2)}) collective-permute-start(bf16[256,640]{1,0:T(8,128)(2,1)S(1)} %pad_maximum_fusion), channel_id=1, source_target_pairs={{0,4},{1,29},{2,6},{3,31},{4,8},{5,1},{6,10},{7,3},{8,12},{9,5},{1... | collective-permute-start | bytes 983048 | tf_op jit(solution)/shard_map/ppermute | solution.py:467
  101.4 5.8 %collective-permute-start.28 = (bf16[64,512]{1,0:T(8,128)(2,1)S(1)}, bf16[64,512]{1,0:T(8,128)(2,1)S(1)}, u32[]{:S(2)}, u32[]{:S(2)}) collective-permute-start(bf16[64,512]{1,0:T(8,128)(2,1)S(1)} %add_convert_fusion.11), channel_id=1, source_target_pairs={{0,8},{1,9},{2,10},{3,11},{4,12},{5,13},{6,14},{7,15},{8,0},{9,1},... | collective-permute-start | bytes 196616 | tf_op jit(solution)/shard_map/ppermute | solution.py:467
  107.2 7.1 %collective-permute-start.29 = (bf16[64,512]{1,0:T(8,128)(2,1)S(1)}, bf16[64,512]{1,0:T(8,128)(2,1)S(1)}, u32[]{:S(2)}, u32[]{:S(2)}) collective-permute-start(bf16[64,512]{1,0:T(8,128)(2,1)S(1)} %add_convert_fusion.10), channel_id=1, source_target_pairs={{0,16},{1,17},{2,18},{3,19},{4,20},{5,21},{6,22},{7,23},{8,24},{9,... | collective-permute-start | bytes 196616 | tf_op jit(solution)/shard_map/ppermute | solution.py:467
  109.6 8.6 %collective-permute-start.14 = (bf16[256,640]{1,0:T(8,128)(2,1)S(1)}, bf16[256,640]{1,0:T(8,128)(2,1)S(1)}, u32[]{:S(2)}, u32[]{:S(2)}) collective-permute-start(bf16[256,640]{1,0:T(8,128)(2,1)S(1)} %pad_maximum_fusion.1), channel_id=1, source_target_pairs={{0,4},{1,29},{2,6},{3,31},{4,8},{5,1},{6,10},{7,3},{8,12},{9,5},{1... | collective-permute-start | bytes 983048 | tf_op jit(solution)/shard_map/ppermute | solution.py:467
  110.0 30.4 %collective-permute-start.18 = (bf16[128,1536]{1,0:T(8,128)(2,1)S(1)}, bf16[128,1536]{1,0:T(8,128)(2,1)S(1)}, u32[]{:S(2)}, u32[]{:S(2)}) collective-permute-start(bf16[128,1536]{1,0:T(8,128)(2,1)S(1)} %slice_bitcast_fusion), channel_id=1, source_target_pairs={{0,2},{1,3},{2,0},{3,1},{4,6},{5,7},{6,4},{7,5},{8,10},{9,11},{10,... | collective-permute-start | bytes 1179656 | tf_op jit(solution)/shard_map/ppermute | solution.py:467
  114.3 4.8 %collective-permute-start.32 = (bf16[64,512]{1,0:T(8,128)(2,1)S(1)}, bf16[64,512]{1,0:T(8,128)(2,1)S(1)}, u32[]{:S(2)}, u32[]{:S(2)}) collective-permute-start(bf16[64,512]{1,0:T(8,128)(2,1)S(1)} %add_convert_fusion.9), channel_id=1, source_target_pairs={{0,34},{1,35},{2,0},{3,1},{4,38},{5,39},{6,4},{7,5},{8,42},{9,43},... | collective-permute-start | bytes 196616 | tf_op jit(solution)/shard_map/ppermute | solution.py:467
  114.6 5.3 %collective-permute-start.31 = (bf16[64,512]{1,0:T(8,128)(2,1)S(1)}, bf16[64,512]{1,0:T(8,128)(2,1)S(1)}, u32[]{:S(2)}, u32[]{:S(2)}) collective-permute-start(bf16[64,512]{1,0:T(8,128)(2,1)S(1)} %add_convert_fusion.9), channel_id=1, source_target_pairs={{0,32},{1,33},{2,34},{3,35},{4,36},{5,37},{6,38},{7,39},{8,40},{9,... | collective-permute-start | bytes 196616 | tf_op jit(solution)/shard_map/ppermute | solution.py:467
  115.6 5.0 %collective-permute-start.30 = (bf16[64,512]{1,0:T(8,128)(2,1)S(1)}, bf16[64,512]{1,0:T(8,128)(2,1)S(1)}, u32[]{:S(2)}, u32[]{:S(2)}) collective-permute-start(bf16[64,512]{1,0:T(8,128)(2,1)S(1)} %add_convert_fusion.9), channel_id=1, source_target_pairs={{0,2},{1,3},{2,32},{3,33},{4,6},{5,7},{6,36},{7,37},{8,10},{9,11},... | collective-permute-start | bytes 196616 | tf_op jit(solution)/shard_map/ppermute | solution.py:467
  118.4 22.0 %collective-permute-start.15 = (bf16[256,640]{1,0:T(8,128)(2,1)S(1)}, bf16[256,640]{1,0:T(8,128)(2,1)S(1)}, u32[]{:S(2)}, u32[]{:S(2)}) collective-permute-start(bf16[256,640]{1,0:T(8,128)(2,1)S(1)} %pad_maximum_fusion.2), channel_id=1, source_target_pairs={{0,4},{1,29},{2,6},{3,31},{4,8},{5,1},{6,10},{7,3},{8,12},{9,5},{1... | collective-permute-start | bytes 983048 | tf_op jit(solution)/shard_map/ppermute | solution.py:467
  120.6 5.6 %collective-permute-start.35 = (bf16[256,512]{1,0:T(8,128)(2,1)S(1)}, bf16[256,512]{1,0:T(8,128)(2,1)S(1)}, u32[]{:S(2)}, u32[]{:S(2)}) collective-permute-start(bf16[256,512]{1,0:T(8,128)(2,1)S(1)} %pad_maximum_fusion.4.refs_0_), channel_id=1, source_target_pairs={{0,192},{1,193},{2,194},{3,195},{4,196},{5,197},{6,198},{7,199},{8... | collective-permute-start | bytes 786440 | tf_op jit(solution)/shard_map/ppermute | solution.py:467
  122.1 14.3 %collective-permute-start.34 = (bf16[256,512]{1,0:T(8,128)(2,1)S(1)}, bf16[256,512]{1,0:T(8,128)(2,1)S(1)}, u32[]{:S(2)}, u32[]{:S(2)}) collective-permute-start(bf16[256,512]{1,0:T(8,128)(2,1)S(1)} %pad_maximum_fusion.4.refs_0_), channel_id=1, source_target_pairs={{0,128},{1,129},{2,130},{3,131},{4,132},{5,133},{6,134},{7,135},{8... | collective-permute-start | bytes 786440 | tf_op jit(solution)/shard_map/ppermute | solution.py:467
  124.0 13.6 %collective-permute-start.33 = (bf16[256,512]{1,0:T(8,128)(2,1)S(1)}, bf16[256,512]{1,0:T(8,128)(2,1)S(1)}, u32[]{:S(2)}, u32[]{:S(2)}) collective-permute-start(bf16[256,512]{1,0:T(8,128)(2,1)S(1)} %pad_maximum_fusion.4.refs_0_), channel_id=1, source_target_pairs={{0,64},{1,65},{2,66},{3,67},{4,68},{5,69},{6,70},{7,71},{8,72},{9,... | collective-permute-start | bytes 786440 | tf_op jit(solution)/shard_map/ppermute | solution.py:467
  126.2 14.7 %collective-permute-start.36 = (bf16[256,512]{1,0:T(8,128)(2,1)S(1)}, bf16[256,512]{1,0:T(8,128)(2,1)S(1)}, u32[]{:S(2)}, u32[]{:S(2)}) collective-permute-start(bf16[256,512]{1,0:T(8,128)(2,1)S(1)} %pad_maximum_fusion.4.refs_0_), channel_id=1, source_target_pairs={{0,1},{1,0},{2,3},{3,2},{4,5},{5,4},{6,7},{7,6},{8,9},{9,8},{10,11... | collective-permute-start | bytes 786440 | tf_op jit(solution)/shard_map/ppermute | solution.py:467
  136.4 4.6 %collective-permute-start.39 = (bf16[256,512]{1,0:T(8,128)(2,1)S(1)}, bf16[256,512]{1,0:T(8,128)(2,1)S(1)}, u32[]{:S(2)}, u32[]{:S(2)}) collective-permute-start(bf16[256,512]{1,0:T(8,128)(2,1)S(1)} %collective-permute-done.35.refs_3_), channel_id=1, source_target_pairs={{0,1},{1,0},{2,3},{3,2},{4,5},{5,4},{6,7},{7,6},{8,9},{9,8},{10,11... | collective-permute-start | bytes 786440 | tf_op jit(solution)/shard_map/ppermute | solution.py:467
  137.6 3.9 %collective-permute-start.38 = (bf16[256,512]{1,0:T(8,128)(2,1)S(1)}, bf16[256,512]{1,0:T(8,128)(2,1)S(1)}, u32[]{:S(2)}, u32[]{:S(2)}) collective-permute-start(bf16[256,512]{1,0:T(8,128)(2,1)S(1)} %collective-permute-done.34.refs_2_), channel_id=1, source_target_pairs={{0,1},{1,0},{2,3},{3,2},{4,5},{5,4},{6,7},{7,6},{8,9},{9,8},{10,11... | collective-permute-start | bytes 786440 | tf_op jit(solution)/shard_map/ppermute | solution.py:467
  140.3 1.5 %collective-permute-start.37 = (bf16[256,512]{1,0:T(8,128)(2,1)S(1)}, bf16[256,512]{1,0:T(8,128)(2,1)S(1)}, u32[]{:S(2)}, u32[]{:S(2)}) collective-permute-start(bf16[256,512]{1,0:T(8,128)(2,1)S(1)} %collective-permute-done.33.refs_1_), channel_id=1, source_target_pairs={{0,1},{1,0},{2,3},{3,2},{4,5},{5,4},{6,7},{7,6},{8,9},{9,8},{10,11... | collective-permute-start | bytes 786440 | tf_op jit(solution)/shard_map/ppermute | solution.py:467
  140.3 1.7 %collective-permute-start.16 = (bf16[128,640]{1,0:T(8,128)(2,1)S(1)}, bf16[128,640]{1,0:T(8,128)(2,1)S(1)}, u32[]{:S(2)}, u32[]{:S(2)}) collective-permute-start(bf16[128,640]{1,0:T(8,128)(2,1)S(1)} %slice.114), channel_id=1, source_target_pairs={{0,1},{1,0},{2,3},{3,2},{4,5},{5,4},{6,7},{7,6},{8,9},{9,8},{10,11... | collective-permute-start | bytes 491528 | tf_op jit(solution)/shard_map/ppermute | solution.py:467

commit v2 on v1

--- a/solution.py
+++ b/solution.py
@@ -137,7 +137,7 @@
     n = 2 + nb // 2
     dk_own, dk_far, dk, dk_send = out[0], out[1], out[2 : n - 1], out[n - 1]
     (keep, send), weights = out[n : n + 2], out[n + 2 : n + 2 + nc]
-    PK, KC, Q, G, LB, DB, K, KP, DL, DQ, DO, WA, sems = out[n + 2 + nc :]
+    KC, Q, G, LB, DB, K, KP, DL, DQ, DO, WA = out[n + 2 + nc :]
     y, x, z, core = places(grid, dp_ref[0], ctx_ref[0])
     offsets = [0] + [o for s in range(1, nb // 2) for o in (-s, s)] + [nb // 2]
     xl = x % nxl
@@ -154,23 +154,8 @@
     per = nb // nkb
     kw = per * ch
 
-    copies = [pltpu.make_async_copy(
-            packs[a], PK.at[pl.ds(a * tokens, tokens)], sems.at[a]
-        ) for a in range(na)]
-    copies += [
-        pltpu.make_async_copy(keys[b].at[pl.ds(0, tokens)], KC.at[b], sems.at[na + b])
-        for b in range(nb - 1)
-    ]
     own_half = pl.ds(pl.multiple_of(core * ch, ch), ch)
     other_half = pl.ds(pl.multiple_of((1 - core) * ch, ch), ch)
-    for b, rows_at in ((nb - 1, pl.ds(0, ch)), (nb, pl.ds(ch, ch))):
-        copies.append(
-            pltpu.make_async_copy(
-                keys[b].at[pl.ds(0, ch)], KC.at[nb - 1, rows_at], sems.at[na + b]
-            )
-        )
-    for c in copies:
-        c.start()
 
     def first_of(z_, xl_, c_):
         return ids[0, 2 * ((z_ * nxl + xl_) * nc + c_)]
@@ -197,31 +182,30 @@
 
     DL[...] = jnp.zeros_like(DL)
 
-    for c in copies[:na]:
-        c.wait()
 
     lows = [jnp.where(2 * c < spans, 0, 1) for c in qc]
-    stats = PK[:, wn + wr + wn :].astype(F32)
-    stats = stats[:, : 2 * heads] + stats[:, 2 * heads : 4 * heads] + stats[:, 4 * heads : 6 * heads]
-    for h in range(heads):
-        ql = dot_nn(PK[:, h * hd : (h + 1) * hd], wk[h]).astype(BF)
-        gl = dot_nt(PK[:, wn + wr + h * hd : wn + wr + (h + 1) * hd], wv[h]).astype(BF)
-        qrot = PK[:, wn + h * dr : wn + (h + 1) * dr]
-        to = slice(h * ch, (h + 1) * ch)
-        for a, slot in itertools.product(range(na), range(2)):
-            mine = slice((2 * a + slot) * ch, (2 * a + slot + 1) * ch)
-            half = lows[a] if slot == 0 else 1 - lows[a]
-            Q[a, half, to, :dc] = ql[mine]
-            Q[a, half, to, dc : dc + dr] = qrot[mine]
-            Q[a, half, to, dc + dr :] = jnp.zeros((ch, width - dc - dr), BF)
-            G[a, half, to, :] = gl[mine]
-            LB[a, half, to, :] = jnp.broadcast_to(stats[mine, h : h + 1], (ch, 128))
-            DB[a, half, to, :] = jnp.broadcast_to(
-                stats[mine, heads + h : heads + h + 1], (ch, 128)
-            )
-
-    for c in copies[na:]:
-        c.wait()
+    for a in range(na):
+        stats = packs[a][:, wn + wr + wn :].astype(F32)
+        stats = (
+            stats[:, : 2 * heads] + stats[:, 2 * heads : 4 * heads] + stats[:, 4 * heads : 6 * heads]
+        )
+        for h in range(heads):
+            ql = dot_nn(packs[a][:, h * hd : (h + 1) * hd], wk[h]).astype(BF)
+            gl = dot_nt(packs[a][:, wn + wr + h * hd : wn + wr + (h + 1) * hd], wv[h]).astype(BF)
+            qrot = packs[a][:, wn + h * dr : wn + (h + 1) * dr]
+            to = slice(h * ch, (h + 1) * ch)
+            for slot in range(2):
+                mine = slice(slot * ch, (slot + 1) * ch)
+                half = lows[a] if slot == 0 else 1 - lows[a]
+                Q[a, half, to, :dc] = ql[mine]
+                Q[a, half, to, dc : dc + dr] = qrot[mine]
+                Q[a, half, to, dc + dr :] = jnp.zeros((ch, width - dc - dr), BF)
+                G[a, half, to, :] = gl[mine]
+                LB[a, half, to, :] = jnp.broadcast_to(stats[mine, h : h + 1], (ch, 128))
+                DB[a, half, to, :] = jnp.broadcast_to(
+                    stats[mine, heads + h : heads + h + 1], (ch, 128)
+                )
+
     lane = lax.broadcasted_iota(jnp.int32, (8, kw), 1)
     kps = [jnp.zeros((8, kw), jnp.int32) for _ in range(2 * nkb)]
     key_at = []
@@ -232,8 +216,13 @@
         low_at = pl.multiple_of(jnp.where(first, 0, ch), ch)
         high_at = pl.multiple_of(jnp.where(first, ch, 0), ch)
         key_at.append((blk, pos, low_at, high_at))
-        K[blk, pl.ds(pos, ch), :] = KC[b, pl.ds(low_at, ch), :]
-        K[nkb + blk, pl.ds(pos, ch), :] = KC[b, pl.ds(high_at, ch), :]
+        if b < nb - 1:
+            low_rows, high_rows = keys[b][pl.ds(low_at, ch), :], keys[b][pl.ds(high_at, ch), :]
+        else:
+            low_rows = jnp.where(first, keys[nb - 1][...], keys[nb][...])
+            high_rows = jnp.where(first, keys[nb][...], keys[nb - 1][...])
+        K[blk, pl.ds(pos, ch), :] = low_rows
+        K[nkb + blk, pl.ds(pos, ch), :] = high_rows
         inside = jnp.logical_and(lane >= pos, lane < pos + ch)
         for i in range(nkb):
             here = jnp.logical_and(inside, blk == i)
@@ -338,7 +327,9 @@
     for i, j, k in itertools.product(range(nc), range(ny), range(per_y)):
         h = (core + i) % nc * per_core + (y + j) % ny * per_y + k
         cols = pl.ds(pl.multiple_of(h * hd, hd), hd)
-        w = dot_tn(PK[:, cols], WA[h]).astype(BF)
+        w = sum(
+            dot_tn(packs[a][:, cols], WA[h, a * tokens : (a + 1) * tokens, :]) for a in range(na)
+        ).astype(BF)
         for n in range(nx):
             at = pl.multiple_of((n - x + nx) % nx * group, group)
             weights[i][j * per_y + k, pl.ds(at, group), :] = w[n * group : (n + 1) * group]
@@ -356,7 +347,7 @@
     out = heads * hd + wr
     return pl.pallas_call(
         functools.partial(attn_kernel, grid, na, heads, ids.shape[1], scaling),
-        in_specs=[SMEM] * 3 + [ANY] * (na + nb + 1) + [VMEM] * 2,
+        in_specs=[SMEM] * 3 + [VMEM] * (na + nb + 3),
         out_shape=(
             (
                 jax.ShapeDtypeStruct((tokens, width), BF),
@@ -369,7 +360,6 @@
         ),
         out_specs=(VMEM,) * (nb // 2 + 4 + nc),
         scratch_shapes=[
-            pltpu.VMEM((na * tokens, packs[0].shape[1]), BF),
             pltpu.VMEM((nb, tokens, width), BF),
             pltpu.VMEM((na, 2, rows, width), BF),
             pltpu.VMEM((na, 2, rows, dc), BF),
@@ -381,7 +371,6 @@
             pltpu.VMEM((2, rows, width), F32),
             pltpu.VMEM((na, tokens, out), BF),
             pltpu.VMEM((heads, na * tokens, dc), BF),
-            pltpu.SemaphoreType.DMA((na + nb + 1,)),
         ],
         compiler_params=vmem(44),
         cost_estimate=pl.CostEstimate(

time: 145 us -> 142 us (0.979)
  waiting for transfers between devices: 40.6 us -> 37.8 us
  Pallas kernels: 40.5 us -> 37.8 us
  starting transfers between devices: 60.4 us -> 63.1 us
    ppermute x40, waiting for transfers between devices: 40.6 us -> 37.8 us  [all_perm(): return lax.ppermute(x, ('dp', 'ctx'), pairs)]
    pallas_call x1, Pallas kernels: 32.4 us -> 29.7 us  [attn_call(): pl.pallas_call(functools.partial(attn_kernel, grid, na, heads, ids.shape[...]
    ppermute x40, starting transfers between devices: 60.4 us -> 63.1 us  [all_perm(): return lax.ppermute(x, ('dp', 'ctx'), pairs)]
  transfers between devices with their start and end apart: 40 -> 40, of which waited for: 19 -> 17; matrix products, arithmetic and copies ran while one was open for 1% -> 1% of each run, Pallas kernels for 25% -> 24%
where the time goes in v2:
time: 142 us
  starting transfers between devices  63.1 us (44%)
  Pallas kernels  37.8 us (27%)
  waiting for transfers between devices  37.8 us (27%)
    ppermute x40, starting transfers between devices, all_perm(): return lax.ppermute(x, ('dp', 'ctx'), pairs)  63.1 us
    ppermute x40, waiting for transfers between devices, all_perm(): return lax.ppermute(x, ('dp', 'ctx'), pairs)  37.8 us
    pallas_call x1, Pallas kernels, attn_call(): pl.pallas_call(functools.partial(attn_kernel, grid, na, heads, ids.shape[...  29.7 us
    pallas_call x1, Pallas kernels, own_call(): pl.pallas_call(functools.partial(own_kernel, grid), in_specs=[SMEM, SMEM]...  3.8 us
  transfers between devices with their start and end apart: 40, of which 17 were waited for; matrix products, arithmetic and copies ran while one was open for 1% of the time, Pallas kernels for 24%

profile of v2, /device:TPU:1, one launch (start us, length us, event | category | flops | bytes accessed | tf_op | source)
XLA Modules:
  0.0 141.8 jit_solution(7097125774227016482)
XLA Ops:
  0.6 1.7 %key_rows.1.refs_7_ = bf16[128,640]{1,0:T(8,128)(2,1)} custom-call(bf16[128,512]{1,0:T(8,128)(2,1)} %bitcast.49, bf16[64,128]{1,0:T(8,128)(2,1)} %bitcast.50), custom_call_target="tpu_custom_call" | custom-call | tf_op jit(solution)/shard_map/key_rows/pallas_call | solution.py:118
  2.3 6.4 %collective-permute-start.1 = (bf16[128,640]{1,0:T(8,128)(2,1)}, bf16[128,640]{1,0:T(8,128)(2,1)S(1)}, u32[]{:S(2)}, u32[]{:S(2)}) collective-permute-start(bf16[128,640]{1,0:T(8,128)(2,1)} %key_rows.1.refs_7_), channel_id=1, source_target_pairs={{0,28},{1,29},{2,30},{3,31},{4,0},{5,1},{6,2},{7,3},{8,4},{9,5},{1... | collective-permute-start | bytes 491528 | tf_op jit(solution)/shard_map/ppermute | solution.py:456
  8.7 3.8 %own_rows.1 = (bf16[128,2688]{1,0:T(8,128)(2,1)}, bf16[4,128,512]{2,1,0:T(8,128)(2,1)}, bf16[4,128,512]{2,1,0:T(8,128)(2,1)}) custom-call(s32[1]{0:T(128)} %bitcast.dp_ref.refs_1_, s32[1]{0:T(128)} %bitcast.1.ctx_ref.refs_2_, bf16[128,1024]{1,0:T(8,128)(2,1)} %bitcast.52, bf16[128,512]{1,0:T(8,128)(2,1)} %bitcast.55, bf16[128,1024]{1,0:T(8,128)(2,1)} %bitcast.53, ...), custom_call_target="tpu_custom_call" | custom-call | flops 4000000000 | bytes 4000000 | tf_op jit(solution)/shard_map/own_rows/pallas_call | solution.py:96
  12.5 2.3 %collective-permute-done.refs_8_ = bf16[128,640]{1,0:T(8,128)(2,1)S(1)} collective-permute-done((bf16[128,640]{1,0:T(8,128)(2,1)}, bf16[128,640]{1,0:T(8,128)(2,1)S(1)}, u32[]{:S(2)}, u32[]{:S(2)}) %collective-permute-start) | collective-permute-done | bytes 163872 | tf_op jit(solution)/shard_map/ppermute | solution.py:456
  14.9 1.2 collective-permute-start.2
  16.1 2.7 %collective-permute-start.4 = (bf16[128,640]{1,0:T(8,128)(2,1)S(1)}, bf16[128,640]{1,0:T(8,128)(2,1)S(1)}, u32[]{:S(2)}, u32[]{:S(2)}) collective-permute-start(bf16[128,640]{1,0:T(8,128)(2,1)S(1)} %collective-permute-done.1.refs_9_), channel_id=1, source_target_pairs={{0,28},{1,29},{2,30},{3,31},{4,0},{5,1},{6,2},{7,3},{8,4},{9,5},{1... | collective-permute-start | bytes 491528 | tf_op jit(solution)/shard_map/ppermute | solution.py:456
  18.8 2.7 %collective-permute-done.3.refs_10_ = bf16[128,640]{1,0:T(8,128)(2,1)S(1)} collective-permute-done((bf16[128,640]{1,0:T(8,128)(2,1)S(1)}, bf16[128,640]{1,0:T(8,128)(2,1)S(1)}, u32[]{:S(2)}, u32[]{:S(2)}) %collective-permute-start.3) | collective-permute-done | bytes 163872 | tf_op jit(solution)/shard_map/ppermute | solution.py:456
  21.5 2.7 %collective-permute-start.6 = (bf16[128,640]{1,0:T(8,128)(2,1)S(1)}, bf16[128,640]{1,0:T(8,128)(2,1)S(1)}, u32[]{:S(2)}, u32[]{:S(2)}) collective-permute-start(bf16[128,640]{1,0:T(8,128)(2,1)S(1)} %collective-permute-done.4.refs_11_), channel_id=1, source_target_pairs={{0,28},{1,29},{2,30},{3,31},{4,0},{5,1},{6,2},{7,3},{8,4},{9,5},{1... | collective-permute-start | bytes 491528 | tf_op jit(solution)/shard_map/ppermute | solution.py:456
  24.2 3.9 %collective-permute-start.7 = (bf16[128,2688]{1,0:T(8,128)(2,1)}, bf16[128,2688]{1,0:T(8,128)(2,1)S(1)}, u32[]{:S(2)}, u32[]{:S(2)}) collective-permute-start(bf16[128,2688]{1,0:T(8,128)(2,1)} %get-tuple-element.34.refs_3_), channel_id=1, source_target_pairs={{0,1},{1,0},{2,3},{3,2},{4,5},{5,4},{6,7},{7,6},{8,9},{9,8},{10,11... | collective-permute-start | bytes 2064392 | tf_op jit(solution)/shard_map/ppermute | solution.py:456
  28.0 2.1 %collective-permute-done.2.refs_4_ = bf16[128,2688]{1,0:T(8,128)(2,1)S(1)} collective-permute-done((bf16[128,2688]{1,0:T(8,128)(2,1)}, bf16[128,2688]{1,0:T(8,128)(2,1)S(1)}, u32[]{:S(2)}, u32[]{:S(2)}) %collective-permute-start.2) | collective-permute-done | bytes 688160 | tf_op jit(solution)/shard_map/ppermute | solution.py:456
  30.2 2.8 %collective-permute-start.8 = (bf16[128,2688]{1,0:T(8,128)(2,1)S(1)}, bf16[128,2688]{1,0:T(8,128)(2,1)S(1)}, u32[]{:S(2)}, u32[]{:S(2)}) collective-permute-start(bf16[128,2688]{1,0:T(8,128)(2,1)S(1)} %collective-permute-done.2.refs_4_), channel_id=1, source_target_pairs={{0,1},{1,0},{2,3},{3,2},{4,5},{5,4},{6,7},{7,6},{8,9},{9,8},{10,11... | collective-permute-start | bytes 2064392 | tf_op jit(solution)/shard_map/ppermute | solution.py:456
  33.1 2.7 %collective-permute-start.10 = (bf16[64,640]{1,0:T(8,128)(2,1)S(1)}, bf16[64,640]{1,0:T(8,128)(2,1)S(1)}, u32[]{:S(2)}, u32[]{:S(2)}) collective-permute-start(bf16[64,640]{1,0:T(8,128)(2,1)S(1)} %slice.79), channel_id=1, source_target_pairs={{0,28},{1,29},{2,30},{3,31},{4,0},{5,1},{6,2},{7,3},{8,4},{9,5},{1... | collective-permute-start | bytes 245768 | tf_op jit(solution)/shard_map/ppermute | solution.py:456
  35.7 0.6 collective-permute-start.20
  36.3 2.0 %collective-permute-done.9.refs_14_ = bf16[64,640]{1,0:T(8,128)(2,1)S(1)} collective-permute-done((bf16[64,640]{1,0:T(8,128)(2,1)S(1)}, bf16[64,640]{1,0:T(8,128)(2,1)S(1)}, u32[]{:S(2)}, u32[]{:S(2)}) %collective-permute-start.9) | collective-permute-done | bytes 81952 | tf_op jit(solution)/shard_map/ppermute | solution.py:456
  38.4 1.1 copy-done.3
  39.5 29.7 %attn_grads.1 = (bf16[128,640]{1,0:T(8,128)(2,1)S(1)}, bf16[64,640]{1,0:T(8,128)(2,1)S(1)}, bf16[128,640]{1,0:T(8,128)(2,1)S(1)}, bf16[128,640]{1,0:T(8,128)(2,1...) custom-call(s32[1,64]{1,0:T(1,128)S(1)} %copy-done.4, ...), custom_call_target="tpu_custom_call" | custom-call | flops 30000001024 | bytes 10000000 | tf_op jit(solution)/shard_map/attn_grads/pallas_call | solution.py:348
  69.2 0.8 collective-permute-start.19
  70.3 0.5 collective-permute-start.17
  70.8 0.8 collective-permute-done.19
  71.9 2.7 %collective-permute-start.23 = (bf16[4,64,512]{2,1,0:T(8,128)(2,1)S(1)}, bf16[4,64,512]{2,1,0:T(8,128)(2,1)S(1)}, u32[]{:S(2)}, u32[]{:S(2)}) collective-permute-start(bf16[4,64,512]{2,1,0:T(8,128)(2,1)S(1)} %get-tuple-element.61), channel_id=1, source_target_pairs={{0,192},{1,193},{2,194},{3,195},{4,196},{5,197},{6,198},{7,199},{8... | collective-permute-start | bytes 786440 | tf_op jit(solution)/shard_map/ppermute | solution.py:456
  74.5 1.3 collective-permute-start.22
  75.9 3.2 %collective-permute-start.12 = (bf16[128,640]{1,0:T(8,128)(2,1)S(1)}, bf16[128,640]{1,0:T(8,128)(2,1)S(1)}, u32[]{:S(2)}, u32[]{:S(2)}) collective-permute-start(bf16[128,640]{1,0:T(8,128)(2,1)S(1)} %pad_maximum_fusion.5), channel_id=1, source_target_pairs={{0,4},{1,29},{2,6},{3,31},{4,8},{5,1},{6,10},{7,3},{8,12},{9,5},{1... | collective-permute-start | bytes 491528 | tf_op jit(solution)/shard_map/ppermute | solution.py:456
  79.0 1.5 %collective-permute-done.21 = bf16[4,64,512]{2,1,0:T(8,128)(2,1)S(1)} collective-permute-done((bf16[4,64,512]{2,1,0:T(8,128)(2,1)S(1)}, bf16[4,64,512]{2,1,0:T(8,128)(2,1)S(1)}, u32[]{:S(2)}, u32[]{:S(2)}) %collective-permute-start.21) | collective-permute-done | bytes 262176 | tf_op jit(solution)/shard_map/ppermute | solution.py:456
  80.6 5.9 %collective-permute-done.22 = bf16[4,64,512]{2,1,0:T(8,128)(2,1)S(1)} collective-permute-done((bf16[4,64,512]{2,1,0:T(8,128)(2,1)S(1)}, bf16[4,64,512]{2,1,0:T(8,128)(2,1)S(1)}, u32[]{:S(2)}, u32[]{:S(2)}) %collective-permute-start.22) | collective-permute-done | bytes 262176 | tf_op jit(solution)/shard_map/ppermute | solution.py:456
  86.6 1.2 collective-permute-start.24
  87.8 2.5 %collective-permute-start.26 = (bf16[64,512]{1,0:T(8,128)(2,1)S(1)}, bf16[64,512]{1,0:T(8,128)(2,1)S(1)}, u32[]{:S(2)}, u32[]{:S(2)}) collective-permute-start(bf16[64,512]{1,0:T(8,128)(2,1)S(1)} %get-tuple-element.70), channel_id=1, source_target_pairs={{0,34},{1,35},{2,0},{3,1},{4,38},{5,39},{6,4},{7,5},{8,42},{9,43},... | collective-permute-start | bytes 196616 | tf_op jit(solution)/shard_map/ppermute | solution.py:456
  90.3 1.4 %collective-permute-start.25 = (bf16[64,512]{1,0:T(8,128)(2,1)S(1)}, bf16[64,512]{1,0:T(8,128)(2,1)S(1)}, u32[]{:S(2)}, u32[]{:S(2)}) collective-permute-start(bf16[64,512]{1,0:T(8,128)(2,1)S(1)} %get-tuple-element.71), channel_id=1, source_target_pairs={{0,32},{1,33},{2,34},{3,35},{4,36},{5,37},{6,38},{7,39},{8,40},{9,... | collective-permute-start | bytes 196616 | tf_op jit(solution)/shard_map/ppermute | solution.py:456
  91.8 3.1 %collective-permute-done.25 = bf16[64,512]{1,0:T(8,128)(2,1)S(1)} collective-permute-done((bf16[64,512]{1,0:T(8,128)(2,1)S(1)}, bf16[64,512]{1,0:T(8,128)(2,1)S(1)}, u32[]{:S(2)}, u32[]{:S(2)}) %collective-permute-start.25) | collective-permute-done | bytes 65568 | tf_op jit(solution)/shard_map/ppermute | solution.py:456
  95.1 3.2 %collective-permute-start.13 = (bf16[256,640]{1,0:T(8,128)(2,1)S(1)}, bf16[256,640]{1,0:T(8,128)(2,1)S(1)}, u32[]{:S(2)}, u32[]{:S(2)}) collective-permute-start(bf16[256,640]{1,0:T(8,128)(2,1)S(1)} %pad_maximum_fusion), channel_id=1, source_target_pairs={{0,4},{1,29},{2,6},{3,31},{4,8},{5,1},{6,10},{7,3},{8,12},{9,5},{1... | collective-permute-start | bytes 983048 | tf_op jit(solution)/shard_map/ppermute | solution.py:456
  98.8 4.5 %collective-permute-done.28 = bf16[64,512]{1,0:T(8,128)(2,1)S(1)} collective-permute-done((bf16[64,512]{1,0:T(8,128)(2,1)S(1)}, bf16[64,512]{1,0:T(8,128)(2,1)S(1)}, u32[]{:S(2)}, u32[]{:S(2)}) %collective-permute-start.28) | collective-permute-done | bytes 65568 | tf_op jit(solution)/shard_map/ppermute | solution.py:456
  103.3 3.8 %collective-permute-start.29 = (bf16[64,512]{1,0:T(8,128)(2,1)S(1)}, bf16[64,512]{1,0:T(8,128)(2,1)S(1)}, u32[]{:S(2)}, u32[]{:S(2)}) collective-permute-start(bf16[64,512]{1,0:T(8,128)(2,1)S(1)} %add_convert_fusion.10), channel_id=1, source_target_pairs={{0,16},{1,17},{2,18},{3,19},{4,20},{5,21},{6,22},{7,23},{8,24},{9,... | collective-permute-start | bytes 196616 | tf_op jit(solution)/shard_map/ppermute | solution.py:456
  107.2 0.4 collective-permute-start.14
  107.6 0.6 collective-permute-start.18
  108.2 2.2 %collective-permute-done.29 = bf16[64,512]{1,0:T(8,128)(2,1)S(1)} collective-permute-done((bf16[64,512]{1,0:T(8,128)(2,1)S(1)}, bf16[64,512]{1,0:T(8,128)(2,1)S(1)}, u32[]{:S(2)}, u32[]{:S(2)}) %collective-permute-start.29) | collective-permute-done | bytes 65568 | tf_op jit(solution)/shard_map/ppermute | solution.py:456
  110.5 1.3 collective-permute-start.32
  112.1 0.8 collective-permute-start.30
  112.9 2.9 %collective-permute-done.14 = bf16[256,640]{1,0:T(8,128)(2,1)S(1)} collective-permute-done((bf16[256,640]{1,0:T(8,128)(2,1)S(1)}, bf16[256,640]{1,0:T(8,128)(2,1)S(1)}, u32[]{:S(2)}, u32[]{:S(2)}) %collective-permute-start.14) | collective-permute-done | bytes 327712 | tf_op jit(solution)/shard_map/ppermute | solution.py:456
  116.0 0.4 collective-permute-start.15
  116.7 0.7 collective-permute-done.30
  117.5 1.6 %collective-permute-start.35 = (bf16[256,512]{1,0:T(8,128)(2,1)S(1)}, bf16[256,512]{1,0:T(8,128)(2,1)S(1)}, u32[]{:S(2)}, u32[]{:S(2)}) collective-permute-start(bf16[256,512]{1,0:T(8,128)(2,1)S(1)} %pad_maximum_fusion.4.refs_0_), channel_id=1, source_target_pairs={{0,192},{1,193},{2,194},{3,195},{4,196},{5,197},{6,198},{7,199},{8... | collective-permute-start | bytes 786440 | tf_op jit(solution)/shard_map/ppermute | solution.py:456
  119.1 0.8 collective-permute-start.34
  119.9 5.3 %collective-permute-done.35.refs_3_ = bf16[256,512]{1,0:T(8,128)(2,1)S(1)} collective-permute-done((bf16[256,512]{1,0:T(8,128)(2,1)S(1)}, bf16[256,512]{1,0:T(8,128)(2,1)S(1)}, u32[]{:S(2)}, u32[]{:S(2)}) %collective-permute-start.35) | collective-permute-done | bytes 262176 | tf_op jit(solution)/shard_map/ppermute | solution.py:456
  125.2 8.3 %collective-permute-start.36 = (bf16[256,512]{1,0:T(8,128)(2,1)S(1)}, bf16[256,512]{1,0:T(8,128)(2,1)S(1)}, u32[]{:S(2)}, u32[]{:S(2)}) collective-permute-start(bf16[256,512]{1,0:T(8,128)(2,1)S(1)} %pad_maximum_fusion.4.refs_0_), channel_id=1, source_target_pairs={{0,1},{1,0},{2,3},{3,2},{4,5},{5,4},{6,7},{7,6},{8,9},{9,8},{10,11... | collective-permute-start | bytes 786440 | tf_op jit(solution)/shard_map/ppermute | solution.py:456
  133.5 1.2 collective-permute-start.39
  134.7 2.7 %collective-permute-start.38 = (bf16[256,512]{1,0:T(8,128)(2,1)S(1)}, bf16[256,512]{1,0:T(8,128)(2,1)S(1)}, u32[]{:S(2)}, u32[]{:S(2)}) collective-permute-start(bf16[256,512]{1,0:T(8,128)(2,1)S(1)} %collective-permute-done.34.refs_2_), channel_id=1, source_target_pairs={{0,1},{1,0},{2,3},{3,2},{4,5},{5,4},{6,7},{7,6},{8,9},{9,8},{10,11... | collective-permute-start | bytes 786440 | tf_op jit(solution)/shard_map/ppermute | solution.py:456
  137.5 0.6 collective-permute-start.16
  138.1 0.5 collective-permute-done.38.refs_6_
  139.2 2.6 %outputs.1 = (bf16[128,1024]{1,0:T(8,128)(2,1)}, bf16[128,512]{1,0:T(8,128)(2,1)}, bf16[128,512]{1,0:T(8,128)(2,1)}, bf16[64,128]{1,0:T(8,128)(2,1)}, f32[8,128,512]{2,1,0:T(8,128)}, /*index=5*/f32[8,512,128]{2,1,0:T(8,128)}) custom-call(s32[1]{0:T(128)} %bitcast.dp_ref.refs_1_, s32[1]{0:T(128)} %bitcast.1.ctx_ref.refs_2_, ...), custom_call_target="tpu_custom_call" | custom-call | tf_op jit(solution)/shard_map/outputs/pallas_call | solution.py:427
  (72 shorter events, 3.3 us)
Async XLA Ops:
  2.3 10.2 %collective-permute-start.1 = (bf16[128,640]{1,0:T(8,128)(2,1)}, bf16[128,640]{1,0:T(8,128)(2,1)S(1)}, u32[]{:S(2)}, u32[]{:S(2)}) collective-permute-start(bf16[128,640]{1,0:T(8,128)(2,1)} %key_rows.1.refs_7_), channel_id=1, source_target_pairs={{0,28},{1,29},{2,30},{3,31},{4,0},{5,1},{6,2},{7,3},{8,4},{9,5},{1... | collective-permute-start | bytes 491528 | tf_op jit(solution)/shard_map/ppermute | solution.py:456
  8.7 6.2 %collective-permute-start = (bf16[128,640]{1,0:T(8,128)(2,1)}, bf16[128,640]{1,0:T(8,128)(2,1)S(1)}, u32[]{:S(2)}, u32[]{:S(2)}) collective-permute-start(bf16[128,640]{1,0:T(8,128)(2,1)} %key_rows.1.refs_7_), channel_id=1, source_target_pairs={{0,4},{1,5},{2,6},{3,7},{4,8},{5,9},{6,10},{7,11},{8,12},{9,13},{1... | collective-permute-start | bytes 491528 | tf_op jit(solution)/shard_map/ppermute | solution.py:456
  8.7 29.6 %copy-start = (bf16[128,640]{1,0:T(8,128)(2,1)S(1)}, bf16[128,640]{1,0:T(8,128)(2,1)}, u32[]{:S(2)}) copy-start(bf16[128,640]{1,0:T(8,128)(2,1)} %key_rows.1.refs_7_) | copy-start | bytes 491524
  8.7 29.6 %copy-start.1 = (bf16[8,512,128]{2,1,0:T(8,128)(2,1)S(1)}, bf16[8,512,128]{2,1,0:T(8,128)(2,1)}, u32[]{:S(2)}) copy-start(bf16[8,512,128]{2,1,0:T(8,128)(2,1)} %refs_17_.1) | copy-start | bytes 3145732
  8.7 29.7 %copy-start.2 = (bf16[8,128,512]{2,1,0:T(8,128)(2,1)S(1)}, bf16[8,128,512]{2,1,0:T(8,128)(2,1)}, u32[]{:S(2)}) copy-start(bf16[8,128,512]{2,1,0:T(8,128)(2,1)} %refs_16_.1) | copy-start | bytes 3145732
  8.7 29.7 %copy-start.4 = (s32[1,64]{1,0:T(1,128)S(1)}, s32[1,64]{1,0:T(1,128)}, u32[]{:S(2)}) copy-start(s32[1,64]{1,0:T(1,128)} %refs_0_.1) | copy-start | bytes 772
  14.9 15.3 %collective-permute-start.2 = (bf16[128,2688]{1,0:T(8,128)(2,1)}, bf16[128,2688]{1,0:T(8,128)(2,1)S(1)}, u32[]{:S(2)}, u32[]{:S(2)}) collective-permute-start(bf16[128,2688]{1,0:T(8,128)(2,1)} %get-tuple-element.34.refs_3_), channel_id=1, source_target_pairs={{0,2},{1,3},{2,0},{3,1},{4,6},{5,7},{6,4},{7,5},{8,10},{9,11},{10,... | collective-permute-start | bytes 2064392 | tf_op jit(solution)/shard_map/ppermute | solution.py:456
  16.1 5.4 %collective-permute-start.3 = (bf16[128,640]{1,0:T(8,128)(2,1)S(1)}, bf16[128,640]{1,0:T(8,128)(2,1)S(1)}, u32[]{:S(2)}, u32[]{:S(2)}) collective-permute-start(bf16[128,640]{1,0:T(8,128)(2,1)S(1)} %collective-permute-done.refs_8_), channel_id=1, source_target_pairs={{0,4},{1,5},{2,6},{3,7},{4,8},{5,9},{6,10},{7,11},{8,12},{9,13},{1... | collective-permute-start | bytes 491528 | tf_op jit(solution)/shard_map/ppermute | solution.py:456
  16.1 5.4 %collective-permute-start.4 = (bf16[128,640]{1,0:T(8,128)(2,1)S(1)}, bf16[128,640]{1,0:T(8,128)(2,1)S(1)}, u32[]{:S(2)}, u32[]{:S(2)}) collective-permute-start(bf16[128,640]{1,0:T(8,128)(2,1)S(1)} %collective-permute-done.1.refs_9_), channel_id=1, source_target_pairs={{0,28},{1,29},{2,30},{3,31},{4,0},{5,1},{6,2},{7,3},{8,4},{9,5},{1... | collective-permute-start | bytes 491528 | tf_op jit(solution)/shard_map/ppermute | solution.py:456
  21.5 6.5 %collective-permute-start.5 = (bf16[128,640]{1,0:T(8,128)(2,1)S(1)}, bf16[128,640]{1,0:T(8,128)(2,1)S(1)}, u32[]{:S(2)}, u32[]{:S(2)}) collective-permute-start(bf16[128,640]{1,0:T(8,128)(2,1)S(1)} %collective-permute-done.3.refs_10_), channel_id=1, source_target_pairs={{0,4},{1,5},{2,6},{3,7},{4,8},{5,9},{6,10},{7,11},{8,12},{9,13},{1... | collective-permute-start | bytes 491528 | tf_op jit(solution)/shard_map/ppermute | solution.py:456
  21.5 6.5 %collective-permute-start.6 = (bf16[128,640]{1,0:T(8,128)(2,1)S(1)}, bf16[128,640]{1,0:T(8,128)(2,1)S(1)}, u32[]{:S(2)}, u32[]{:S(2)}) collective-permute-start(bf16[128,640]{1,0:T(8,128)(2,1)S(1)} %collective-permute-done.4.refs_11_), channel_id=1, source_target_pairs={{0,28},{1,29},{2,30},{3,31},{4,0},{5,1},{6,2},{7,3},{8,4},{9,5},{1... | collective-permute-start | bytes 491528 | tf_op jit(solution)/shard_map/ppermute | solution.py:456
  24.2 14.2 %collective-permute-start.7 = (bf16[128,2688]{1,0:T(8,128)(2,1)}, bf16[128,2688]{1,0:T(8,128)(2,1)S(1)}, u32[]{:S(2)}, u32[]{:S(2)}) collective-permute-start(bf16[128,2688]{1,0:T(8,128)(2,1)} %get-tuple-element.34.refs_3_), channel_id=1, source_target_pairs={{0,1},{1,0},{2,3},{3,2},{4,5},{5,4},{6,7},{7,6},{8,9},{9,8},{10,11... | collective-permute-start | bytes 2064392 | tf_op jit(solution)/shard_map/ppermute | solution.py:456
  30.2 8.2 %collective-permute-start.8 = (bf16[128,2688]{1,0:T(8,128)(2,1)S(1)}, bf16[128,2688]{1,0:T(8,128)(2,1)S(1)}, u32[]{:S(2)}, u32[]{:S(2)}) collective-permute-start(bf16[128,2688]{1,0:T(8,128)(2,1)S(1)} %collective-permute-done.2.refs_4_), channel_id=1, source_target_pairs={{0,1},{1,0},{2,3},{3,2},{4,5},{5,4},{6,7},{7,6},{8,9},{9,8},{10,11... | collective-permute-start | bytes 2064392 | tf_op jit(solution)/shard_map/ppermute | solution.py:456
  33.0 5.4 %collective-permute-start.9 = (bf16[64,640]{1,0:T(8,128)(2,1)S(1)}, bf16[64,640]{1,0:T(8,128)(2,1)S(1)}, u32[]{:S(2)}, u32[]{:S(2)}) collective-permute-start(bf16[64,640]{1,0:T(8,128)(2,1)S(1)} %slice.78), channel_id=1, source_target_pairs={{0,4},{1,5},{2,6},{3,7},{4,8},{5,9},{6,10},{7,11},{8,12},{9,13},{1... | collective-permute-start | bytes 245768 | tf_op jit(solution)/shard_map/ppermute | solution.py:456
  33.1 5.3 %collective-permute-start.10 = (bf16[64,640]{1,0:T(8,128)(2,1)S(1)}, bf16[64,640]{1,0:T(8,128)(2,1)S(1)}, u32[]{:S(2)}, u32[]{:S(2)}) collective-permute-start(bf16[64,640]{1,0:T(8,128)(2,1)S(1)} %slice.79), channel_id=1, source_target_pairs={{0,28},{1,29},{2,30},{3,31},{4,0},{5,1},{6,2},{7,3},{8,4},{9,5},{1... | collective-permute-start | bytes 245768 | tf_op jit(solution)/shard_map/ppermute | solution.py:456
  35.7 34.4 %collective-permute-start.20 = (bf16[4,128,512]{2,1,0:T(8,128)(2,1)}, bf16[4,128,512]{2,1,0:T(8,128)(2,1)S(1)}, u32[]{:S(2)}, u32[]{:S(2)}) collective-permute-start(bf16[4,128,512]{2,1,0:T(8,128)(2,1)} %get-tuple-element.53), channel_id=1, source_target_pairs={{0,1},{1,0},{2,3},{3,2},{4,5},{5,4},{6,7},{7,6},{8,9},{9,8},{10,11... | collective-permute-start | bytes 1572872 | tf_op jit(solution)/shard_map/ppermute | solution.py:456
  38.4 1.1 copy-start.3
  39.5 30.6 %copy-start.5 = (bf16[4,128,512]{2,1,0:T(8,128)(2,1)S(1)}, bf16[4,128,512]{2,1,0:T(8,128)(2,1)}, u32[]{:S(2)}) copy-start(bf16[4,128,512]{2,1,0:T(8,128)(2,1)} %get-tuple-element.52) | copy-start | bytes 1572868
  69.2 2.4 %collective-permute-start.19 = (bf16[4,128,512]{2,1,0:T(8,128)(2,1)S(1)}, bf16[4,128,512]{2,1,0:T(8,128)(2,1)S(1)}, u32[]{:S(2)}, u32[]{:S(2)}) collective-permute-start(bf16[4,128,512]{2,1,0:T(8,128)(2,1)S(1)} %get-tuple-element.51), channel_id=1, source_target_pairs={{0,1},{1,0},{2,3},{3,2},{4,5},{5,4},{6,7},{7,6},{8,9},{9,8},{10,11... | collective-permute-start | bytes 1572872 | tf_op jit(solution)/shard_map/ppermute | solution.py:456
  70.0 5.8 %collective-permute-start.11 = (bf16[448,640]{1,0:T(8,128)(2,1)S(1)}, bf16[448,640]{1,0:T(8,128)(2,1)S(1)}, u32[]{:S(2)}, u32[]{:S(2)}) collective-permute-start(bf16[448,640]{1,0:T(8,128)(2,1)S(1)} %get-tuple-element.47), channel_id=1, source_target_pairs={{0,1},{1,0},{2,3},{3,2},{4,5},{5,4},{6,7},{7,6},{8,9},{9,8},{10,11... | collective-permute-start | bytes 1720328 | tf_op jit(solution)/shard_map/ppermute | solution.py:456
  70.3 28.3 %collective-permute-start.17 = (bf16[2,128,1536]{2,1,0:T(8,128)(2,1)S(1)}, bf16[2,128,1536]{2,1,0:T(8,128)(2,1)S(1)}, u32[]{:S(2)}, u32[]{:S(2)}) collective-permute-start(bf16[2,128,1536]{2,1,0:T(8,128)(2,1)S(1)} %get-tuple-element.49), channel_id=1, source_target_pairs={{0,1},{1,0},{2,3},{3,2},{4,5},{5,4},{6,7},{7,6},{8,9},{9,8},{10,11... | collective-permute-start | bytes 2359304 | tf_op jit(solution)/shard_map/ppermute | solution.py:456
  71.8 8.8 %collective-permute-start.21 = (bf16[4,64,512]{2,1,0:T(8,128)(2,1)S(1)}, bf16[4,64,512]{2,1,0:T(8,128)(2,1)S(1)}, u32[]{:S(2)}, u32[]{:S(2)}) collective-permute-start(bf16[4,64,512]{2,1,0:T(8,128)(2,1)S(1)} %get-tuple-element.60), channel_id=1, source_target_pairs={{0,64},{1,65},{2,66},{3,67},{4,68},{5,69},{6,70},{7,71},{8,72},{9,... | collective-permute-start | bytes 786440 | tf_op jit(solution)/shard_map/ppermute | solution.py:456
  71.9 8.7 %collective-permute-start.23 = (bf16[4,64,512]{2,1,0:T(8,128)(2,1)S(1)}, bf16[4,64,512]{2,1,0:T(8,128)(2,1)S(1)}, u32[]{:S(2)}, u32[]{:S(2)}) collective-permute-start(bf16[4,64,512]{2,1,0:T(8,128)(2,1)S(1)} %get-tuple-element.61), channel_id=1, source_target_pairs={{0,192},{1,193},{2,194},{3,195},{4,196},{5,197},{6,198},{7,199},{8... | collective-permute-start | bytes 786440 | tf_op jit(solution)/shard_map/ppermute | solution.py:456
  74.5 11.9 %collective-permute-start.22 = (bf16[4,64,512]{2,1,0:T(8,128)(2,1)S(1)}, bf16[4,64,512]{2,1,0:T(8,128)(2,1)S(1)}, u32[]{:S(2)}, u32[]{:S(2)}) collective-permute-start(bf16[4,64,512]{2,1,0:T(8,128)(2,1)S(1)} %get-tuple-element.62), channel_id=1, source_target_pairs={{0,128},{1,129},{2,130},{3,131},{4,132},{5,133},{6,134},{7,135},{8... | collective-permute-start | bytes 786440 | tf_op jit(solution)/shard_map/ppermute | solution.py:456
  75.9 15.9 %collective-permute-start.12 = (bf16[128,640]{1,0:T(8,128)(2,1)S(1)}, bf16[128,640]{1,0:T(8,128)(2,1)S(1)}, u32[]{:S(2)}, u32[]{:S(2)}) collective-permute-start(bf16[128,640]{1,0:T(8,128)(2,1)S(1)} %pad_maximum_fusion.5), channel_id=1, source_target_pairs={{0,4},{1,29},{2,6},{3,31},{4,8},{5,1},{6,10},{7,3},{8,12},{9,5},{1... | collective-permute-start | bytes 491528 | tf_op jit(solution)/shard_map/ppermute | solution.py:456
  86.6 5.2 %collective-permute-start.24 = (bf16[64,512]{1,0:T(8,128)(2,1)S(1)}, bf16[64,512]{1,0:T(8,128)(2,1)S(1)}, u32[]{:S(2)}, u32[]{:S(2)}) collective-permute-start(bf16[64,512]{1,0:T(8,128)(2,1)S(1)} %get-tuple-element.69), channel_id=1, source_target_pairs={{0,2},{1,3},{2,32},{3,33},{4,6},{5,7},{6,36},{7,37},{8,10},{9,11},... | collective-permute-start | bytes 196616 | tf_op jit(solution)/shard_map/ppermute | solution.py:456
  87.8 4.0 %collective-permute-start.26 = (bf16[64,512]{1,0:T(8,128)(2,1)S(1)}, bf16[64,512]{1,0:T(8,128)(2,1)S(1)}, u32[]{:S(2)}, u32[]{:S(2)}) collective-permute-start(bf16[64,512]{1,0:T(8,128)(2,1)S(1)} %get-tuple-element.70), channel_id=1, source_target_pairs={{0,34},{1,35},{2,0},{3,1},{4,38},{5,39},{6,4},{7,5},{8,42},{9,43},... | collective-permute-start | bytes 196616 | tf_op jit(solution)/shard_map/ppermute | solution.py:456
  90.3 4.6 %collective-permute-start.25 = (bf16[64,512]{1,0:T(8,128)(2,1)S(1)}, bf16[64,512]{1,0:T(8,128)(2,1)S(1)}, u32[]{:S(2)}, u32[]{:S(2)}) collective-permute-start(bf16[64,512]{1,0:T(8,128)(2,1)S(1)} %get-tuple-element.71), channel_id=1, source_target_pairs={{0,32},{1,33},{2,34},{3,35},{4,36},{5,37},{6,38},{7,39},{8,40},{9,... | collective-permute-start | bytes 196616 | tf_op jit(solution)/shard_map/ppermute | solution.py:456
  95.0 3.3 %collective-permute-start.27 = (bf16[64,512]{1,0:T(8,128)(2,1)S(1)}, bf16[64,512]{1,0:T(8,128)(2,1)S(1)}, u32[]{:S(2)}, u32[]{:S(2)}) collective-permute-start(bf16[64,512]{1,0:T(8,128)(2,1)S(1)} %fusion.12), channel_id=1, source_target_pairs={{0,4},{1,5},{2,6},{3,7},{4,0},{5,1},{6,2},{7,3},{8,12},{9,13},{10,... | collective-permute-start | bytes 196616 | tf_op jit(solution)/shard_map/ppermute | solution.py:456
  95.1 12.0 %collective-permute-start.13 = (bf16[256,640]{1,0:T(8,128)(2,1)S(1)}, bf16[256,640]{1,0:T(8,128)(2,1)S(1)}, u32[]{:S(2)}, u32[]{:S(2)}) collective-permute-start(bf16[256,640]{1,0:T(8,128)(2,1)S(1)} %pad_maximum_fusion), channel_id=1, source_target_pairs={{0,4},{1,29},{2,6},{3,31},{4,8},{5,1},{6,10},{7,3},{8,12},{9,5},{1... | collective-permute-start | bytes 983048 | tf_op jit(solution)/shard_map/ppermute | solution.py:456
  98.3 5.0 %collective-permute-start.28 = (bf16[64,512]{1,0:T(8,128)(2,1)S(1)}, bf16[64,512]{1,0:T(8,128)(2,1)S(1)}, u32[]{:S(2)}, u32[]{:S(2)}) collective-permute-start(bf16[64,512]{1,0:T(8,128)(2,1)S(1)} %add_convert_fusion.11), channel_id=1, source_target_pairs={{0,8},{1,9},{2,10},{3,11},{4,12},{5,13},{6,14},{7,15},{8,0},{9,1},... | collective-permute-start | bytes 196616 | tf_op jit(solution)/shard_map/ppermute | solution.py:456
  103.3 7.2 %collective-permute-start.29 = (bf16[64,512]{1,0:T(8,128)(2,1)S(1)}, bf16[64,512]{1,0:T(8,128)(2,1)S(1)}, u32[]{:S(2)}, u32[]{:S(2)}) collective-permute-start(bf16[64,512]{1,0:T(8,128)(2,1)S(1)} %add_convert_fusion.10), channel_id=1, source_target_pairs={{0,16},{1,17},{2,18},{3,19},{4,20},{5,21},{6,22},{7,23},{8,24},{9,... | collective-permute-start | bytes 196616 | tf_op jit(solution)/shard_map/ppermute | solution.py:456
  107.2 8.6 %collective-permute-start.14 = (bf16[256,640]{1,0:T(8,128)(2,1)S(1)}, bf16[256,640]{1,0:T(8,128)(2,1)S(1)}, u32[]{:S(2)}, u32[]{:S(2)}) collective-permute-start(bf16[256,640]{1,0:T(8,128)(2,1)S(1)} %pad_maximum_fusion.1), channel_id=1, source_target_pairs={{0,4},{1,29},{2,6},{3,31},{4,8},{5,1},{6,10},{7,3},{8,12},{9,5},{1... | collective-permute-start | bytes 983048 | tf_op jit(solution)/shard_map/ppermute | solution.py:456
  107.6 29.8 %collective-permute-start.18 = (bf16[128,1536]{1,0:T(8,128)(2,1)S(1)}, bf16[128,1536]{1,0:T(8,128)(2,1)S(1)}, u32[]{:S(2)}, u32[]{:S(2)}) collective-permute-start(bf16[128,1536]{1,0:T(8,128)(2,1)S(1)} %slice_bitcast_fusion), channel_id=1, source_target_pairs={{0,2},{1,3},{2,0},{3,1},{4,6},{5,7},{6,4},{7,5},{8,10},{9,11},{10,... | collective-permute-start | bytes 1179656 | tf_op jit(solution)/shard_map/ppermute | solution.py:456
  110.5 5.9 %collective-permute-start.32 = (bf16[64,512]{1,0:T(8,128)(2,1)S(1)}, bf16[64,512]{1,0:T(8,128)(2,1)S(1)}, u32[]{:S(2)}, u32[]{:S(2)}) collective-permute-start(bf16[64,512]{1,0:T(8,128)(2,1)S(1)} %add_convert_fusion.9), channel_id=1, source_target_pairs={{0,34},{1,35},{2,0},{3,1},{4,38},{5,39},{6,4},{7,5},{8,42},{9,43},... | collective-permute-start | bytes 196616 | tf_op jit(solution)/shard_map/ppermute | solution.py:456
  111.8 4.9 %collective-permute-start.31 = (bf16[64,512]{1,0:T(8,128)(2,1)S(1)}, bf16[64,512]{1,0:T(8,128)(2,1)S(1)}, u32[]{:S(2)}, u32[]{:S(2)}) collective-permute-start(bf16[64,512]{1,0:T(8,128)(2,1)S(1)} %add_convert_fusion.9), channel_id=1, source_target_pairs={{0,32},{1,33},{2,34},{3,35},{4,36},{5,37},{6,38},{7,39},{8,40},{9,... | collective-permute-start | bytes 196616 | tf_op jit(solution)/shard_map/ppermute | solution.py:456
  112.1 5.3 %collective-permute-start.30 = (bf16[64,512]{1,0:T(8,128)(2,1)S(1)}, bf16[64,512]{1,0:T(8,128)(2,1)S(1)}, u32[]{:S(2)}, u32[]{:S(2)}) collective-permute-start(bf16[64,512]{1,0:T(8,128)(2,1)S(1)} %add_convert_fusion.9), channel_id=1, source_target_pairs={{0,2},{1,3},{2,32},{3,33},{4,6},{5,7},{6,36},{7,37},{8,10},{9,11},... | collective-permute-start | bytes 196616 | tf_op jit(solution)/shard_map/ppermute | solution.py:456
  116.0 21.5 %collective-permute-start.15 = (bf16[256,640]{1,0:T(8,128)(2,1)S(1)}, bf16[256,640]{1,0:T(8,128)(2,1)S(1)}, u32[]{:S(2)}, u32[]{:S(2)}) collective-permute-start(bf16[256,640]{1,0:T(8,128)(2,1)S(1)} %pad_maximum_fusion.2), channel_id=1, source_target_pairs={{0,4},{1,29},{2,6},{3,31},{4,8},{5,1},{6,10},{7,3},{8,12},{9,5},{1... | collective-permute-start | bytes 983048 | tf_op jit(solution)/shard_map/ppermute | solution.py:456
  117.5 7.7 %collective-permute-start.35 = (bf16[256,512]{1,0:T(8,128)(2,1)S(1)}, bf16[256,512]{1,0:T(8,128)(2,1)S(1)}, u32[]{:S(2)}, u32[]{:S(2)}) collective-permute-start(bf16[256,512]{1,0:T(8,128)(2,1)S(1)} %pad_maximum_fusion.4.refs_0_), channel_id=1, source_target_pairs={{0,192},{1,193},{2,194},{3,195},{4,196},{5,197},{6,198},{7,199},{8... | collective-permute-start | bytes 786440 | tf_op jit(solution)/shard_map/ppermute | solution.py:456
  119.1 14.4 %collective-permute-start.34 = (bf16[256,512]{1,0:T(8,128)(2,1)S(1)}, bf16[256,512]{1,0:T(8,128)(2,1)S(1)}, u32[]{:S(2)}, u32[]{:S(2)}) collective-permute-start(bf16[256,512]{1,0:T(8,128)(2,1)S(1)} %pad_maximum_fusion.4.refs_0_), channel_id=1, source_target_pairs={{0,128},{1,129},{2,130},{3,131},{4,132},{5,133},{6,134},{7,135},{8... | collective-permute-start | bytes 786440 | tf_op jit(solution)/shard_map/ppermute | solution.py:456
  119.9 14.9 %collective-permute-start.33 = (bf16[256,512]{1,0:T(8,128)(2,1)S(1)}, bf16[256,512]{1,0:T(8,128)(2,1)S(1)}, u32[]{:S(2)}, u32[]{:S(2)}) collective-permute-start(bf16[256,512]{1,0:T(8,128)(2,1)S(1)} %pad_maximum_fusion.4.refs_0_), channel_id=1, source_target_pairs={{0,64},{1,65},{2,66},{3,67},{4,68},{5,69},{6,70},{7,71},{8,72},{9,... | collective-permute-start | bytes 786440 | tf_op jit(solution)/shard_map/ppermute | solution.py:456
  125.2 12.9 %collective-permute-start.36 = (bf16[256,512]{1,0:T(8,128)(2,1)S(1)}, bf16[256,512]{1,0:T(8,128)(2,1)S(1)}, u32[]{:S(2)}, u32[]{:S(2)}) collective-permute-start(bf16[256,512]{1,0:T(8,128)(2,1)S(1)} %pad_maximum_fusion.4.refs_0_), channel_id=1, source_target_pairs={{0,1},{1,0},{2,3},{3,2},{4,5},{5,4},{6,7},{7,6},{8,9},{9,8},{10,11... | collective-permute-start | bytes 786440 | tf_op jit(solution)/shard_map/ppermute | solution.py:456
  133.5 4.6 %collective-permute-start.39 = (bf16[256,512]{1,0:T(8,128)(2,1)S(1)}, bf16[256,512]{1,0:T(8,128)(2,1)S(1)}, u32[]{:S(2)}, u32[]{:S(2)}) collective-permute-start(bf16[256,512]{1,0:T(8,128)(2,1)S(1)} %collective-permute-done.35.refs_3_), channel_id=1, source_target_pairs={{0,1},{1,0},{2,3},{3,2},{4,5},{5,4},{6,7},{7,6},{8,9},{9,8},{10,11... | collective-permute-start | bytes 786440 | tf_op jit(solution)/shard_map/ppermute | solution.py:456
  134.7 3.9 %collective-permute-start.38 = (bf16[256,512]{1,0:T(8,128)(2,1)S(1)}, bf16[256,512]{1,0:T(8,128)(2,1)S(1)}, u32[]{:S(2)}, u32[]{:S(2)}) collective-permute-start(bf16[256,512]{1,0:T(8,128)(2,1)S(1)} %collective-permute-done.34.refs_2_), channel_id=1, source_target_pairs={{0,1},{1,0},{2,3},{3,2},{4,5},{5,4},{6,7},{7,6},{8,9},{9,8},{10,11... | collective-permute-start | bytes 786440 | tf_op jit(solution)/shard_map/ppermute | solution.py:456
  137.4 1.5 %collective-permute-start.37 = (bf16[256,512]{1,0:T(8,128)(2,1)S(1)}, bf16[256,512]{1,0:T(8,128)(2,1)S(1)}, u32[]{:S(2)}, u32[]{:S(2)}) collective-permute-start(bf16[256,512]{1,0:T(8,128)(2,1)S(1)} %collective-permute-done.33.refs_1_), channel_id=1, source_target_pairs={{0,1},{1,0},{2,3},{3,2},{4,5},{5,4},{6,7},{7,6},{8,9},{9,8},{10,11... | collective-permute-start | bytes 786440 | tf_op jit(solution)/shard_map/ppermute | solution.py:456
  137.5 1.7 %collective-permute-start.16 = (bf16[128,640]{1,0:T(8,128)(2,1)S(1)}, bf16[128,640]{1,0:T(8,128)(2,1)S(1)}, u32[]{:S(2)}, u32[]{:S(2)}) collective-permute-start(bf16[128,640]{1,0:T(8,128)(2,1)S(1)} %slice.114), channel_id=1, source_target_pairs={{0,1},{1,0},{2,3},{3,2},{4,5},{5,4},{6,7},{7,6},{8,9},{9,8},{10,11... | collective-permute-start | bytes 491528 | tf_op jit(solution)/shard_map/ppermute | solution.py:456

commit v3 on v2

--- a/solution.py
+++ b/solution.py
@@ -98,7 +98,7 @@
         in_specs=[SMEM, SMEM] + [VMEM] * 6,
         out_specs=(VMEM,) * (1 + nc),
         out_shape=(
-            jax.ShapeDtypeStruct((rows, qn.shape[1] + qr.shape[1] + do.shape[1] + 128), BF),
+            pltpu.VMEM((rows, qn.shape[1] + qr.shape[1] + do.shape[1] + 128), BF),
         )
         + (jax.ShapeDtypeStruct((heads // nc, hd, dc), BF),) * nc,
         compiler_params=vmem(60),

time: 142 us -> 141 us (level)
  transfers between devices with their start and end apart: 40 -> 40, of which waited for: 17 -> 19; matrix products, arithmetic and copies ran while one was open for 1% -> 1% of each run, Pallas kernels for 24% -> 24%
where the time goes in v3:
time: 141 us
  starting transfers between devices  63.1 us (45%)
  Pallas kernels  37.7 us (27%)
  waiting for transfers between devices  37.7 us (27%)
    ppermute x40, starting transfers between devices, all_perm(): return lax.ppermute(x, ('dp', 'ctx'), pairs)  63.1 us
    ppermute x40, waiting for transfers between devices, all_perm(): return lax.ppermute(x, ('dp', 'ctx'), pairs)  37.7 us
    pallas_call x1, Pallas kernels, attn_call(): pl.pallas_call(functools.partial(attn_kernel, grid, na, heads, ids.shape[...  29.7 us
    pallas_call x1, Pallas kernels, own_call(): pl.pallas_call(functools.partial(own_kernel, grid), in_specs=[SMEM, SMEM]...  3.66 us
  transfers between devices with their start and end apart: 40, of which 19 were waited for; matrix products, arithmetic and copies ran while one was open for 1% of the time, Pallas kernels for 24%

profile of v3, /device:TPU:1, one launch (start us, length us, event | category | flops | bytes accessed | tf_op | source)
XLA Modules:
  0.0 140.5 jit_solution(4701634937472661994)
XLA Ops:
  0.6 1.7 %key_rows.1.refs_7_ = bf16[128,640]{1,0:T(8,128)(2,1)} custom-call(bf16[128,512]{1,0:T(8,128)(2,1)} %bitcast.49, bf16[64,128]{1,0:T(8,128)(2,1)} %bitcast.50), custom_call_target="tpu_custom_call" | custom-call | tf_op jit(solution)/shard_map/key_rows/pallas_call | solution.py:118
  2.3 6.4 %collective-permute-start.1 = (bf16[128,640]{1,0:T(8,128)(2,1)}, bf16[128,640]{1,0:T(8,128)(2,1)S(1)}, u32[]{:S(2)}, u32[]{:S(2)}) collective-permute-start(bf16[128,640]{1,0:T(8,128)(2,1)} %key_rows.1.refs_7_), channel_id=1, source_target_pairs={{0,28},{1,29},{2,30},{3,31},{4,0},{5,1},{6,2},{7,3},{8,4},{9,5},{1... | collective-permute-start | bytes 491528 | tf_op jit(solution)/shard_map/ppermute | solution.py:456
  8.7 3.7 %own_rows.1 = (bf16[128,2688]{1,0:T(8,128)(2,1)S(1)}, bf16[4,128,512]{2,1,0:T(8,128)(2,1)}, bf16[4,128,512]{2,1,0:T(8,128)(2,1)}) custom-call(s32[1]{0:T(128)} %bitcast.dp_ref.refs_1_, s32[1]{0:T(128)} %bitcast.1.ctx_ref.refs_2_, bf16[128,1024]{1,0:T(8,128)(2,1)} %bitcast.52, bf16[128,512]{1,0:T(8,128)(2,1)} %bitcast.55, bf16[128,1024]{1,0:T(8,128)(2,1)} %bitcast.53, ...), custom_call_target="tpu_custom_call" | custom-call | flops 4000000000 | bytes 4000000 | tf_op jit(solution)/shard_map/own_rows/pallas_call | solution.py:96
  12.4 2.5 %collective-permute-done.refs_8_ = bf16[128,640]{1,0:T(8,128)(2,1)S(1)} collective-permute-done((bf16[128,640]{1,0:T(8,128)(2,1)}, bf16[128,640]{1,0:T(8,128)(2,1)S(1)}, u32[]{:S(2)}, u32[]{:S(2)}) %collective-permute-start) | collective-permute-done | bytes 163872 | tf_op jit(solution)/shard_map/ppermute | solution.py:456
  14.9 1.2 collective-permute-start.2
  16.1 2.7 %collective-permute-start.4 = (bf16[128,640]{1,0:T(8,128)(2,1)S(1)}, bf16[128,640]{1,0:T(8,128)(2,1)S(1)}, u32[]{:S(2)}, u32[]{:S(2)}) collective-permute-start(bf16[128,640]{1,0:T(8,128)(2,1)S(1)} %collective-permute-done.1.refs_9_), channel_id=1, source_target_pairs={{0,28},{1,29},{2,30},{3,31},{4,0},{5,1},{6,2},{7,3},{8,4},{9,5},{1... | collective-permute-start | bytes 491528 | tf_op jit(solution)/shard_map/ppermute | solution.py:456
  18.8 2.7 %collective-permute-done.3.refs_10_ = bf16[128,640]{1,0:T(8,128)(2,1)S(1)} collective-permute-done((bf16[128,640]{1,0:T(8,128)(2,1)S(1)}, bf16[128,640]{1,0:T(8,128)(2,1)S(1)}, u32[]{:S(2)}, u32[]{:S(2)}) %collective-permute-start.3) | collective-permute-done | bytes 163872 | tf_op jit(solution)/shard_map/ppermute | solution.py:456
  21.5 2.7 %collective-permute-start.6 = (bf16[128,640]{1,0:T(8,128)(2,1)S(1)}, bf16[128,640]{1,0:T(8,128)(2,1)S(1)}, u32[]{:S(2)}, u32[]{:S(2)}) collective-permute-start(bf16[128,640]{1,0:T(8,128)(2,1)S(1)} %collective-permute-done.4.refs_11_), channel_id=1, source_target_pairs={{0,28},{1,29},{2,30},{3,31},{4,0},{5,1},{6,2},{7,3},{8,4},{9,5},{1... | collective-permute-start | bytes 491528 | tf_op jit(solution)/shard_map/ppermute | solution.py:456
  24.2 3.9 %collective-permute-start.7 = (bf16[128,2688]{1,0:T(8,128)(2,1)S(1)}, bf16[128,2688]{1,0:T(8,128)(2,1)S(1)}, u32[]{:S(2)}, u32[]{:S(2)}) collective-permute-start(bf16[128,2688]{1,0:T(8,128)(2,1)S(1)} %get-tuple-element.34.refs_3_), channel_id=1, source_target_pairs={{0,1},{1,0},{2,3},{3,2},{4,5},{5,4},{6,7},{7,6},{8,9},{9,8},{10,11... | collective-permute-start | bytes 2064392 | tf_op jit(solution)/shard_map/ppermute | solution.py:456
  28.0 1.9 %collective-permute-done.2.refs_4_ = bf16[128,2688]{1,0:T(8,128)(2,1)S(1)} collective-permute-done((bf16[128,2688]{1,0:T(8,128)(2,1)S(1)}, bf16[128,2688]{1,0:T(8,128)(2,1)S(1)}, u32[]{:S(2)}, u32[]{:S(2)}) %collective-permute-start.2) | collective-permute-done | bytes 688160 | tf_op jit(solution)/shard_map/ppermute | solution.py:456
  29.9 2.8 %collective-permute-start.8 = (bf16[128,2688]{1,0:T(8,128)(2,1)S(1)}, bf16[128,2688]{1,0:T(8,128)(2,1)S(1)}, u32[]{:S(2)}, u32[]{:S(2)}) collective-permute-start(bf16[128,2688]{1,0:T(8,128)(2,1)S(1)} %collective-permute-done.2.refs_4_), channel_id=1, source_target_pairs={{0,1},{1,0},{2,3},{3,2},{4,5},{5,4},{6,7},{7,6},{8,9},{9,8},{10,11... | collective-permute-start | bytes 2064392 | tf_op jit(solution)/shard_map/ppermute | solution.py:456
  32.9 2.7 %collective-permute-start.10 = (bf16[64,640]{1,0:T(8,128)(2,1)S(1)}, bf16[64,640]{1,0:T(8,128)(2,1)S(1)}, u32[]{:S(2)}, u32[]{:S(2)}) collective-permute-start(bf16[64,640]{1,0:T(8,128)(2,1)S(1)} %slice.79), channel_id=1, source_target_pairs={{0,28},{1,29},{2,30},{3,31},{4,0},{5,1},{6,2},{7,3},{8,4},{9,5},{1... | collective-permute-start | bytes 245768 | tf_op jit(solution)/shard_map/ppermute | solution.py:456
  35.5 0.6 collective-permute-start.20
  36.1 2.0 %collective-permute-done.9.refs_14_ = bf16[64,640]{1,0:T(8,128)(2,1)S(1)} collective-permute-done((bf16[64,640]{1,0:T(8,128)(2,1)S(1)}, bf16[64,640]{1,0:T(8,128)(2,1)S(1)}, u32[]{:S(2)}, u32[]{:S(2)}) %collective-permute-start.9) | collective-permute-done | bytes 81952 | tf_op jit(solution)/shard_map/ppermute | solution.py:456
  38.2 29.7 %attn_grads.1 = (bf16[128,640]{1,0:T(8,128)(2,1)S(1)}, bf16[64,640]{1,0:T(8,128)(2,1)S(1)}, bf16[128,640]{1,0:T(8,128)(2,1)S(1)}, bf16[128,640]{1,0:T(8,128)(2,1...) custom-call(s32[1,64]{1,0:T(1,128)S(1)} %copy-done.3, ...), custom_call_target="tpu_custom_call" | custom-call | flops 30000001024 | bytes 10000000 | tf_op jit(solution)/shard_map/attn_grads/pallas_call | solution.py:348
  68.0 0.5 collective-permute-start.11
  68.8 1.0 collective-permute-done.19
  70.1 1.8 %collective-permute-start.21 = (bf16[4,64,512]{2,1,0:T(8,128)(2,1)S(1)}, bf16[4,64,512]{2,1,0:T(8,128)(2,1)S(1)}, u32[]{:S(2)}, u32[]{:S(2)}) collective-permute-start(bf16[4,64,512]{2,1,0:T(8,128)(2,1)S(1)} %get-tuple-element.60), channel_id=1, source_target_pairs={{0,64},{1,65},{2,66},{3,67},{4,68},{5,69},{6,70},{7,71},{8,72},{9,... | collective-permute-start | bytes 786440 | tf_op jit(solution)/shard_map/ppermute | solution.py:456
  71.8 1.0 collective-permute-start.23
  72.8 1.7 %collective-permute-start.22 = (bf16[4,64,512]{2,1,0:T(8,128)(2,1)S(1)}, bf16[4,64,512]{2,1,0:T(8,128)(2,1)S(1)}, u32[]{:S(2)}, u32[]{:S(2)}) collective-permute-start(bf16[4,64,512]{2,1,0:T(8,128)(2,1)S(1)} %get-tuple-element.62), channel_id=1, source_target_pairs={{0,128},{1,129},{2,130},{3,131},{4,132},{5,133},{6,134},{7,135},{8... | collective-permute-start | bytes 786440 | tf_op jit(solution)/shard_map/ppermute | solution.py:456
  74.6 3.1 %collective-permute-start.12 = (bf16[128,640]{1,0:T(8,128)(2,1)S(1)}, bf16[128,640]{1,0:T(8,128)(2,1)S(1)}, u32[]{:S(2)}, u32[]{:S(2)}) collective-permute-start(bf16[128,640]{1,0:T(8,128)(2,1)S(1)} %pad_maximum_fusion.5), channel_id=1, source_target_pairs={{0,4},{1,29},{2,6},{3,31},{4,8},{5,1},{6,10},{7,3},{8,12},{9,5},{1... | collective-permute-start | bytes 491528 | tf_op jit(solution)/shard_map/ppermute | solution.py:456
  77.7 1.4 %collective-permute-done.21 = bf16[4,64,512]{2,1,0:T(8,128)(2,1)S(1)} collective-permute-done((bf16[4,64,512]{2,1,0:T(8,128)(2,1)S(1)}, bf16[4,64,512]{2,1,0:T(8,128)(2,1)S(1)}, u32[]{:S(2)}, u32[]{:S(2)}) %collective-permute-start.21) | collective-permute-done | bytes 262176 | tf_op jit(solution)/shard_map/ppermute | solution.py:456
  79.1 5.9 %collective-permute-done.22 = bf16[4,64,512]{2,1,0:T(8,128)(2,1)S(1)} collective-permute-done((bf16[4,64,512]{2,1,0:T(8,128)(2,1)S(1)}, bf16[4,64,512]{2,1,0:T(8,128)(2,1)S(1)}, u32[]{:S(2)}, u32[]{:S(2)}) %collective-permute-start.22) | collective-permute-done | bytes 262176 | tf_op jit(solution)/shard_map/ppermute | solution.py:456
  85.2 2.4 %collective-permute-start.24 = (bf16[64,512]{1,0:T(8,128)(2,1)S(1)}, bf16[64,512]{1,0:T(8,128)(2,1)S(1)}, u32[]{:S(2)}, u32[]{:S(2)}) collective-permute-start(bf16[64,512]{1,0:T(8,128)(2,1)S(1)} %get-tuple-element.69), channel_id=1, source_target_pairs={{0,2},{1,3},{2,32},{3,33},{4,6},{5,7},{6,36},{7,37},{8,10},{9,11},... | collective-permute-start | bytes 196616 | tf_op jit(solution)/shard_map/ppermute | solution.py:456
  87.6 1.6 %collective-permute-start.26 = (bf16[64,512]{1,0:T(8,128)(2,1)S(1)}, bf16[64,512]{1,0:T(8,128)(2,1)S(1)}, u32[]{:S(2)}, u32[]{:S(2)}) collective-permute-start(bf16[64,512]{1,0:T(8,128)(2,1)S(1)} %get-tuple-element.70), channel_id=1, source_target_pairs={{0,34},{1,35},{2,0},{3,1},{4,38},{5,39},{6,4},{7,5},{8,42},{9,43},... | collective-permute-start | bytes 196616 | tf_op jit(solution)/shard_map/ppermute | solution.py:456
  89.2 0.9 collective-permute-start.25
  90.1 0.4 collective-permute-done.24
  90.8 3.3 %collective-permute-done.25 = bf16[64,512]{1,0:T(8,128)(2,1)S(1)} collective-permute-done((bf16[64,512]{1,0:T(8,128)(2,1)S(1)}, bf16[64,512]{1,0:T(8,128)(2,1)S(1)}, u32[]{:S(2)}, u32[]{:S(2)}) %collective-permute-start.25) | collective-permute-done | bytes 65568 | tf_op jit(solution)/shard_map/ppermute | solution.py:456
  94.3 2.8 %collective-permute-start.13 = (bf16[256,640]{1,0:T(8,128)(2,1)S(1)}, bf16[256,640]{1,0:T(8,128)(2,1)S(1)}, u32[]{:S(2)}, u32[]{:S(2)}) collective-permute-start(bf16[256,640]{1,0:T(8,128)(2,1)S(1)} %pad_maximum_fusion), channel_id=1, source_target_pairs={{0,4},{1,29},{2,6},{3,31},{4,8},{5,1},{6,10},{7,3},{8,12},{9,5},{1... | collective-permute-start | bytes 983048 | tf_op jit(solution)/shard_map/ppermute | solution.py:456
  97.3 0.8 collective-permute-start.28
  98.3 4.1 %collective-permute-done.28 = bf16[64,512]{1,0:T(8,128)(2,1)S(1)} collective-permute-done((bf16[64,512]{1,0:T(8,128)(2,1)S(1)}, bf16[64,512]{1,0:T(8,128)(2,1)S(1)}, u32[]{:S(2)}, u32[]{:S(2)}) %collective-permute-start.28) | collective-permute-done | bytes 65568 | tf_op jit(solution)/shard_map/ppermute | solution.py:456
  102.4 3.4 %collective-permute-start.29 = (bf16[64,512]{1,0:T(8,128)(2,1)S(1)}, bf16[64,512]{1,0:T(8,128)(2,1)S(1)}, u32[]{:S(2)}, u32[]{:S(2)}) collective-permute-start(bf16[64,512]{1,0:T(8,128)(2,1)S(1)} %add_convert_fusion.10), channel_id=1, source_target_pairs={{0,16},{1,17},{2,18},{3,19},{4,20},{5,21},{6,22},{7,23},{8,24},{9,... | collective-permute-start | bytes 196616 | tf_op jit(solution)/shard_map/ppermute | solution.py:456
  106.0 1.1 collective-permute-start.14
  107.2 2.4 %collective-permute-done.29 = bf16[64,512]{1,0:T(8,128)(2,1)S(1)} collective-permute-done((bf16[64,512]{1,0:T(8,128)(2,1)S(1)}, bf16[64,512]{1,0:T(8,128)(2,1)S(1)}, u32[]{:S(2)}, u32[]{:S(2)}) %collective-permute-start.29) | collective-permute-done | bytes 65568 | tf_op jit(solution)/shard_map/ppermute | solution.py:456
  109.7 1.6 %collective-permute-start.32 = (bf16[64,512]{1,0:T(8,128)(2,1)S(1)}, bf16[64,512]{1,0:T(8,128)(2,1)S(1)}, u32[]{:S(2)}, u32[]{:S(2)}) collective-permute-start(bf16[64,512]{1,0:T(8,128)(2,1)S(1)} %add_convert_fusion.9), channel_id=1, source_target_pairs={{0,34},{1,35},{2,0},{3,1},{4,38},{5,39},{6,4},{7,5},{8,42},{9,43},... | collective-permute-start | bytes 196616 | tf_op jit(solution)/shard_map/ppermute | solution.py:456
  111.2 0.7 collective-permute-start.30
  111.9 2.7 %collective-permute-done.14 = bf16[256,640]{1,0:T(8,128)(2,1)S(1)} collective-permute-done((bf16[256,640]{1,0:T(8,128)(2,1)S(1)}, bf16[256,640]{1,0:T(8,128)(2,1)S(1)}, u32[]{:S(2)}, u32[]{:S(2)}) %collective-permute-start.14) | collective-permute-done | bytes 327712 | tf_op jit(solution)/shard_map/ppermute | solution.py:456
  114.7 1.6 %collective-permute-start.15 = (bf16[256,640]{1,0:T(8,128)(2,1)S(1)}, bf16[256,640]{1,0:T(8,128)(2,1)S(1)}, u32[]{:S(2)}, u32[]{:S(2)}) collective-permute-start(bf16[256,640]{1,0:T(8,128)(2,1)S(1)} %pad_maximum_fusion.2), channel_id=1, source_target_pairs={{0,4},{1,29},{2,6},{3,31},{4,8},{5,1},{6,10},{7,3},{8,12},{9,5},{1... | collective-permute-start | bytes 983048 | tf_op jit(solution)/shard_map/ppermute | solution.py:456
  116.6 1.6 %collective-permute-start.35 = (bf16[256,512]{1,0:T(8,128)(2,1)S(1)}, bf16[256,512]{1,0:T(8,128)(2,1)S(1)}, u32[]{:S(2)}, u32[]{:S(2)}) collective-permute-start(bf16[256,512]{1,0:T(8,128)(2,1)S(1)} %pad_maximum_fusion.4.refs_0_), channel_id=1, source_target_pairs={{0,192},{1,193},{2,194},{3,195},{4,196},{5,197},{6,198},{7,199},{8... | collective-permute-start | bytes 786440 | tf_op jit(solution)/shard_map/ppermute | solution.py:456
  118.2 0.9 collective-permute-start.34
  119.1 5.2 %collective-permute-done.35.refs_3_ = bf16[256,512]{1,0:T(8,128)(2,1)S(1)} collective-permute-done((bf16[256,512]{1,0:T(8,128)(2,1)S(1)}, bf16[256,512]{1,0:T(8,128)(2,1)S(1)}, u32[]{:S(2)}, u32[]{:S(2)}) %collective-permute-start.35) | collective-permute-done | bytes 262176 | tf_op jit(solution)/shard_map/ppermute | solution.py:456
  124.3 7.9 %collective-permute-start.36 = (bf16[256,512]{1,0:T(8,128)(2,1)S(1)}, bf16[256,512]{1,0:T(8,128)(2,1)S(1)}, u32[]{:S(2)}, u32[]{:S(2)}) collective-permute-start(bf16[256,512]{1,0:T(8,128)(2,1)S(1)} %pad_maximum_fusion.4.refs_0_), channel_id=1, source_target_pairs={{0,1},{1,0},{2,3},{3,2},{4,5},{5,4},{6,7},{7,6},{8,9},{9,8},{10,11... | collective-permute-start | bytes 786440 | tf_op jit(solution)/shard_map/ppermute | solution.py:456
  132.2 1.2 collective-permute-start.39
  133.4 2.7 %collective-permute-start.38 = (bf16[256,512]{1,0:T(8,128)(2,1)S(1)}, bf16[256,512]{1,0:T(8,128)(2,1)S(1)}, u32[]{:S(2)}, u32[]{:S(2)}) collective-permute-start(bf16[256,512]{1,0:T(8,128)(2,1)S(1)} %collective-permute-done.34.refs_2_), channel_id=1, source_target_pairs={{0,1},{1,0},{2,3},{3,2},{4,5},{5,4},{6,7},{7,6},{8,9},{9,8},{10,11... | collective-permute-start | bytes 786440 | tf_op jit(solution)/shard_map/ppermute | solution.py:456
  136.1 0.6 collective-permute-start.16
  136.7 0.5 collective-permute-done.38.refs_6_
  137.3 0.4 collective-permute-done.37.refs_5_
  137.9 2.6 %outputs.1 = (bf16[128,1024]{1,0:T(8,128)(2,1)}, bf16[128,512]{1,0:T(8,128)(2,1)}, bf16[128,512]{1,0:T(8,128)(2,1)}, bf16[64,128]{1,0:T(8,128)(2,1)}, f32[8,128,512]{2,1,0:T(8,128)}, /*index=5*/f32[8,512,128]{2,1,0:T(8,128)}) custom-call(s32[1]{0:T(128)} %bitcast.dp_ref.refs_1_, s32[1]{0:T(128)} %bitcast.1.ctx_ref.refs_2_, ...), custom_call_target="tpu_custom_call" | custom-call | tf_op jit(solution)/shard_map/outputs/pallas_call | solution.py:427
  (70 shorter events, 2.8 us)
Async XLA Ops:
  2.3 10.1 %collective-permute-start.1 = (bf16[128,640]{1,0:T(8,128)(2,1)}, bf16[128,640]{1,0:T(8,128)(2,1)S(1)}, u32[]{:S(2)}, u32[]{:S(2)}) collective-permute-start(bf16[128,640]{1,0:T(8,128)(2,1)} %key_rows.1.refs_7_), channel_id=1, source_target_pairs={{0,28},{1,29},{2,30},{3,31},{4,0},{5,1},{6,2},{7,3},{8,4},{9,5},{1... | collective-permute-start | bytes 491528 | tf_op jit(solution)/shard_map/ppermute | solution.py:456
  8.7 6.2 %collective-permute-start = (bf16[128,640]{1,0:T(8,128)(2,1)}, bf16[128,640]{1,0:T(8,128)(2,1)S(1)}, u32[]{:S(2)}, u32[]{:S(2)}) collective-permute-start(bf16[128,640]{1,0:T(8,128)(2,1)} %key_rows.1.refs_7_), channel_id=1, source_target_pairs={{0,4},{1,5},{2,6},{3,7},{4,8},{5,9},{6,10},{7,11},{8,12},{9,13},{1... | collective-permute-start | bytes 491528 | tf_op jit(solution)/shard_map/ppermute | solution.py:456
  8.7 29.4 %copy-start = (bf16[128,640]{1,0:T(8,128)(2,1)S(1)}, bf16[128,640]{1,0:T(8,128)(2,1)}, u32[]{:S(2)}) copy-start(bf16[128,640]{1,0:T(8,128)(2,1)} %key_rows.1.refs_7_) | copy-start | bytes 491524
  8.7 29.4 %copy-start.1 = (bf16[8,512,128]{2,1,0:T(8,128)(2,1)S(1)}, bf16[8,512,128]{2,1,0:T(8,128)(2,1)}, u32[]{:S(2)}) copy-start(bf16[8,512,128]{2,1,0:T(8,128)(2,1)} %refs_17_.1) | copy-start | bytes 3145732
  8.7 29.4 %copy-start.2 = (bf16[8,128,512]{2,1,0:T(8,128)(2,1)S(1)}, bf16[8,128,512]{2,1,0:T(8,128)(2,1)}, u32[]{:S(2)}) copy-start(bf16[8,128,512]{2,1,0:T(8,128)(2,1)} %refs_16_.1) | copy-start | bytes 3145732
  8.7 29.4 %copy-start.3 = (s32[1,64]{1,0:T(1,128)S(1)}, s32[1,64]{1,0:T(1,128)}, u32[]{:S(2)}) copy-start(s32[1,64]{1,0:T(1,128)} %refs_0_.1) | copy-start | bytes 772
  14.9 15.1 %collective-permute-start.2 = (bf16[128,2688]{1,0:T(8,128)(2,1)S(1)}, bf16[128,2688]{1,0:T(8,128)(2,1)S(1)}, u32[]{:S(2)}, u32[]{:S(2)}) collective-permute-start(bf16[128,2688]{1,0:T(8,128)(2,1)S(1)} %get-tuple-element.34.refs_3_), channel_id=1, source_target_pairs={{0,2},{1,3},{2,0},{3,1},{4,6},{5,7},{6,4},{7,5},{8,10},{9,11},{10,... | collective-permute-start | bytes 2064392 | tf_op jit(solution)/shard_map/ppermute | solution.py:456
  16.1 5.4 %collective-permute-start.3 = (bf16[128,640]{1,0:T(8,128)(2,1)S(1)}, bf16[128,640]{1,0:T(8,128)(2,1)S(1)}, u32[]{:S(2)}, u32[]{:S(2)}) collective-permute-start(bf16[128,640]{1,0:T(8,128)(2,1)S(1)} %collective-permute-done.refs_8_), channel_id=1, source_target_pairs={{0,4},{1,5},{2,6},{3,7},{4,8},{5,9},{6,10},{7,11},{8,12},{9,13},{1... | collective-permute-start | bytes 491528 | tf_op jit(solution)/shard_map/ppermute | solution.py:456
  16.1 5.4 %collective-permute-start.4 = (bf16[128,640]{1,0:T(8,128)(2,1)S(1)}, bf16[128,640]{1,0:T(8,128)(2,1)S(1)}, u32[]{:S(2)}, u32[]{:S(2)}) collective-permute-start(bf16[128,640]{1,0:T(8,128)(2,1)S(1)} %collective-permute-done.1.refs_9_), channel_id=1, source_target_pairs={{0,28},{1,29},{2,30},{3,31},{4,0},{5,1},{6,2},{7,3},{8,4},{9,5},{1... | collective-permute-start | bytes 491528 | tf_op jit(solution)/shard_map/ppermute | solution.py:456
  21.5 6.5 %collective-permute-start.5 = (bf16[128,640]{1,0:T(8,128)(2,1)S(1)}, bf16[128,640]{1,0:T(8,128)(2,1)S(1)}, u32[]{:S(2)}, u32[]{:S(2)}) collective-permute-start(bf16[128,640]{1,0:T(8,128)(2,1)S(1)} %collective-permute-done.3.refs_10_), channel_id=1, source_target_pairs={{0,4},{1,5},{2,6},{3,7},{4,8},{5,9},{6,10},{7,11},{8,12},{9,13},{1... | collective-permute-start | bytes 491528 | tf_op jit(solution)/shard_map/ppermute | solution.py:456
  21.5 6.5 %collective-permute-start.6 = (bf16[128,640]{1,0:T(8,128)(2,1)S(1)}, bf16[128,640]{1,0:T(8,128)(2,1)S(1)}, u32[]{:S(2)}, u32[]{:S(2)}) collective-permute-start(bf16[128,640]{1,0:T(8,128)(2,1)S(1)} %collective-permute-done.4.refs_11_), channel_id=1, source_target_pairs={{0,28},{1,29},{2,30},{3,31},{4,0},{5,1},{6,2},{7,3},{8,4},{9,5},{1... | collective-permute-start | bytes 491528 | tf_op jit(solution)/shard_map/ppermute | solution.py:456
  24.2 14.0 %collective-permute-start.7 = (bf16[128,2688]{1,0:T(8,128)(2,1)S(1)}, bf16[128,2688]{1,0:T(8,128)(2,1)S(1)}, u32[]{:S(2)}, u32[]{:S(2)}) collective-permute-start(bf16[128,2688]{1,0:T(8,128)(2,1)S(1)} %get-tuple-element.34.refs_3_), channel_id=1, source_target_pairs={{0,1},{1,0},{2,3},{3,2},{4,5},{5,4},{6,7},{7,6},{8,9},{9,8},{10,11... | collective-permute-start | bytes 2064392 | tf_op jit(solution)/shard_map/ppermute | solution.py:456
  29.9 8.2 %collective-permute-start.8 = (bf16[128,2688]{1,0:T(8,128)(2,1)S(1)}, bf16[128,2688]{1,0:T(8,128)(2,1)S(1)}, u32[]{:S(2)}, u32[]{:S(2)}) collective-permute-start(bf16[128,2688]{1,0:T(8,128)(2,1)S(1)} %collective-permute-done.2.refs_4_), channel_id=1, source_target_pairs={{0,1},{1,0},{2,3},{3,2},{4,5},{5,4},{6,7},{7,6},{8,9},{9,8},{10,11... | collective-permute-start | bytes 2064392 | tf_op jit(solution)/shard_map/ppermute | solution.py:456
  32.8 5.4 %collective-permute-start.9 = (bf16[64,640]{1,0:T(8,128)(2,1)S(1)}, bf16[64,640]{1,0:T(8,128)(2,1)S(1)}, u32[]{:S(2)}, u32[]{:S(2)}) collective-permute-start(bf16[64,640]{1,0:T(8,128)(2,1)S(1)} %slice.78), channel_id=1, source_target_pairs={{0,4},{1,5},{2,6},{3,7},{4,8},{5,9},{6,10},{7,11},{8,12},{9,13},{1... | collective-permute-start | bytes 245768 | tf_op jit(solution)/shard_map/ppermute | solution.py:456
  32.9 5.3 %collective-permute-start.10 = (bf16[64,640]{1,0:T(8,128)(2,1)S(1)}, bf16[64,640]{1,0:T(8,128)(2,1)S(1)}, u32[]{:S(2)}, u32[]{:S(2)}) collective-permute-start(bf16[64,640]{1,0:T(8,128)(2,1)S(1)} %slice.79), channel_id=1, source_target_pairs={{0,28},{1,29},{2,30},{3,31},{4,0},{5,1},{6,2},{7,3},{8,4},{9,5},{1... | collective-permute-start | bytes 245768 | tf_op jit(solution)/shard_map/ppermute | solution.py:456
  35.5 33.0 %copy-start.4 = (bf16[4,128,512]{2,1,0:T(8,128)(2,1)S(1)}, bf16[4,128,512]{2,1,0:T(8,128)(2,1)}, u32[]{:S(2)}) copy-start(bf16[4,128,512]{2,1,0:T(8,128)(2,1)} %get-tuple-element.52) | copy-start | bytes 1572868
  35.5 32.9 %collective-permute-start.20 = (bf16[4,128,512]{2,1,0:T(8,128)(2,1)}, bf16[4,128,512]{2,1,0:T(8,128)(2,1)S(1)}, u32[]{:S(2)}, u32[]{:S(2)}) collective-permute-start(bf16[4,128,512]{2,1,0:T(8,128)(2,1)} %get-tuple-element.53), channel_id=1, source_target_pairs={{0,1},{1,0},{2,3},{3,2},{4,5},{5,4},{6,7},{7,6},{8,9},{9,8},{10,11... | collective-permute-start | bytes 1572872 | tf_op jit(solution)/shard_map/ppermute | solution.py:456
  67.9 2.0 %collective-permute-start.19 = (bf16[4,128,512]{2,1,0:T(8,128)(2,1)S(1)}, bf16[4,128,512]{2,1,0:T(8,128)(2,1)S(1)}, u32[]{:S(2)}, u32[]{:S(2)}) collective-permute-start(bf16[4,128,512]{2,1,0:T(8,128)(2,1)S(1)} %get-tuple-element.51), channel_id=1, source_target_pairs={{0,1},{1,0},{2,3},{3,2},{4,5},{5,4},{6,7},{7,6},{8,9},{9,8},{10,11... | collective-permute-start | bytes 1572872 | tf_op jit(solution)/shard_map/ppermute | solution.py:456
  68.0 6.5 %collective-permute-start.11 = (bf16[448,640]{1,0:T(8,128)(2,1)S(1)}, bf16[448,640]{1,0:T(8,128)(2,1)S(1)}, u32[]{:S(2)}, u32[]{:S(2)}) collective-permute-start(bf16[448,640]{1,0:T(8,128)(2,1)S(1)} %get-tuple-element.47), channel_id=1, source_target_pairs={{0,1},{1,0},{2,3},{3,2},{4,5},{5,4},{6,7},{7,6},{8,9},{9,8},{10,11... | collective-permute-start | bytes 1720328 | tf_op jit(solution)/shard_map/ppermute | solution.py:456
  68.6 29.5 %collective-permute-start.17 = (bf16[2,128,1536]{2,1,0:T(8,128)(2,1)S(1)}, bf16[2,128,1536]{2,1,0:T(8,128)(2,1)S(1)}, u32[]{:S(2)}, u32[]{:S(2)}) collective-permute-start(bf16[2,128,1536]{2,1,0:T(8,128)(2,1)S(1)} %get-tuple-element.49), channel_id=1, source_target_pairs={{0,1},{1,0},{2,3},{3,2},{4,5},{5,4},{6,7},{7,6},{8,9},{9,8},{10,11... | collective-permute-start | bytes 2359304 | tf_op jit(solution)/shard_map/ppermute | solution.py:456
  70.1 9.1 %collective-permute-start.21 = (bf16[4,64,512]{2,1,0:T(8,128)(2,1)S(1)}, bf16[4,64,512]{2,1,0:T(8,128)(2,1)S(1)}, u32[]{:S(2)}, u32[]{:S(2)}) collective-permute-start(bf16[4,64,512]{2,1,0:T(8,128)(2,1)S(1)} %get-tuple-element.60), channel_id=1, source_target_pairs={{0,64},{1,65},{2,66},{3,67},{4,68},{5,69},{6,70},{7,71},{8,72},{9,... | collective-permute-start | bytes 786440 | tf_op jit(solution)/shard_map/ppermute | solution.py:456
  71.8 7.3 %collective-permute-start.23 = (bf16[4,64,512]{2,1,0:T(8,128)(2,1)S(1)}, bf16[4,64,512]{2,1,0:T(8,128)(2,1)S(1)}, u32[]{:S(2)}, u32[]{:S(2)}) collective-permute-start(bf16[4,64,512]{2,1,0:T(8,128)(2,1)S(1)} %get-tuple-element.61), channel_id=1, source_target_pairs={{0,192},{1,193},{2,194},{3,195},{4,196},{5,197},{6,198},{7,199},{8... | collective-permute-start | bytes 786440 | tf_op jit(solution)/shard_map/ppermute | solution.py:456
  72.8 12.2 %collective-permute-start.22 = (bf16[4,64,512]{2,1,0:T(8,128)(2,1)S(1)}, bf16[4,64,512]{2,1,0:T(8,128)(2,1)S(1)}, u32[]{:S(2)}, u32[]{:S(2)}) collective-permute-start(bf16[4,64,512]{2,1,0:T(8,128)(2,1)S(1)} %get-tuple-element.62), channel_id=1, source_target_pairs={{0,128},{1,129},{2,130},{3,131},{4,132},{5,133},{6,134},{7,135},{8... | collective-permute-start | bytes 786440 | tf_op jit(solution)/shard_map/ppermute | solution.py:456
  74.6 15.5 %collective-permute-start.12 = (bf16[128,640]{1,0:T(8,128)(2,1)S(1)}, bf16[128,640]{1,0:T(8,128)(2,1)S(1)}, u32[]{:S(2)}, u32[]{:S(2)}) collective-permute-start(bf16[128,640]{1,0:T(8,128)(2,1)S(1)} %pad_maximum_fusion.5), channel_id=1, source_target_pairs={{0,4},{1,29},{2,6},{3,31},{4,8},{5,1},{6,10},{7,3},{8,12},{9,5},{1... | collective-permute-start | bytes 491528 | tf_op jit(solution)/shard_map/ppermute | solution.py:456
  85.2 5.3 %collective-permute-start.24 = (bf16[64,512]{1,0:T(8,128)(2,1)S(1)}, bf16[64,512]{1,0:T(8,128)(2,1)S(1)}, u32[]{:S(2)}, u32[]{:S(2)}) collective-permute-start(bf16[64,512]{1,0:T(8,128)(2,1)S(1)} %get-tuple-element.69), channel_id=1, source_target_pairs={{0,2},{1,3},{2,32},{3,33},{4,6},{5,7},{6,36},{7,37},{8,10},{9,11},... | collective-permute-start | bytes 196616 | tf_op jit(solution)/shard_map/ppermute | solution.py:456
  87.6 3.1 %collective-permute-start.26 = (bf16[64,512]{1,0:T(8,128)(2,1)S(1)}, bf16[64,512]{1,0:T(8,128)(2,1)S(1)}, u32[]{:S(2)}, u32[]{:S(2)}) collective-permute-start(bf16[64,512]{1,0:T(8,128)(2,1)S(1)} %get-tuple-element.70), channel_id=1, source_target_pairs={{0,34},{1,35},{2,0},{3,1},{4,38},{5,39},{6,4},{7,5},{8,42},{9,43},... | collective-permute-start | bytes 196616 | tf_op jit(solution)/shard_map/ppermute | solution.py:456
  89.2 4.9 %collective-permute-start.25 = (bf16[64,512]{1,0:T(8,128)(2,1)S(1)}, bf16[64,512]{1,0:T(8,128)(2,1)S(1)}, u32[]{:S(2)}, u32[]{:S(2)}) collective-permute-start(bf16[64,512]{1,0:T(8,128)(2,1)S(1)} %get-tuple-element.71), channel_id=1, source_target_pairs={{0,32},{1,33},{2,34},{3,35},{4,36},{5,37},{6,38},{7,39},{8,40},{9,... | collective-permute-start | bytes 196616 | tf_op jit(solution)/shard_map/ppermute | solution.py:456
  94.1 3.2 %collective-permute-start.27 = (bf16[64,512]{1,0:T(8,128)(2,1)S(1)}, bf16[64,512]{1,0:T(8,128)(2,1)S(1)}, u32[]{:S(2)}, u32[]{:S(2)}) collective-permute-start(bf16[64,512]{1,0:T(8,128)(2,1)S(1)} %fusion.12), channel_id=1, source_target_pairs={{0,4},{1,5},{2,6},{3,7},{4,0},{5,1},{6,2},{7,3},{8,12},{9,13},{10,... | collective-permute-start | bytes 196616 | tf_op jit(solution)/shard_map/ppermute | solution.py:456
  94.3 11.6 %collective-permute-start.13 = (bf16[256,640]{1,0:T(8,128)(2,1)S(1)}, bf16[256,640]{1,0:T(8,128)(2,1)S(1)}, u32[]{:S(2)}, u32[]{:S(2)}) collective-permute-start(bf16[256,640]{1,0:T(8,128)(2,1)S(1)} %pad_maximum_fusion), channel_id=1, source_target_pairs={{0,4},{1,29},{2,6},{3,31},{4,8},{5,1},{6,10},{7,3},{8,12},{9,5},{1... | collective-permute-start | bytes 983048 | tf_op jit(solution)/shard_map/ppermute | solution.py:456
  97.3 5.1 %collective-permute-start.28 = (bf16[64,512]{1,0:T(8,128)(2,1)S(1)}, bf16[64,512]{1,0:T(8,128)(2,1)S(1)}, u32[]{:S(2)}, u32[]{:S(2)}) collective-permute-start(bf16[64,512]{1,0:T(8,128)(2,1)S(1)} %add_convert_fusion.11), channel_id=1, source_target_pairs={{0,8},{1,9},{2,10},{3,11},{4,12},{5,13},{6,14},{7,15},{8,0},{9,1},... | collective-permute-start | bytes 196616 | tf_op jit(solution)/shard_map/ppermute | solution.py:456
  102.4 7.2 %collective-permute-start.29 = (bf16[64,512]{1,0:T(8,128)(2,1)S(1)}, bf16[64,512]{1,0:T(8,128)(2,1)S(1)}, u32[]{:S(2)}, u32[]{:S(2)}) collective-permute-start(bf16[64,512]{1,0:T(8,128)(2,1)S(1)} %add_convert_fusion.10), channel_id=1, source_target_pairs={{0,16},{1,17},{2,18},{3,19},{4,20},{5,21},{6,22},{7,23},{8,24},{9,... | collective-permute-start | bytes 196616 | tf_op jit(solution)/shard_map/ppermute | solution.py:456
  106.0 8.6 %collective-permute-start.14 = (bf16[256,640]{1,0:T(8,128)(2,1)S(1)}, bf16[256,640]{1,0:T(8,128)(2,1)S(1)}, u32[]{:S(2)}, u32[]{:S(2)}) collective-permute-start(bf16[256,640]{1,0:T(8,128)(2,1)S(1)} %pad_maximum_fusion.1), channel_id=1, source_target_pairs={{0,4},{1,29},{2,6},{3,31},{4,8},{5,1},{6,10},{7,3},{8,12},{9,5},{1... | collective-permute-start | bytes 983048 | tf_op jit(solution)/shard_map/ppermute | solution.py:456
  107.1 29.0 %collective-permute-start.18 = (bf16[128,1536]{1,0:T(8,128)(2,1)S(1)}, bf16[128,1536]{1,0:T(8,128)(2,1)S(1)}, u32[]{:S(2)}, u32[]{:S(2)}) collective-permute-start(bf16[128,1536]{1,0:T(8,128)(2,1)S(1)} %slice_bitcast_fusion), channel_id=1, source_target_pairs={{0,2},{1,3},{2,0},{3,1},{4,6},{5,7},{6,4},{7,5},{8,10},{9,11},{10,... | collective-permute-start | bytes 1179656 | tf_op jit(solution)/shard_map/ppermute | solution.py:456
  109.7 6.6 %collective-permute-start.32 = (bf16[64,512]{1,0:T(8,128)(2,1)S(1)}, bf16[64,512]{1,0:T(8,128)(2,1)S(1)}, u32[]{:S(2)}, u32[]{:S(2)}) collective-permute-start(bf16[64,512]{1,0:T(8,128)(2,1)S(1)} %add_convert_fusion.9), channel_id=1, source_target_pairs={{0,34},{1,35},{2,0},{3,1},{4,38},{5,39},{6,4},{7,5},{8,42},{9,43},... | collective-permute-start | bytes 196616 | tf_op jit(solution)/shard_map/ppermute | solution.py:456
  111.2 5.1 %collective-permute-start.31 = (bf16[64,512]{1,0:T(8,128)(2,1)S(1)}, bf16[64,512]{1,0:T(8,128)(2,1)S(1)}, u32[]{:S(2)}, u32[]{:S(2)}) collective-permute-start(bf16[64,512]{1,0:T(8,128)(2,1)S(1)} %add_convert_fusion.9), channel_id=1, source_target_pairs={{0,32},{1,33},{2,34},{3,35},{4,36},{5,37},{6,38},{7,39},{8,40},{9,... | collective-permute-start | bytes 196616 | tf_op jit(solution)/shard_map/ppermute | solution.py:456
  111.2 5.3 %collective-permute-start.30 = (bf16[64,512]{1,0:T(8,128)(2,1)S(1)}, bf16[64,512]{1,0:T(8,128)(2,1)S(1)}, u32[]{:S(2)}, u32[]{:S(2)}) collective-permute-start(bf16[64,512]{1,0:T(8,128)(2,1)S(1)} %add_convert_fusion.9), channel_id=1, source_target_pairs={{0,2},{1,3},{2,32},{3,33},{4,6},{5,7},{6,36},{7,37},{8,10},{9,11},... | collective-permute-start | bytes 196616 | tf_op jit(solution)/shard_map/ppermute | solution.py:456
  114.7 21.4 %collective-permute-start.15 = (bf16[256,640]{1,0:T(8,128)(2,1)S(1)}, bf16[256,640]{1,0:T(8,128)(2,1)S(1)}, u32[]{:S(2)}, u32[]{:S(2)}) collective-permute-start(bf16[256,640]{1,0:T(8,128)(2,1)S(1)} %pad_maximum_fusion.2), channel_id=1, source_target_pairs={{0,4},{1,29},{2,6},{3,31},{4,8},{5,1},{6,10},{7,3},{8,12},{9,5},{1... | collective-permute-start | bytes 983048 | tf_op jit(solution)/shard_map/ppermute | solution.py:456
  116.6 7.7 %collective-permute-start.35 = (bf16[256,512]{1,0:T(8,128)(2,1)S(1)}, bf16[256,512]{1,0:T(8,128)(2,1)S(1)}, u32[]{:S(2)}, u32[]{:S(2)}) collective-permute-start(bf16[256,512]{1,0:T(8,128)(2,1)S(1)} %pad_maximum_fusion.4.refs_0_), channel_id=1, source_target_pairs={{0,192},{1,193},{2,194},{3,195},{4,196},{5,197},{6,198},{7,199},{8... | collective-permute-start | bytes 786440 | tf_op jit(solution)/shard_map/ppermute | solution.py:456
  118.2 14.0 %collective-permute-start.34 = (bf16[256,512]{1,0:T(8,128)(2,1)S(1)}, bf16[256,512]{1,0:T(8,128)(2,1)S(1)}, u32[]{:S(2)}, u32[]{:S(2)}) collective-permute-start(bf16[256,512]{1,0:T(8,128)(2,1)S(1)} %pad_maximum_fusion.4.refs_0_), channel_id=1, source_target_pairs={{0,128},{1,129},{2,130},{3,131},{4,132},{5,133},{6,134},{7,135},{8... | collective-permute-start | bytes 786440 | tf_op jit(solution)/shard_map/ppermute | solution.py:456
  119.1 14.3 %collective-permute-start.33 = (bf16[256,512]{1,0:T(8,128)(2,1)S(1)}, bf16[256,512]{1,0:T(8,128)(2,1)S(1)}, u32[]{:S(2)}, u32[]{:S(2)}) collective-permute-start(bf16[256,512]{1,0:T(8,128)(2,1)S(1)} %pad_maximum_fusion.4.refs_0_), channel_id=1, source_target_pairs={{0,64},{1,65},{2,66},{3,67},{4,68},{5,69},{6,70},{7,71},{8,72},{9,... | collective-permute-start | bytes 786440 | tf_op jit(solution)/shard_map/ppermute | solution.py:456
  124.3 12.5 %collective-permute-start.36 = (bf16[256,512]{1,0:T(8,128)(2,1)S(1)}, bf16[256,512]{1,0:T(8,128)(2,1)S(1)}, u32[]{:S(2)}, u32[]{:S(2)}) collective-permute-start(bf16[256,512]{1,0:T(8,128)(2,1)S(1)} %pad_maximum_fusion.4.refs_0_), channel_id=1, source_target_pairs={{0,1},{1,0},{2,3},{3,2},{4,5},{5,4},{6,7},{7,6},{8,9},{9,8},{10,11... | collective-permute-start | bytes 786440 | tf_op jit(solution)/shard_map/ppermute | solution.py:456
  132.2 4.6 %collective-permute-start.39 = (bf16[256,512]{1,0:T(8,128)(2,1)S(1)}, bf16[256,512]{1,0:T(8,128)(2,1)S(1)}, u32[]{:S(2)}, u32[]{:S(2)}) collective-permute-start(bf16[256,512]{1,0:T(8,128)(2,1)S(1)} %collective-permute-done.35.refs_3_), channel_id=1, source_target_pairs={{0,1},{1,0},{2,3},{3,2},{4,5},{5,4},{6,7},{7,6},{8,9},{9,8},{10,11... | collective-permute-start | bytes 786440 | tf_op jit(solution)/shard_map/ppermute | solution.py:456
  133.4 3.9 %collective-permute-start.38 = (bf16[256,512]{1,0:T(8,128)(2,1)S(1)}, bf16[256,512]{1,0:T(8,128)(2,1)S(1)}, u32[]{:S(2)}, u32[]{:S(2)}) collective-permute-start(bf16[256,512]{1,0:T(8,128)(2,1)S(1)} %collective-permute-done.34.refs_2_), channel_id=1, source_target_pairs={{0,1},{1,0},{2,3},{3,2},{4,5},{5,4},{6,7},{7,6},{8,9},{9,8},{10,11... | collective-permute-start | bytes 786440 | tf_op jit(solution)/shard_map/ppermute | solution.py:456
  136.1 1.5 %collective-permute-start.37 = (bf16[256,512]{1,0:T(8,128)(2,1)S(1)}, bf16[256,512]{1,0:T(8,128)(2,1)S(1)}, u32[]{:S(2)}, u32[]{:S(2)}) collective-permute-start(bf16[256,512]{1,0:T(8,128)(2,1)S(1)} %collective-permute-done.33.refs_1_), channel_id=1, source_target_pairs={{0,1},{1,0},{2,3},{3,2},{4,5},{5,4},{6,7},{7,6},{8,9},{9,8},{10,11... | collective-permute-start | bytes 786440 | tf_op jit(solution)/shard_map/ppermute | solution.py:456
  136.1 1.7 %collective-permute-start.16 = (bf16[128,640]{1,0:T(8,128)(2,1)S(1)}, bf16[128,640]{1,0:T(8,128)(2,1)S(1)}, u32[]{:S(2)}, u32[]{:S(2)}) collective-permute-start(bf16[128,640]{1,0:T(8,128)(2,1)S(1)} %slice.114), channel_id=1, source_target_pairs={{0,1},{1,0},{2,3},{3,2},{4,5},{5,4},{6,7},{7,6},{8,9},{9,8},{10,11... | collective-permute-start | bytes 491528 | tf_op jit(solution)/shard_map/ppermute | solution.py:456
